TPU v7x, 32 devices: a whole 2x2x4 slice. The times are simulated.
32 devices in a mesh: row: 8 (over z, y), col: 4 (over x, core).
Axes of the slice: x: 2, y: 2, z: 4, core: 2. Of those that a mesh axis runs over, the one named last changes fastest.
Arguments:
- amplitudes: bfloat16 [4, 1280, 1280], P(None, ('row', 'col')), may hold values from -0.75 to 0.75
- integrals: bfloat16 [24, 1280, 1280], P('row', 'col'), may hold values from -0.15625 to 0.15625
- occupied_integrals: bfloat16 [24, 160, 1280], P('row'), may hold values from -1 to 1
- pair_orbitals: int32 [4, 2], replicated, may hold values from 0 to 159
- amplitude_tiles: int32 [4, 20, 20], replicated, may hold values 0 or 1
- integral_tiles: int32 [20, 20], replicated, may hold values 0 or 1
Outputs:
- residual: float32 [4, 1280, 1280], P(None, 'col', 'row')
All inputs are finite; a program needn't handle non-finite values.
Results may differ from a plain program's by a relative error of at most 0.005.
Values may be sent and summed in bfloat16 or wider, within the bound.
No kernel may reach another device: no remote copies, remote signals or barrier semaphores. Data moves between devices by JAX's collectives and lax.ppermute only.
A program may use at most 128 MiB of HBM per device.

v0:
```python
import jax
import jax.numpy as jnp
from jax import lax
from jax.sharding import PartitionSpec as P

TILE = 64


def mask_rows(amp_rows, amp_tiles, tile_size):
    row_count = amp_rows.shape[1]
    tile_count = amp_tiles.shape[1]
    tile_of = jnp.arange(row_count, dtype=jnp.int32) // tile_size
    picker = (tile_of[:, None] == jnp.arange(tile_count, dtype=jnp.int32)[None, :]).astype(
        jnp.float32
    )
    row_mask = jnp.einsum("nk,pkm->pnm", picker, amp_tiles.astype(jnp.float32))
    row_mask = jnp.repeat(row_mask, tile_size, axis=2)
    return amp_rows * row_mask.astype(amp_rows.dtype)


def local(
    amplitudes, integrals, occupied_integrals, pair_orbitals, amplitude_tiles, integral_tiles
):
    column_index = lax.axis_index("col")
    local_rows = integrals.shape[1]
    tiles_here = local_rows // TILE
    tile_rows = lax.dynamic_slice_in_dim(integral_tiles, column_index * tiles_here, tiles_here, 0)
    factor_mask = jnp.repeat(jnp.repeat(tile_rows, TILE, axis=0), TILE, axis=1)
    masked_int = integrals * factor_mask.astype(jnp.bfloat16)[None]
    orbital_ids = jnp.arange(occupied_integrals.shape[1], dtype=jnp.int32)
    pick_first = (pair_orbitals[:, 0][:, None] == orbital_ids[None, :]).astype(jnp.bfloat16)
    pick_second = (pair_orbitals[:, 1][:, None] == orbital_ids[None, :]).astype(jnp.bfloat16)
    first_rows = jnp.einsum(
        "po,qov->qpv", pick_first, occupied_integrals, preferred_element_type=jnp.float32
    )
    second_rows = jnp.einsum(
        "po,qov->qpv", pick_second, occupied_integrals, preferred_element_type=jnp.float32
    ).astype(jnp.bfloat16)
    whole_amp = lax.all_gather(amplitudes, ("row", "col"), axis=1, tiled=True)
    masked_amp = mask_rows(whole_amp, amplitude_tiles, TILE)
    inter = jnp.einsum(
        "qac,pcd->qpad", masked_int, masked_amp, preferred_element_type=jnp.float32
    ).astype(jnp.bfloat16)
    carried = jnp.einsum(
        "qpc,pcd->qpd", second_rows, masked_amp, preferred_element_type=jnp.float32
    )
    first_here = lax.dynamic_slice_in_dim(first_rows, column_index * local_rows, local_rows, 2)
    ladder = jnp.einsum(
        "qpad,qbd->pab",
        inter,
        lax.all_gather(masked_int, "col", axis=1, tiled=True),
        preferred_element_type=jnp.float32,
    )
    cycle = jnp.einsum("qpa,qpb->pab", first_here, carried)
    return lax.psum_scatter(ladder + cycle, "row", scatter_dimension=2, tiled=True)


def solution(mesh):
    placed = (
        P(None, ("row", "col"), None),
        P("row", "col", None),
        P("row", None, None),
        P(),
        P(),
        P(),
    )
    return jax.shard_map(
        local, mesh=mesh, in_specs=placed, out_specs=P(None, "col", "row"), check_vma=False
    )
```

profile of v0, /device:TPU:0, one launch (start us, length us, event | category | flops | bytes accessed | tf_op | source)
XLA Modules:
  0.0 361.1 jit_solution(7694052003759360732)
XLA Ops:
  6.5 0.0 copy-start
  6.5 0.0 copy-start.4
  6.5 0.0 copy-start.5
  6.5 0.0 all-gather.3.cloned.1.call-start
  6.5 2.0 copy.21
  8.6 0.0 all-gather.3.cloned.1.call-update
  8.6 0.0 all-gather.5.cloned.1.call-start
  8.6 0.7 dynamic-slice_convert_fusion
  9.3 0.1 copy.24
  9.5 0.1 broadcast_in_dim.7
  9.6 0.1 convert_element_type.48
  9.6 0.1 broadcast_in_dim.16
  9.7 0.6 copy.25
  10.4 3.4 broadcast_multiply_fusion
  13.8 0.0 all-gather.5.cloned.1.call-update
  13.8 0.0 reduce-scatter.2.cloned.1.call-start
  13.9 0.0 copy-done.4
  13.9 0.0 copy-done.5
  13.9 0.0 copy-done
  13.9 0.3 fusion.20
  14.3 0.1 dynamic-slice_bitcast_fusion
  14.4 0.3 fusion.7
  14.6 0.3 fusion.8
  15.0 96.5 %all-gather.3.cloned.1.call-done = bf16[4,1280,1280]{2,0,1:T(4,128)(2,1)} async-done(((bf16[4,40,1280]{2,0,1:T(4,128)(2,1)}), bf16[4,1280,1280]{2,0,1:T(4,128)(2,1)}) %all-gather.3.cloned.1.call-update) | async-done | bytes 13107216 | tf_op jit(solution)/shard_map/all_gather | solution.py:39
  111.4 21.4 %copy.23 = bf16[4,1280,1280]{1,2,0:T(8,128)(2,1)} copy(bf16[4,1280,1280]{2,0,1:T(4,128)(2,1)} %all-gather.3.cloned.1.call-done) | data formatting | bytes 26214400 | tf_op jit(solution)/shard_map/all_gather | solution.py:39
  132.9 0.0 copy-start.3
  132.9 6.4 %bitcast_multiply_fusion = bf16[4,1280,1280]{1,2,0:T(8,128)(2,1)S(1)} fusion(bf16[4,1280,1280]{1,2,0:T(8,128)(2,1)} %copy.23, bf16[4,1280,20]{1,2,0:T(8,128)(2,1)S(1)} %fusion.7), kind=kLoop, calls=%fused_computation.2 | loop fusion | flops 6553600 | bytes 26419200 | tf_op jit(solution)/shard_map/mul | solution.py:18
  139.2 0.0 copy-start.2
  139.2 4.7 %copy-done.2 = bf16[4,1280,1280]{1,2,0:T(8,128)(2,1)} copy-done((bf16[4,1280,1280]{1,2,0:T(8,128)(2,1)}, bf16[4,1280,1280]{1,2,0:T(8,128)(2,1)S(1)}, u32[]{:S(2)}) %copy-start.2) | copy-done | bytes 13107224
  143.9 0.0 copy-done.3
  143.9 15.0 %fusion.1 = bf16[3,4,320,1280]{3,2,0,1:T(8,128)(2,1)} fusion(bf16[4,1280,1280]{1,2,0:T(8,128)(2,1)S(1)} %bitcast_multiply_fusion, bf16[3,320,1280]{2,1,0:T(8,128)(2,1)S(1)} %copy-done.3), kind=kOutput, calls=%fused_computation.3 | convolution fusion | flops 12587827200 | bytes 25395200 | tf_op jit(solution)/shard_map/qac,pcd->qpad/dot_general | solution.py:41
  158.9 18.8 %all-gather.5.cloned.1.call-done = bf16[3,1280,1280]{2,1,0:T(8,128)(2,1)} async-done(((bf16[3,320,1280]{2,1,0:T(8,128)(2,1)}), bf16[3,1280,1280]{2,1,0:T(8,128)(2,1)}) %all-gather.5.cloned.1.call-update) | async-done | bytes 9830416 | tf_op jit(solution)/shard_map/all_gather | solution.py:51
  177.7 21.9 %fusion.4 = f32[4,320,1280,1]{1,2,3,0:T(8,128)} fusion(bf16[3,4,320,1280]{3,2,0,1:T(8,128)(2,1)} %fusion.1, bf16[3,1280,1280]{2,1,0:T(8,128)(2,1)} %all-gather.5.cloned.1.call-done), kind=kOutput, calls=%fused_computation.4 | convolution fusion | flops 12582912000 | bytes 26214400 | tf_op jit(solution)/shard_map/qpad,qbd->pab/dot_general | solution.py:48
  199.6 0.0 copy-start.1
  199.6 14.8 %bitcast_add_fusion = f32[4,320,1280]{1,2,0:T(8,128)} fusion(f32[4,320,1280,1]{1,2,3,0:T(8,128)} %fusion.4, bf16[4,1280,1280]{1,2,0:T(8,128)(2,1)} %copy-done.2, bf16[3,4,1280]{2,1,0:T(4,128)(2,1)S(1)} %fusion.8, bf16[3,4,320]{2,1,0:T(4,128)(2,1)S(1)} %dynamic-slice_bitcast_fusion), kind=kOutput, calls=%fused_computation.6 | convolution fusion | flops 50790400 | bytes 26252800 | tf_op jit(solution)/shard_map/qpa,qpb->pab/dot_general | solution.py:54
  214.4 0.0 reduce-scatter.2.cloned.1.call-update
  214.4 140.1 %reduce-scatter.2.cloned.1.call-done = f32[4,320,160]{1,2,0:T(8,128)} async-done(((f32[4,320,1280]{1,2,0:T(8,128)}), f32[4,320,160]{1,2,0:T(8,128)}) %reduce-scatter.2.cloned.1.call-update) | async-done | bytes 819216 | tf_op jit(solution)/shard_map/reduce_scatter | solution.py:55
  354.6 0.0 copy-done.1
  (3 shorter events, 0.0 us)
Async XLA Ops:
  6.5 7.4 %copy-start = (bf16[3,160,1280]{2,1,0:T(8,128)(2,1)S(1)}, bf16[3,160,1280]{2,1,0:T(8,128)(2,1)}, u32[]{:S(2)}) copy-start(bf16[3,160,1280]{2,1,0:T(8,128)(2,1)} %param.8) | copy-start | bytes 3686404
  6.5 7.3 %copy-start.4 = (s32[4,20,20]{2,0,1:T(4,128)S(1)}, s32[4,20,20]{2,0,1:T(4,128)}, u32[]{:S(2)}) copy-start(s32[4,20,20]{2,0,1:T(4,128)} %param.10) | copy-start | bytes 19204
  6.5 7.4 %copy-start.5 = (s32[4,2]{0,1:T(2,128)S(1)}, s32[4,2]{0,1:T(2,128)}, u32[]{:S(2)}) copy-start(s32[4,2]{0,1:T(2,128)} %param.9) | copy-start | bytes 100
  6.5 104.9 %all-gather.3.cloned.1.call-start = ((), (), s32[]{:S(2)}) async-start(), calls=%async_computation.1 | async-start | bytes 13516800 | tf_op jit(solution)/shard_map/all_gather | solution.py:39
  8.6 169.1 %all-gather.5.cloned.1.call-start = ((), (), s32[]{:S(2)}) async-start(), calls=%async_computation.2 | async-start | bytes 12288000 | tf_op jit(solution)/shard_map/all_gather | solution.py:51
  13.8 340.7 %reduce-scatter.2.cloned.1.call-start = ((), (), s32[]{:S(2)}) async-start(), calls=%async_computation.3 | async-start | bytes 8847360 | tf_op jit(solution)/shard_map/reduce_scatter | solution.py:55
  132.9 11.1 %copy-start.3 = (bf16[3,320,1280]{2,1,0:T(8,128)(2,1)S(1)}, bf16[3,320,1280]{2,1,0:T(8,128)(2,1)}, u32[]{:S(2)}) copy-start(bf16[3,320,1280]{2,1,0:T(8,128)(2,1)} %broadcast_multiply_fusion) | copy-start | bytes 7372804
  139.2 4.7 %copy-start.2 = (bf16[4,1280,1280]{1,2,0:T(8,128)(2,1)}, bf16[4,1280,1280]{1,2,0:T(8,128)(2,1)S(1)}, u32[]{:S(2)}) copy-start(bf16[4,1280,1280]{1,2,0:T(8,128)(2,1)S(1)} %bitcast_multiply_fusion) | copy-start | bytes 39321604
  199.6 155.0 %copy-start.1 = (bf16[3,160,1280]{2,1,0:T(8,128)(2,1)S(1)}, bf16[3,160,1280]{2,1,0:T(8,128)(2,1)}, u32[]{:S(2)}) copy-start(bf16[3,160,1280]{2,1,0:T(8,128)(2,1)} %param.8) | copy-start | bytes 3686404
Sparse Core Ops, SparseCore 0:
  10.2 101.1 all-gather.2
  113.0 64.6 all-gather.4
  214.5 139.9 reduce-scatter.1
where the time goes:
time: 362 us; the launch traced here: 361 us
  waiting for transfers between devices  255 us (70%)
  matrix products  52.6 us (15%)
  local copies, waits for them, and re-layouts  29.2 us (8%)
  between operations  13.2 us (4%)
  other arithmetic  10.5 us (3%)
    reduce_scatter x1, waiting for transfers between devices, local(): lax.psum_scatter(ladder + cycle, 'row', scatter_dimension=2, tiled=True)  140 us
    all_gather x1, waiting for transfers between devices, local(): whole_amp = lax.all_gather(amplitudes, ('row', 'col'), axis=1, tiled=True)  96.5 us
    dot_general x1, matrix products, local(): jnp.einsum('qpad,qbd->pab', inter, lax.all_gather(masked_int, 'col', axis...  21.9 us
    all_gather x1, local copies, waits for them, and re-layouts, local(): whole_amp = lax.all_gather(amplitudes, ('row', 'col'), axis=1, tiled=True)  21.4 us
    all_gather x1, waiting for transfers between devices, local(): lax.all_gather(masked_int, 'col', axis=1, tiled=True)  18.8 us
    dot_general x1, matrix products, local(): jnp.einsum('qac,pcd->qpad', masked_int, masked_amp, preferred_element_typ...  15 us
    dot_general x1, matrix products, local(): cycle = jnp.einsum('qpa,qpb->pab', first_here, carried)  14.8 us
  transfers between devices with their start and end apart: 3, of which 3 were waited for; matrix products, arithmetic and copies ran while one was open for 14% of the time, Pallas kernels for 0%

commit v1 on v0

v1 whole, which is shorter than its diff:
```python
import functools

import jax
import jax.numpy as jnp
from jax import lax
from jax.experimental import pallas as pl
from jax.experimental.pallas import tpu as pltpu
from jax.sharding import PartitionSpec as P

TILE = 64
BF = jnp.bfloat16
F32 = jnp.float32
VMEM = pl.BlockSpec(memory_space=pltpu.VMEM)
SMEM = pl.BlockSpec(memory_space=pltpu.SMEM)
LIMIT = 30 * 2**20


def kernel_call(body, outs, ins, scratch=(), flops=0, nbytes=0, name=None):
    return pl.pallas_call(
        body,
        out_shape=outs,
        in_specs=[SMEM] + [VMEM] * (len(ins) - 1),
        out_specs=jax.tree.map(lambda _: VMEM, outs),
        scratch_shapes=scratch,
        compiler_params=pltpu.CompilerParams(vmem_limit_bytes=LIMIT),
        cost_estimate=pl.CostEstimate(flops=flops, bytes_accessed=nbytes, transcendentals=0),
        name=name,
    )(*ins)


def like(shape, dtype):
    return jax.ShapeDtypeStruct(shape, dtype)


def place_blocks(order, ids, *refs):
    blocks, out = refs[:-1], refs[-1]
    for place, block in zip(order(ids), blocks, strict=True):
        out[place] = block[...]


def carried_terms(width, ids, second, amp, out):
    u = jnp.dot(second[...], amp[...], preferred_element_type=F32)
    high = u.astype(BF)
    low = (u - high.astype(F32)).astype(BF)
    both = jnp.concatenate([high.astype(F32)[:width], low.astype(F32)[:width]], axis=0)
    out[...] = both.T.astype(BF)


def segments(chunk, width, rows):
    found, at, end, to = [], chunk * width, (chunk + 1) * width, 0
    while at < end:
        piece, low = divmod(at, rows)
        count = min(rows - low, end - at)
        found.append((piece, low, count, to))
        at, to = at + count, to + count
    return found


def partial_sums(chunk, width, pieces, aux, block, ids, *refs):
    factors = [refs[j * aux : (j + 1) * aux] for j in range(pieces)]
    amp, carried, first, keep, send, picked, inter, total = refs[pieces * aux :]
    rows = factors[0][0].shape[0]
    size = amp.shape[1]
    col, low = ids[0], ids[1]
    for piece, start, count, to in segments(chunk, width, rows):
        for q in range(aux):
            picked[pl.ds(q * width + to, count), :] = factors[piece][q][start : start + count, :]

    step = 256 if size % 256 == 0 else size

    def columns(i, _):
        at = pl.ds(pl.multiple_of(i * step, step), step)
        inter[:, at] = jnp.dot(picked[...], amp[:, at], preferred_element_type=F32).astype(BF)
        return 0

    lax.fori_loop(0, size // step, columns, 0)
    for j in range(pieces):
        at = pl.ds(pl.multiple_of((col ^ j) * rows, 16), rows)
        value = jnp.dot(carried[at, :], first[...], preferred_element_type=F32)
        for q in range(aux):
            value += lax.dot_general(
                factors[j][q][...],
                inter[pl.ds(q * width, width), :],
                (((1,), (1,)), ((), ())),
                preferred_element_type=F32,
            )
        total[at, :] = value
    for h in range(keep.shape[0]):
        mine = pl.multiple_of((2 * h + low) * block, 8)
        theirs = pl.multiple_of((2 * h + 1 - low) * block, 8)
        keep[h] = total[pl.ds(mine, block), :]
        send[h] = total[pl.ds(theirs, block), :].astype(BF)


def add_and_split(ids, keep, got, own, *messages):
    high = ids[2]
    own[...] = keep[high] + got[high].astype(F32)
    for k, message in enumerate(messages, 1):
        message[...] = (keep[high ^ k] + got[high ^ k].astype(F32)).astype(BF)


def add_up(ids, own, *refs):
    value = own[...]
    for got in refs[:-1]:
        value += got[...].astype(F32)
    refs[-1][...] = value


def finish(ids, *refs):
    out = refs[-1]
    for k, part in enumerate(refs[:-1]):
        out[ids[0] ^ k] = part[...].T


def local(n_row, n_col, amplitudes, integrals, occupied, pairs, amp_tiles, int_tiles):
    n_pair, chunk_rows, size = amplitudes.shape
    aux, piece_rows, _ = integrals.shape
    n_high = n_row // 2
    block = size // n_row
    col, row = lax.axis_index("col"), lax.axis_index("row")
    low, high = row % 2, row // 2
    ids = jnp.stack([col, low, high, row]).astype(jnp.int32)

    def over_col(x, k):
        return lax.ppermute(x, "col", [(i, i ^ k) for i in range(n_col)])

    def over_low(x):
        return lax.ppermute(x, "row", [(i, i ^ 1) for i in range(n_row)])

    def over_high(x, k):
        return lax.ppermute(x, "row", [(i, (i // 2 ^ k) * 2 + i % 2) for i in range(n_row)])

    def up(x):
        return lax.ppermute(x, "row", [(i, (i + 2) % n_row) for i in range(n_row)])

    tiles_here = piece_rows // TILE
    own_tiles = lax.dynamic_slice_in_dim(int_tiles, col * tiles_here, tiles_here, 0)
    int_mask = jnp.repeat(jnp.repeat(own_tiles.astype(BF), TILE, axis=0), TILE, axis=1)
    factors = [None] * n_col
    factors[0] = [integrals[q] * int_mask for q in range(aux)]
    factors[2] = [over_col(x, 2) for x in factors[0]]
    factors[1] = [over_col(x, 1) for x in factors[0]]
    factors[3] = [over_col(x, 1) for x in factors[2]]

    tile_of = ((row * n_col + col) * chunk_rows + jnp.arange(chunk_rows, dtype=jnp.int32)) // TILE
    picker = (tile_of[:, None] == jnp.arange(amp_tiles.shape[1], dtype=jnp.int32)[None, :]).astype(BF)
    row_mask = jnp.einsum("nk,pkm->pnm", picker, amp_tiles.astype(BF))
    masked = amplitudes * jnp.repeat(row_mask, TILE, axis=2)
    mine = [lax.dynamic_index_in_dim(masked, col ^ k, 0, keepdims=False) for k in range(n_col)]
    mine = [mine[0]] + [over_col(mine[k], k) for k in range(1, n_col)]
    slab = kernel_call(
        functools.partial(place_blocks, lambda ids: [ids[0] ^ k for k in range(n_col)]),
        like((n_col, chunk_rows, size), BF),
        (ids, *mine),
        nbytes=4 * n_col * chunk_rows * size,
        name="own_rows",
    ).reshape(n_col * chunk_rows, size)
    slabs = [slab]
    for _ in range(n_high - 1):
        slabs.append(up(slabs[-1]))
    slabs = slabs + [over_low(x) for x in slabs]

    def slab_places(ids):
        ring = [lax.rem(ids[2] + (n_high - s), n_high) * 2 for s in range(n_high)]
        return [h + ids[1] for h in ring] + [h + 1 - ids[1] for h in ring]

    amp = kernel_call(
        functools.partial(place_blocks, slab_places),
        like((n_row, n_col * chunk_rows, size), BF),
        (ids, *slabs),
        nbytes=4 * size * size,
        name="all_rows",
    ).reshape(size, size)

    pair = lax.dynamic_index_in_dim(pairs, col, 0, keepdims=False)
    first = lax.dynamic_index_in_dim(occupied, pair[0], 1, keepdims=False)
    second = lax.dynamic_index_in_dim(occupied, pair[1], 1, keepdims=False)
    second = jnp.concatenate([second, jnp.zeros((16 - aux, size), BF)], axis=0)
    first = first.reshape(aux, n_col, piece_rows)
    first = jnp.concatenate(
        [lax.dynamic_index_in_dim(first, col ^ k, 1, keepdims=False) for k in range(n_col)], axis=1
    )
    first = jnp.concatenate([first, first], axis=0)
    carried = kernel_call(
        functools.partial(carried_terms, aux),
        like((size, 2 * aux), BF),
        (ids, second, amp),
        flops=32 * size * size,
        nbytes=2 * size * size,
        name="carried",
    )

    width = 256 if size % 256 == 0 else piece_rows
    flat = [x for piece in factors for x in piece]
    sums = []
    for c in range(size // width):
        keep, send = kernel_call(
            functools.partial(partial_sums, c, width, n_col, aux, block),
            (like((n_high, block, width), F32), like((n_high, block, width), BF)),
            (ids, *flat, amp, carried, first[:, c * width : (c + 1) * width]),
            scratch=[
                pltpu.VMEM((aux * width, size), BF),
                pltpu.VMEM((aux * width, size), BF),
                pltpu.VMEM((size, width), F32),
            ],
            flops=4 * aux * width * size * size,
            nbytes=2 * size * size,
            name="partial_sums",
        )
        got = over_low(send)
        own, *messages = kernel_call(
            add_and_split,
            (like((block, width), F32),) + (like((block, width), BF),) * (n_high - 1),
            (ids, keep, got),
            nbytes=10 * n_high * block * width,
            name="add_low",
        )
        messages = [over_high(m, k) for k, m in enumerate(messages, 1)]
        sums.append(
            kernel_call(
                add_up, like((block, width), F32), (ids, own, *messages), nbytes=14 * block * width, name="add_high"
            )
        )
    whole = jnp.concatenate(sums, axis=1)
    parts = [whole[:, k * piece_rows : (k + 1) * piece_rows] for k in range(n_col)]
    parts = [parts[0]] + [over_col(parts[k], k) for k in range(1, n_col)]
    return kernel_call(
        finish, like((n_pair, piece_rows, block), F32), (ids, *parts), nbytes=8 * n_pair * piece_rows * block, name="finish"
    )


def solution(mesh):
    placed = (
        P(None, ("row", "col"), None),
        P("row", "col", None),
        P("row", None, None),
        P(),
        P(),
        P(),
    )
    return jax.shard_map(
        functools.partial(local, mesh.shape["row"], mesh.shape["col"]),
        mesh=mesh,
        in_specs=placed,
        out_specs=P(None, "col", "row"),
        check_vma=False,
    )
```

time: 362 us -> 198 us (0.55)
  waiting for transfers between devices: 255 us -> 67.7 us
  Pallas kernels: 0 us -> 56.6 us
  matrix products: 52.6 us -> 0.19 us
  starting transfers between devices: 0.09 us -> 46.5 us
  local copies, waits for them, and re-layouts: 29.2 us -> 17.7 us
  between operations: 13.2 us -> 4.23 us
  other arithmetic: 10.5 us -> 4.05 us
    reduce_scatter x1 -> x0, waiting for transfers between devices: 140 us -> none  [local(): lax.psum_scatter(ladder + cycle, 'row', scatter_dimension=2, tiled=True)]
    all_gather x2 -> x0, waiting for transfers between devices: 115 us -> none  [the longest x1 96.5 us: local(): whole_amp = lax.all_gather(amplitudes, ('row', 'col'), axis=1, tiled=True)]
    ppermute x0 -> x42, waiting for transfers between devices: none -> 67.7 us  [the longest x15 43.4 us: over_col(): return lax.ppermute(x, 'col', [(i, i ^ k) for i in range(n_col)])]
    pallas_call x0 -> x19, Pallas kernels: none -> 56.6 us  [kernel_call(): pl.pallas_call(body, out_shape=outs, in_specs=[SMEM] + [VMEM] * (len(ins)...]
    dot_general x6 -> x1, matrix products: 52.6 us -> 0.19 us  [local(): row_mask = jnp.einsum('nk,pkm->pnm', picker, amp_tiles.astype(BF))]
    ppermute x0 -> x42, starting transfers between devices: none -> 46.5 us  [the longest x15 25.9 us: over_high(): lax.ppermute(x, 'row', [(i, (i // 2 ^ k) * 2 + i % 2) for i in range(n_ro...]
    all_gather x1 -> x0, local copies, waits for them, and re-layouts: 21.4 us -> none  [local(): whole_amp = lax.all_gather(amplitudes, ('row', 'col'), axis=1, tiled=True)]
    mul x2, other arithmetic: 9.81 us -> 2.17 us  [the longest x1 2.07 us: local(): factors[0] = [integrals[q] * int_mask for q in range(aux)]]
  transfers between devices with their start and end apart: 3 -> 42, of which waited for: 3 -> 13; matrix products, arithmetic and copies ran while one was open for 14% -> 3% of each run, Pallas kernels for 0% -> 23%
where the time goes in v1:
time: 198 us; the launch traced here: 197 us
  waiting for transfers between devices  67.7 us (34%)
  Pallas kernels  56.6 us (29%)
  starting transfers between devices  46.5 us (23%)
  local copies, waits for them, and re-layouts  17.7 us (9%)
  between operations  4.23 us (2%)
  other arithmetic  4.05 us (2%)
    pallas_call x19, Pallas kernels, kernel_call(): pl.pallas_call(body, out_shape=outs, in_specs=[SMEM] + [VMEM] * (len(ins)...  56.6 us
    ppermute x15, waiting for transfers between devices, over_col(): return lax.ppermute(x, 'col', [(i, i ^ k) for i in range(n_col)])  43.4 us
    ppermute x15, starting transfers between devices, over_high(): lax.ppermute(x, 'row', [(i, (i // 2 ^ k) * 2 + i % 2) for i in range(n_ro...  25.9 us
    ppermute x3, waiting for transfers between devices, up(): return lax.ppermute(x, 'row', [(i, (i + 2) % n_row) for i in range(n_row)])  16.4 us
    unnamed x35, local copies, waits for them, and re-layouts  11.6 us
    ppermute x15, starting transfers between devices, over_col(): return lax.ppermute(x, 'col', [(i, i ^ k) for i in range(n_col)])  9.52 us
    ppermute x9, starting transfers between devices, over_low(): return lax.ppermute(x, 'row', [(i, i ^ 1) for i in range(n_row)])  9.38 us
    ppermute x15, waiting for transfers between devices, over_high(): lax.ppermute(x, 'row', [(i, (i // 2 ^ k) * 2 + i % 2) for i in range(n_ro...  5.66 us
  transfers between devices with their start and end apart: 42, of which 13 were waited for; matrix products, arithmetic and copies ran while one was open for 3% of the time, Pallas kernels for 23%

profile of v1, /device:TPU:0, one launch (start us, length us, event | category | flops | bytes accessed | tf_op | source)
XLA Modules:
  0.0 197.0 jit_solution(3850612785374434864)
XLA Ops:
  2.5 3.0 %collective-permute-start.10 = (bf16[40,1280]{1,0:T(8,128)(2,1)S(1)}, bf16[40,1280]{1,0:T(8,128)(2,1)S(1)}, u32[]{:S(2)}, u32[]{:S(2)}) collective-permute-start(bf16[40,1280]{1,0:T(8,128)(2,1)S(1)} %get-tuple-element.71), channel_id=1, source_target_pairs={{0,2},{1,3},{2,0},{3,1},{4,6},{5,7},{6,4},{7,5},{8,10},{9,11},{10,... | collective-permute-start | bytes 307208 | tf_op jit(solution)/shard_map/ppermute | solution.py:125
  6.8 1.3 copy.18
  8.8 1.8 collective-permute-done.11.refs_3_
  11.2 1.7 collective-permute-start.12
  12.9 2.1 %bitcast_multiply_fusion = (bf16[320,1280]{1,0:T(8,128)(2,1)S(1)}, bf16[320,1280]{1,0:T(8,128)(2,1)S(1)}, bf16[320,1280]{1,0:T(8,128)(2,1)S(1)}) fusion(bf16[320,1280]{1,0:T(8,128)(2,1)} %copy.18, bf16[3,320,1280]{2,1,0:T(8,128)(2,1)} %param.7), kind=kLoop, calls=%fused_computation.1 | loop fusion | flops 1228800 | bytes 5734400 | tf_op jit(solution)/shard_map/mul | solution.py:140
  14.9 1.6 collective-permute-start.15
  17.1 1.5 collective-permute-start.4
  18.6 6.1 %collective-permute-done.12.refs_1_ = bf16[160,1280]{1,0:T(8,128)(2,1)S(1)} collective-permute-done((bf16[160,1280]{1,0:T(8,128)(2,1)S(1)}, bf16[160,1280]{1,0:T(8,128)(2,1)S(1)}, u32[]{:S(2)}, u32[]{:S(2)}) %collective-permute-start.12) | collective-permute-done | bytes 409632 | tf_op jit(solution)/shard_map/ppermute | solution.py:134
  24.6 1.3 collective-permute-start.5
  27.0 10.3 %collective-permute-done.13.refs_2_ = bf16[160,1280]{1,0:T(8,128)(2,1)S(1)} collective-permute-done((bf16[160,1280]{1,0:T(8,128)(2,1)S(1)}, bf16[160,1280]{1,0:T(8,128)(2,1)S(1)}, u32[]{:S(2)}, u32[]{:S(2)}) %collective-permute-start.13) | collective-permute-done | bytes 409632 | tf_op jit(solution)/shard_map/ppermute | solution.py:134
  38.7 16.7 %collective-permute-done.4.refs_7_ = bf16[320,1280]{1,0:T(8,128)(2,1)} collective-permute-done((bf16[320,1280]{1,0:T(8,128)(2,1)S(1)}, bf16[320,1280]{1,0:T(8,128)(2,1)}, u32[]{:S(2)}, u32[]{:S(2)}) %collective-permute-start.4) | collective-permute-done | bytes 819232 | tf_op jit(solution)/shard_map/ppermute | solution.py:125
  56.6 1.5 collective-permute-start.18
  59.0 12.4 %collective-permute-done.5.refs_8_ = bf16[320,1280]{1,0:T(8,128)(2,1)} collective-permute-done((bf16[320,1280]{1,0:T(8,128)(2,1)S(1)}, bf16[320,1280]{1,0:T(8,128)(2,1)}, u32[]{:S(2)}, u32[]{:S(2)}) %collective-permute-start.5) | collective-permute-done | bytes 819232 | tf_op jit(solution)/shard_map/ppermute | solution.py:125
  71.5 0.9 copy-done.13
  80.0 0.9 dynamic-slice_reduce_fusion
  81.3 1.0 copy-done.2
  82.3 1.0 copy-done.4
  83.3 1.0 copy-done.6
  84.3 1.0 copy-done.8
  85.3 1.0 copy-done.10
  86.3 1.0 copy-done.12
  88.1 1.2 carried.1.refs_13_
  89.4 9.4 %partial_sums.5 = (f32[4,160,256]{2,1,0:T(8,128)S(1)}, bf16[4,160,256]{2,1,0:T(8,128)(2,1)S(1)}) custom-call(s32[4]{0:T(128)S(1)} %pad_add_fusion.ids, bf16[320,1280]{1,0:T(8,128)(2,1)S(1)} %get-tuple-element.67.refs_0_, bf16[320,1280]{1,0:T(8,128)(2,1)S(1)} %get-tuple-element.66.refs_1_, bf16[320,1280]{1,0:T(8,128)(2,1)S(1)} %get-tuple-element.65.refs_2_, ...), custom_call_target="tpu_custom_call" | custom-call | flops 5033164800 | bytes 3276800 | tf_op jit(solution)/shard_map/partial_sums/pallas_call | solution.py:19
  99.3 9.4 %partial_sums.6 = (f32[4,160,256]{2,1,0:T(8,128)S(1)}, bf16[4,160,256]{2,1,0:T(8,128)(2,1)S(1)}) custom-call(s32[4]{0:T(128)S(1)} %pad_add_fusion.ids, bf16[320,1280]{1,0:T(8,128)(2,1)S(1)} %get-tuple-element.67.refs_0_, bf16[320,1280]{1,0:T(8,128)(2,1)S(1)} %get-tuple-element.66.refs_1_, bf16[320,1280]{1,0:T(8,128)(2,1)S(1)} %get-tuple-element.65.refs_2_, ...), custom_call_target="tpu_custom_call" | custom-call | flops 5033164800 | bytes 3276800 | tf_op jit(solution)/shard_map/partial_sums/pallas_call | solution.py:19
  108.7 1.6 collective-permute-start.23
  110.3 9.4 %partial_sums.7 = (f32[4,160,256]{2,1,0:T(8,128)S(1)}, bf16[4,160,256]{2,1,0:T(8,128)(2,1)S(1)}) custom-call(s32[4]{0:T(128)S(1)} %pad_add_fusion.ids, bf16[320,1280]{1,0:T(8,128)(2,1)S(1)} %get-tuple-element.67.refs_0_, bf16[320,1280]{1,0:T(8,128)(2,1)S(1)} %get-tuple-element.66.refs_1_, bf16[320,1280]{1,0:T(8,128)(2,1)S(1)} %get-tuple-element.65.refs_2_, ...), custom_call_target="tpu_custom_call" | custom-call | flops 5033164800 | bytes 3276800 | tf_op jit(solution)/shard_map/partial_sums/pallas_call | solution.py:19
  120.3 9.4 %partial_sums.8 = (f32[4,160,256]{2,1,0:T(8,128)S(1)}, bf16[4,160,256]{2,1,0:T(8,128)(2,1)S(1)}) custom-call(s32[4]{0:T(128)S(1)} %pad_add_fusion.ids, bf16[320,1280]{1,0:T(8,128)(2,1)S(1)} %get-tuple-element.67.refs_0_, bf16[320,1280]{1,0:T(8,128)(2,1)S(1)} %get-tuple-element.66.refs_1_, bf16[320,1280]{1,0:T(8,128)(2,1)S(1)} %get-tuple-element.65.refs_2_, ...), custom_call_target="tpu_custom_call" | custom-call | flops 5033164800 | bytes 3276800 | tf_op jit(solution)/shard_map/partial_sums/pallas_call | solution.py:19
  129.7 1.6 collective-permute-start.32
  131.3 9.6 %partial_sums.9 = (f32[4,160,256]{2,1,0:T(8,128)S(1)}, bf16[4,160,256]{2,1,0:T(8,128)(2,1)S(1)}) custom-call(s32[4]{0:T(128)S(1)} %pad_add_fusion.ids, bf16[320,1280]{1,0:T(8,128)(2,1)S(1)} %get-tuple-element.67.refs_0_, bf16[320,1280]{1,0:T(8,128)(2,1)S(1)} %get-tuple-element.66.refs_1_, bf16[320,1280]{1,0:T(8,128)(2,1)S(1)} %get-tuple-element.65.refs_2_, ...), custom_call_target="tpu_custom_call" | custom-call | flops 5033164800 | bytes 3276800 | tf_op jit(solution)/shard_map/partial_sums/pallas_call | solution.py:19
  142.1 1.7 collective-permute-start.20
  143.8 1.3 collective-permute-start.21
  145.7 1.5 collective-permute-start.22
  147.9 2.0 %collective-permute-done.37.got = bf16[4,160,256]{2,1,0:T(8,128)(2,1)S(1)} collective-permute-done((bf16[4,160,256]{2,1,0:T(8,128)(2,1)S(1)}, bf16[4,160,256]{2,1,0:T(8,128)(2,1)S(1)}, u32[]{:S(2)}, u32[]{:S(2)}) %collective-permute-start.37) | collective-permute-done | bytes 327712 | tf_op jit(solution)/shard_map/ppermute | solution.py:128
  150.0 2.6 %collective-permute-start.25 = (bf16[160,256]{1,0:T(8,128)(2,1)S(1)}, bf16[160,256]{1,0:T(8,128)(2,1)S(1)}, u32[]{:S(2)}, u32[]{:S(2)}) collective-permute-start(bf16[160,256]{1,0:T(8,128)(2,1)S(1)} %get-tuple-element.45), channel_id=1, source_target_pairs={{0,16},{4,20},{8,24},{12,28},{16,0},{20,4},{24,8},{28,12},{1,17},{... | collective-permute-start | bytes 245768 | tf_op jit(solution)/shard_map/ppermute | solution.py:131
  153.8 1.4 collective-permute-start.26
  155.2 3.0 %collective-permute-start.29 = (bf16[160,256]{1,0:T(8,128)(2,1)S(1)}, bf16[160,256]{1,0:T(8,128)(2,1)S(1)}, u32[]{:S(2)}, u32[]{:S(2)}) collective-permute-start(bf16[160,256]{1,0:T(8,128)(2,1)S(1)} %get-tuple-element.51), channel_id=1, source_target_pairs={{0,16},{4,20},{8,24},{12,28},{16,0},{20,4},{24,8},{28,12},{1,17},{... | collective-permute-start | bytes 245768 | tf_op jit(solution)/shard_map/ppermute | solution.py:131
  158.3 1.3 collective-permute-start.30
  159.6 1.3 collective-permute-done.25.refs_1_
  161.6 5.4 %collective-permute-start.34 = (bf16[160,256]{1,0:T(8,128)(2,1)S(1)}, bf16[160,256]{1,0:T(8,128)(2,1)S(1)}, u32[]{:S(2)}, u32[]{:S(2)}) collective-permute-start(bf16[160,256]{1,0:T(8,128)(2,1)S(1)} %get-tuple-element.57), channel_id=1, source_target_pairs={{0,16},{4,20},{8,24},{12,28},{16,0},{20,4},{24,8},{28,12},{1,17},{... | collective-permute-start | bytes 245768 | tf_op jit(solution)/shard_map/ppermute | solution.py:131
  167.0 1.4 collective-permute-start.35
  168.4 2.9 %collective-permute-start.39 = (bf16[160,256]{1,0:T(8,128)(2,1)S(1)}, bf16[160,256]{1,0:T(8,128)(2,1)S(1)}, u32[]{:S(2)}, u32[]{:S(2)}) collective-permute-start(bf16[160,256]{1,0:T(8,128)(2,1)S(1)} %get-tuple-element.63), channel_id=1, source_target_pairs={{0,16},{4,20},{8,24},{12,28},{16,0},{20,4},{24,8},{28,12},{1,17},{... | collective-permute-start | bytes 245768 | tf_op jit(solution)/shard_map/ppermute | solution.py:131
  171.4 2.6 %collective-permute-start.40 = (bf16[160,256]{1,0:T(8,128)(2,1)S(1)}, bf16[160,256]{1,0:T(8,128)(2,1)S(1)}, u32[]{:S(2)}, u32[]{:S(2)}) collective-permute-start(bf16[160,256]{1,0:T(8,128)(2,1)S(1)} %get-tuple-element.64), channel_id=1, source_target_pairs={{0,24},{4,28},{8,16},{12,20},{16,8},{20,12},{24,0},{28,4},{1,25},{... | collective-permute-start | bytes 245768 | tf_op jit(solution)/shard_map/ppermute | solution.py:131
  176.3 4.3 %collective-permute-done.39.refs_1_ = bf16[160,256]{1,0:T(8,128)(2,1)S(1)} collective-permute-done((bf16[160,256]{1,0:T(8,128)(2,1)S(1)}, bf16[160,256]{1,0:T(8,128)(2,1)S(1)}, u32[]{:S(2)}, u32[]{:S(2)}) %collective-permute-start.39) | collective-permute-done | bytes 81952 | tf_op jit(solution)/shard_map/ppermute | solution.py:131
  181.5 1.4 collective-permute-start.36
  183.3 7.0 %collective-permute-done.36.refs_2_ = f32[160,320]{1,0:T(8,128)S(1)} collective-permute-done((f32[160,320]{1,0:T(8,128)S(1)}, f32[160,320]{1,0:T(8,128)S(1)}, u32[]{:S(2)}, u32[]{:S(2)}) %collective-permute-start.36) | collective-permute-done | bytes 204832 | tf_op jit(solution)/shard_map/ppermute | solution.py:125
  190.3 4.4 %collective-permute-done.41.refs_3_ = f32[160,320]{1,0:T(8,128)S(1)} collective-permute-done((f32[160,320]{1,0:T(8,128)S(1)}, f32[160,320]{1,0:T(8,128)S(1)}, u32[]{:S(2)}, u32[]{:S(2)}) %collective-permute-start.41) | collective-permute-done | bytes 204832 | tf_op jit(solution)/shard_map/ppermute | solution.py:125
  194.7 1.0 finish.1
  195.6 1.4 copy.23
  (116 shorter events, 24.2 us)
Async XLA Ops:
  0.0 58.9 %copy-start = (s32[4,2]{0,1:T(2,128)S(1)}, s32[4,2]{0,1:T(2,128)}, u32[]{:S(2)}) copy-start(s32[4,2]{0,1:T(2,128)} %param.9) | copy-start | bytes 100
  0.0 2.3 %copy-start.15 = (bf16[4,40,1280]{2,1,0:T(8,128)(2,1)S(1)}, bf16[4,40,1280]{2,1,0:T(8,128)(2,1)}, u32[]{:S(2)}) copy-start(bf16[4,40,1280]{2,1,0:T(8,128)(2,1)} %param.6) | copy-start | bytes 1228804
  2.5 6.3 %collective-permute-start.10 = (bf16[40,1280]{1,0:T(8,128)(2,1)S(1)}, bf16[40,1280]{1,0:T(8,128)(2,1)S(1)}, u32[]{:S(2)}, u32[]{:S(2)}) collective-permute-start(bf16[40,1280]{1,0:T(8,128)(2,1)S(1)} %get-tuple-element.71), channel_id=1, source_target_pairs={{0,2},{1,3},{2,0},{3,1},{4,6},{5,7},{6,4},{7,5},{8,10},{9,11},{10,... | collective-permute-start | bytes 307208 | tf_op jit(solution)/shard_map/ppermute | solution.py:125
  5.5 5.1 %collective-permute-start.11 = (bf16[40,1280]{1,0:T(8,128)(2,1)S(1)}, bf16[40,1280]{1,0:T(8,128)(2,1)S(1)}, u32[]{:S(2)}, u32[]{:S(2)}) collective-permute-start(bf16[40,1280]{1,0:T(8,128)(2,1)S(1)} %get-tuple-element.70), channel_id=1, source_target_pairs={{0,3},{1,2},{2,1},{3,0},{4,7},{5,6},{6,5},{7,4},{8,11},{9,10},{10,... | collective-permute-start | bytes 307208 | tf_op jit(solution)/shard_map/ppermute | solution.py:125
  5.5 5.1 %collective-permute-start.9 = (bf16[40,1280]{1,0:T(8,128)(2,1)S(1)}, bf16[40,1280]{1,0:T(8,128)(2,1)S(1)}, u32[]{:S(2)}, u32[]{:S(2)}) collective-permute-start(bf16[40,1280]{1,0:T(8,128)(2,1)S(1)} %get-tuple-element.72), channel_id=1, source_target_pairs={{0,1},{1,0},{2,3},{3,2},{4,5},{5,4},{6,7},{7,6},{8,9},{9,8},{10,11... | collective-permute-start | bytes 307208 | tf_op jit(solution)/shard_map/ppermute | solution.py:125
  11.2 13.5 %collective-permute-start.12 = (bf16[160,1280]{1,0:T(8,128)(2,1)S(1)}, bf16[160,1280]{1,0:T(8,128)(2,1)S(1)}, u32[]{:S(2)}, u32[]{:S(2)}) collective-permute-start(bf16[160,1280]{1,0:T(8,128)(2,1)S(1)} %bitcast.47), channel_id=1, source_target_pairs={{0,8},{4,12},{8,16},{12,20},{16,24},{20,28},{24,0},{28,4},{1,9},{5... | collective-permute-start | bytes 1228808 | tf_op jit(solution)/shard_map/ppermute | solution.py:134
  14.9 11.3 %collective-permute-start.15 = (bf16[160,1280]{1,0:T(8,128)(2,1)S(1)}, bf16[160,1280]{1,0:T(8,128)(2,1)S(1)}, u32[]{:S(2)}, u32[]{:S(2)}) collective-permute-start(bf16[160,1280]{1,0:T(8,128)(2,1)S(1)} %bitcast.48), channel_id=1, source_target_pairs={{0,4},{4,0},{8,12},{12,8},{16,20},{20,16},{24,28},{28,24},{1,5},{5... | collective-permute-start | bytes 1228808 | tf_op jit(solution)/shard_map/ppermute | solution.py:128
  16.5 21.3 %collective-permute-start.3 = (bf16[320,1280]{1,0:T(8,128)(2,1)S(1)}, bf16[320,1280]{1,0:T(8,128)(2,1)}, u32[]{:S(2)}, u32[]{:S(2)}) collective-permute-start(bf16[320,1280]{1,0:T(8,128)(2,1)S(1)} %get-tuple-element.67.refs_0_), channel_id=1, source_target_pairs={{0,2},{1,3},{2,0},{3,1},{4,6},{5,7},{6,4},{7,5},{8,10},{9,11},{10,... | collective-permute-start | bytes 2457608 | tf_op jit(solution)/shard_map/ppermute | solution.py:125
  17.1 38.3 %collective-permute-start.4 = (bf16[320,1280]{1,0:T(8,128)(2,1)S(1)}, bf16[320,1280]{1,0:T(8,128)(2,1)}, u32[]{:S(2)}, u32[]{:S(2)}) collective-permute-start(bf16[320,1280]{1,0:T(8,128)(2,1)S(1)} %get-tuple-element.66.refs_1_), channel_id=1, source_target_pairs={{0,2},{1,3},{2,0},{3,1},{4,6},{5,7},{6,4},{7,5},{8,10},{9,11},{10,... | collective-permute-start | bytes 2457608 | tf_op jit(solution)/shard_map/ppermute | solution.py:125
  24.6 12.6 %collective-permute-start.13 = (bf16[160,1280]{1,0:T(8,128)(2,1)S(1)}, bf16[160,1280]{1,0:T(8,128)(2,1)S(1)}, u32[]{:S(2)}, u32[]{:S(2)}) collective-permute-start(bf16[160,1280]{1,0:T(8,128)(2,1)S(1)} %collective-permute-done.12.refs_1_), channel_id=1, source_target_pairs={{0,8},{4,12},{8,16},{12,20},{16,24},{20,28},{24,0},{28,4},{1,9},{5... | collective-permute-start | bytes 1228808 | tf_op jit(solution)/shard_map/ppermute | solution.py:134
  24.6 46.8 %collective-permute-start.5 = (bf16[320,1280]{1,0:T(8,128)(2,1)S(1)}, bf16[320,1280]{1,0:T(8,128)(2,1)}, u32[]{:S(2)}, u32[]{:S(2)}) collective-permute-start(bf16[320,1280]{1,0:T(8,128)(2,1)S(1)} %get-tuple-element.65.refs_2_), channel_id=1, source_target_pairs={{0,2},{1,3},{2,0},{3,1},{4,6},{5,7},{6,4},{7,5},{8,10},{9,11},{10,... | collective-permute-start | bytes 2457608 | tf_op jit(solution)/shard_map/ppermute | solution.py:125
  27.0 44.5 %collective-permute-start = (bf16[320,1280]{1,0:T(8,128)(2,1)S(1)}, bf16[320,1280]{1,0:T(8,128)(2,1)S(1)}, u32[]{:S(2)}, u32[]{:S(2)}) collective-permute-start(bf16[320,1280]{1,0:T(8,128)(2,1)S(1)} %get-tuple-element.67.refs_0_), channel_id=1, source_target_pairs={{0,1},{1,0},{2,3},{3,2},{4,5},{5,4},{6,7},{7,6},{8,9},{9,8},{10,11... | collective-permute-start | bytes 2457608 | tf_op jit(solution)/shard_map/ppermute | solution.py:125
  37.3 19.4 %collective-permute-start.14 = (bf16[160,1280]{1,0:T(8,128)(2,1)S(1)}, bf16[160,1280]{1,0:T(8,128)(2,1)S(1)}, u32[]{:S(2)}, u32[]{:S(2)}) collective-permute-start(bf16[160,1280]{1,0:T(8,128)(2,1)S(1)} %collective-permute-done.13.refs_2_), channel_id=1, source_target_pairs={{0,8},{4,12},{8,16},{12,20},{16,24},{20,28},{24,0},{28,4},{1,9},{5... | collective-permute-start | bytes 1228808 | tf_op jit(solution)/shard_map/ppermute | solution.py:134
  37.8 35.1 %collective-permute-start.16 = (bf16[160,1280]{1,0:T(8,128)(2,1)S(1)}, bf16[160,1280]{1,0:T(8,128)(2,1)S(1)}, u32[]{:S(2)}, u32[]{:S(2)}) collective-permute-start(bf16[160,1280]{1,0:T(8,128)(2,1)S(1)} %collective-permute-done.12.refs_1_), channel_id=1, source_target_pairs={{0,4},{4,0},{8,12},{12,8},{16,20},{20,16},{24,28},{28,24},{1,5},{5... | collective-permute-start | bytes 1228808 | tf_op jit(solution)/shard_map/ppermute | solution.py:128
  55.4 18.3 %collective-permute-start.17 = (bf16[160,1280]{1,0:T(8,128)(2,1)S(1)}, bf16[160,1280]{1,0:T(8,128)(2,1)S(1)}, u32[]{:S(2)}, u32[]{:S(2)}) collective-permute-start(bf16[160,1280]{1,0:T(8,128)(2,1)S(1)} %collective-permute-done.13.refs_2_), channel_id=1, source_target_pairs={{0,4},{4,0},{8,12},{12,8},{16,20},{20,16},{24,28},{28,24},{1,5},{5... | collective-permute-start | bytes 1228808 | tf_op jit(solution)/shard_map/ppermute | solution.py:128
  56.6 18.3 %collective-permute-start.18 = (bf16[160,1280]{1,0:T(8,128)(2,1)S(1)}, bf16[160,1280]{1,0:T(8,128)(2,1)S(1)}, u32[]{:S(2)}, u32[]{:S(2)}) collective-permute-start(bf16[160,1280]{1,0:T(8,128)(2,1)S(1)} %collective-permute-done.14.refs_3_), channel_id=1, source_target_pairs={{0,4},{4,0},{8,12},{12,8},{16,20},{20,16},{24,28},{28,24},{1,5},{5... | collective-permute-start | bytes 1228808 | tf_op jit(solution)/shard_map/ppermute | solution.py:128
  71.5 17.8 %collective-permute-start.1 = (bf16[320,1280]{1,0:T(8,128)(2,1)S(1)}, bf16[320,1280]{1,0:T(8,128)(2,1)}, u32[]{:S(2)}, u32[]{:S(2)}) collective-permute-start(bf16[320,1280]{1,0:T(8,128)(2,1)S(1)} %get-tuple-element.66.refs_1_), channel_id=1, source_target_pairs={{0,1},{1,0},{2,3},{3,2},{4,5},{5,4},{6,7},{7,6},{8,9},{9,8},{10,11... | collective-permute-start | bytes 2457608 | tf_op jit(solution)/shard_map/ppermute | solution.py:125
  72.3 17.0 %collective-permute-start.2 = (bf16[320,1280]{1,0:T(8,128)(2,1)S(1)}, bf16[320,1280]{1,0:T(8,128)(2,1)}, u32[]{:S(2)}, u32[]{:S(2)}) collective-permute-start(bf16[320,1280]{1,0:T(8,128)(2,1)S(1)} %get-tuple-element.65.refs_2_), channel_id=1, source_target_pairs={{0,1},{1,0},{2,3},{3,2},{4,5},{5,4},{6,7},{7,6},{8,9},{9,8},{10,11... | collective-permute-start | bytes 2457608 | tf_op jit(solution)/shard_map/ppermute | solution.py:125
  73.7 15.6 %collective-permute-start.6 = (bf16[320,1280]{1,0:T(8,128)(2,1)}, bf16[320,1280]{1,0:T(8,128)(2,1)}, u32[]{:S(2)}, u32[]{:S(2)}) collective-permute-start(bf16[320,1280]{1,0:T(8,128)(2,1)} %collective-permute-done.3.refs_6_), channel_id=1, source_target_pairs={{0,1},{1,0},{2,3},{3,2},{4,5},{5,4},{6,7},{7,6},{8,9},{9,8},{10,11... | collective-permute-start | bytes 2457608 | tf_op jit(solution)/shard_map/ppermute | solution.py:125
  74.4 14.9 %collective-permute-start.7 = (bf16[320,1280]{1,0:T(8,128)(2,1)}, bf16[320,1280]{1,0:T(8,128)(2,1)}, u32[]{:S(2)}, u32[]{:S(2)}) collective-permute-start(bf16[320,1280]{1,0:T(8,128)(2,1)} %collective-permute-done.4.refs_7_), channel_id=1, source_target_pairs={{0,1},{1,0},{2,3},{3,2},{4,5},{5,4},{6,7},{7,6},{8,9},{9,8},{10,11... | collective-permute-start | bytes 2457608 | tf_op jit(solution)/shard_map/ppermute | solution.py:125
  75.7 13.6 %collective-permute-start.8 = (bf16[320,1280]{1,0:T(8,128)(2,1)}, bf16[320,1280]{1,0:T(8,128)(2,1)}, u32[]{:S(2)}, u32[]{:S(2)}) collective-permute-start(bf16[320,1280]{1,0:T(8,128)(2,1)} %collective-permute-done.5.refs_8_), channel_id=1, source_target_pairs={{0,1},{1,0},{2,3},{3,2},{4,5},{5,4},{6,7},{7,6},{8,9},{9,8},{10,11... | collective-permute-start | bytes 2457608 | tf_op jit(solution)/shard_map/ppermute | solution.py:125
  81.3 1.0 copy-start.2
  82.3 1.0 copy-start.4
  83.3 1.0 copy-start.6
  88.1 1.3 copy-start.14
  98.8 42.7 %collective-permute-start.19 = (bf16[4,160,256]{2,1,0:T(8,128)(2,1)S(1)}, bf16[4,160,256]{2,1,0:T(8,128)(2,1)S(1)}, u32[]{:S(2)}, u32[]{:S(2)}) collective-permute-start(bf16[4,160,256]{2,1,0:T(8,128)(2,1)S(1)} %get-tuple-element.36), channel_id=1, source_target_pairs={{0,4},{4,0},{8,12},{12,8},{16,20},{20,16},{24,28},{28,24},{1,5},{5... | collective-permute-start | bytes 983048 | tf_op jit(solution)/shard_map/ppermute | solution.py:128
  108.7 35.0 %collective-permute-start.23 = (bf16[4,160,256]{2,1,0:T(8,128)(2,1)S(1)}, bf16[4,160,256]{2,1,0:T(8,128)(2,1)S(1)}, u32[]{:S(2)}, u32[]{:S(2)}) collective-permute-start(bf16[4,160,256]{2,1,0:T(8,128)(2,1)S(1)} %get-tuple-element.42), channel_id=1, source_target_pairs={{0,4},{4,0},{8,12},{12,8},{16,20},{20,16},{24,28},{28,24},{1,5},{5... | collective-permute-start | bytes 983048 | tf_op jit(solution)/shard_map/ppermute | solution.py:128
  119.7 25.9 %collective-permute-start.27 = (bf16[4,160,256]{2,1,0:T(8,128)(2,1)S(1)}, bf16[4,160,256]{2,1,0:T(8,128)(2,1)S(1)}, u32[]{:S(2)}, u32[]{:S(2)}) collective-permute-start(bf16[4,160,256]{2,1,0:T(8,128)(2,1)S(1)} %get-tuple-element.48), channel_id=1, source_target_pairs={{0,4},{4,0},{8,12},{12,8},{16,20},{20,16},{24,28},{28,24},{1,5},{5... | collective-permute-start | bytes 983048 | tf_op jit(solution)/shard_map/ppermute | solution.py:128
  129.7 17.5 %collective-permute-start.32 = (bf16[4,160,256]{2,1,0:T(8,128)(2,1)S(1)}, bf16[4,160,256]{2,1,0:T(8,128)(2,1)S(1)}, u32[]{:S(2)}, u32[]{:S(2)}) collective-permute-start(bf16[4,160,256]{2,1,0:T(8,128)(2,1)S(1)} %get-tuple-element.54), channel_id=1, source_target_pairs={{0,4},{4,0},{8,12},{12,8},{16,20},{20,16},{24,28},{28,24},{1,5},{5... | collective-permute-start | bytes 983048 | tf_op jit(solution)/shard_map/ppermute | solution.py:128
  140.9 9.1 %collective-permute-start.37 = (bf16[4,160,256]{2,1,0:T(8,128)(2,1)S(1)}, bf16[4,160,256]{2,1,0:T(8,128)(2,1)S(1)}, u32[]{:S(2)}, u32[]{:S(2)}) collective-permute-start(bf16[4,160,256]{2,1,0:T(8,128)(2,1)S(1)} %get-tuple-element.60), channel_id=1, source_target_pairs={{0,4},{4,0},{8,12},{12,8},{16,20},{20,16},{24,28},{28,24},{1,5},{5... | collective-permute-start | bytes 983048 | tf_op jit(solution)/shard_map/ppermute | solution.py:128
  142.1 11.7 %collective-permute-start.20 = (bf16[160,256]{1,0:T(8,128)(2,1)S(1)}, bf16[160,256]{1,0:T(8,128)(2,1)S(1)}, u32[]{:S(2)}, u32[]{:S(2)}) collective-permute-start(bf16[160,256]{1,0:T(8,128)(2,1)S(1)} %get-tuple-element.38), channel_id=1, source_target_pairs={{0,8},{4,12},{8,0},{12,4},{16,24},{20,28},{24,16},{28,20},{1,9},{5... | collective-permute-start | bytes 245768 | tf_op jit(solution)/shard_map/ppermute | solution.py:131
  143.8 11.5 %collective-permute-start.21 = (bf16[160,256]{1,0:T(8,128)(2,1)S(1)}, bf16[160,256]{1,0:T(8,128)(2,1)S(1)}, u32[]{:S(2)}, u32[]{:S(2)}) collective-permute-start(bf16[160,256]{1,0:T(8,128)(2,1)S(1)} %get-tuple-element.39), channel_id=1, source_target_pairs={{0,16},{4,20},{8,24},{12,28},{16,0},{20,4},{24,8},{28,12},{1,17},{... | collective-permute-start | bytes 245768 | tf_op jit(solution)/shard_map/ppermute | solution.py:131
  145.7 9.5 %collective-permute-start.22 = (bf16[160,256]{1,0:T(8,128)(2,1)S(1)}, bf16[160,256]{1,0:T(8,128)(2,1)S(1)}, u32[]{:S(2)}, u32[]{:S(2)}) collective-permute-start(bf16[160,256]{1,0:T(8,128)(2,1)S(1)} %get-tuple-element.40), channel_id=1, source_target_pairs={{0,24},{4,28},{8,16},{12,20},{16,8},{20,12},{24,0},{28,4},{1,25},{... | collective-permute-start | bytes 245768 | tf_op jit(solution)/shard_map/ppermute | solution.py:131
  147.2 11.0 %collective-permute-start.24 = (bf16[160,256]{1,0:T(8,128)(2,1)S(1)}, bf16[160,256]{1,0:T(8,128)(2,1)S(1)}, u32[]{:S(2)}, u32[]{:S(2)}) collective-permute-start(bf16[160,256]{1,0:T(8,128)(2,1)S(1)} %get-tuple-element.44), channel_id=1, source_target_pairs={{0,8},{4,12},{8,0},{12,4},{16,24},{20,28},{24,16},{28,20},{1,9},{5... | collective-permute-start | bytes 245768 | tf_op jit(solution)/shard_map/ppermute | solution.py:131
  150.0 11.0 %collective-permute-start.25 = (bf16[160,256]{1,0:T(8,128)(2,1)S(1)}, bf16[160,256]{1,0:T(8,128)(2,1)S(1)}, u32[]{:S(2)}, u32[]{:S(2)}) collective-permute-start(bf16[160,256]{1,0:T(8,128)(2,1)S(1)} %get-tuple-element.45), channel_id=1, source_target_pairs={{0,16},{4,20},{8,24},{12,28},{16,0},{20,4},{24,8},{28,12},{1,17},{... | collective-permute-start | bytes 245768 | tf_op jit(solution)/shard_map/ppermute | solution.py:131
  153.8 7.8 %collective-permute-start.26 = (bf16[160,256]{1,0:T(8,128)(2,1)S(1)}, bf16[160,256]{1,0:T(8,128)(2,1)S(1)}, u32[]{:S(2)}, u32[]{:S(2)}) collective-permute-start(bf16[160,256]{1,0:T(8,128)(2,1)S(1)} %get-tuple-element.46), channel_id=1, source_target_pairs={{0,24},{4,28},{8,16},{12,20},{16,8},{20,12},{24,0},{28,4},{1,25},{... | collective-permute-start | bytes 245768 | tf_op jit(solution)/shard_map/ppermute | solution.py:131
  155.2 11.7 %collective-permute-start.28 = (bf16[160,256]{1,0:T(8,128)(2,1)S(1)}, bf16[160,256]{1,0:T(8,128)(2,1)S(1)}, u32[]{:S(2)}, u32[]{:S(2)}) collective-permute-start(bf16[160,256]{1,0:T(8,128)(2,1)S(1)} %get-tuple-element.50), channel_id=1, source_target_pairs={{0,8},{4,12},{8,0},{12,4},{16,24},{20,28},{24,16},{28,20},{1,9},{5... | collective-permute-start | bytes 245768 | tf_op jit(solution)/shard_map/ppermute | solution.py:131
  155.2 13.2 %collective-permute-start.29 = (bf16[160,256]{1,0:T(8,128)(2,1)S(1)}, bf16[160,256]{1,0:T(8,128)(2,1)S(1)}, u32[]{:S(2)}, u32[]{:S(2)}) collective-permute-start(bf16[160,256]{1,0:T(8,128)(2,1)S(1)} %get-tuple-element.51), channel_id=1, source_target_pairs={{0,16},{4,20},{8,24},{12,28},{16,0},{20,4},{24,8},{28,12},{1,17},{... | collective-permute-start | bytes 245768 | tf_op jit(solution)/shard_map/ppermute | solution.py:131
  158.3 10.1 %collective-permute-start.30 = (bf16[160,256]{1,0:T(8,128)(2,1)S(1)}, bf16[160,256]{1,0:T(8,128)(2,1)S(1)}, u32[]{:S(2)}, u32[]{:S(2)}) collective-permute-start(bf16[160,256]{1,0:T(8,128)(2,1)S(1)} %get-tuple-element.52), channel_id=1, source_target_pairs={{0,24},{4,28},{8,16},{12,20},{16,8},{20,12},{24,0},{28,4},{1,25},{... | collective-permute-start | bytes 245768 | tf_op jit(solution)/shard_map/ppermute | solution.py:131
  161.0 10.4 %collective-permute-start.33 = (bf16[160,256]{1,0:T(8,128)(2,1)S(1)}, bf16[160,256]{1,0:T(8,128)(2,1)S(1)}, u32[]{:S(2)}, u32[]{:S(2)}) collective-permute-start(bf16[160,256]{1,0:T(8,128)(2,1)S(1)} %get-tuple-element.56), channel_id=1, source_target_pairs={{0,8},{4,12},{8,0},{12,4},{16,24},{20,28},{24,16},{28,20},{1,9},{5... | collective-permute-start | bytes 245768 | tf_op jit(solution)/shard_map/ppermute | solution.py:131
  161.6 14.1 %collective-permute-start.34 = (bf16[160,256]{1,0:T(8,128)(2,1)S(1)}, bf16[160,256]{1,0:T(8,128)(2,1)S(1)}, u32[]{:S(2)}, u32[]{:S(2)}) collective-permute-start(bf16[160,256]{1,0:T(8,128)(2,1)S(1)} %get-tuple-element.57), channel_id=1, source_target_pairs={{0,16},{4,20},{8,24},{12,28},{16,0},{20,4},{24,8},{28,12},{1,17},{... | collective-permute-start | bytes 245768 | tf_op jit(solution)/shard_map/ppermute | solution.py:131
  167.0 8.7 %collective-permute-start.35 = (bf16[160,256]{1,0:T(8,128)(2,1)S(1)}, bf16[160,256]{1,0:T(8,128)(2,1)S(1)}, u32[]{:S(2)}, u32[]{:S(2)}) collective-permute-start(bf16[160,256]{1,0:T(8,128)(2,1)S(1)} %get-tuple-element.58), channel_id=1, source_target_pairs={{0,24},{4,28},{8,16},{12,20},{16,8},{20,12},{24,0},{28,4},{1,25},{... | collective-permute-start | bytes 245768 | tf_op jit(solution)/shard_map/ppermute | solution.py:131
  168.4 7.9 %collective-permute-start.38 = (bf16[160,256]{1,0:T(8,128)(2,1)S(1)}, bf16[160,256]{1,0:T(8,128)(2,1)S(1)}, u32[]{:S(2)}, u32[]{:S(2)}) collective-permute-start(bf16[160,256]{1,0:T(8,128)(2,1)S(1)} %get-tuple-element.62), channel_id=1, source_target_pairs={{0,8},{4,12},{8,0},{12,4},{16,24},{20,28},{24,16},{28,20},{1,9},{5... | collective-permute-start | bytes 245768 | tf_op jit(solution)/shard_map/ppermute | solution.py:131
  168.4 12.2 %collective-permute-start.39 = (bf16[160,256]{1,0:T(8,128)(2,1)S(1)}, bf16[160,256]{1,0:T(8,128)(2,1)S(1)}, u32[]{:S(2)}, u32[]{:S(2)}) collective-permute-start(bf16[160,256]{1,0:T(8,128)(2,1)S(1)} %get-tuple-element.63), channel_id=1, source_target_pairs={{0,16},{4,20},{8,24},{12,28},{16,0},{20,4},{24,8},{28,12},{1,17},{... | collective-permute-start | bytes 245768 | tf_op jit(solution)/shard_map/ppermute | solution.py:131
  171.4 9.2 %collective-permute-start.40 = (bf16[160,256]{1,0:T(8,128)(2,1)S(1)}, bf16[160,256]{1,0:T(8,128)(2,1)S(1)}, u32[]{:S(2)}, u32[]{:S(2)}) collective-permute-start(bf16[160,256]{1,0:T(8,128)(2,1)S(1)} %get-tuple-element.64), channel_id=1, source_target_pairs={{0,24},{4,28},{8,16},{12,20},{16,8},{20,12},{24,0},{28,4},{1,25},{... | collective-permute-start | bytes 245768 | tf_op jit(solution)/shard_map/ppermute | solution.py:131
  181.4 1.9 collective-permute-start.31
  181.5 8.8 %collective-permute-start.36 = (f32[160,320]{1,0:T(8,128)S(1)}, f32[160,320]{1,0:T(8,128)S(1)}, u32[]{:S(2)}, u32[]{:S(2)}) collective-permute-start(f32[160,320]{1,0:T(8,128)S(1)} %get-tuple-element.75), channel_id=1, source_target_pairs={{0,2},{1,3},{2,0},{3,1},{4,6},{5,7},{6,4},{7,5},{8,10},{9,11},{10,... | collective-permute-start | bytes 614408 | tf_op jit(solution)/shard_map/ppermute | solution.py:125
  182.9 11.8 %collective-permute-start.41 = (f32[160,320]{1,0:T(8,128)S(1)}, f32[160,320]{1,0:T(8,128)S(1)}, u32[]{:S(2)}, u32[]{:S(2)}) collective-permute-start(f32[160,320]{1,0:T(8,128)S(1)} %get-tuple-element.74), channel_id=1, source_target_pairs={{0,3},{1,2},{2,1},{3,0},{4,7},{5,6},{6,5},{7,4},{8,11},{9,10},{10,... | collective-permute-start | bytes 614408 | tf_op jit(solution)/shard_map/ppermute | solution.py:125
  (10 other events, 8.5 us)

commit v2 on v0

v2 whole, which is shorter than its diff:
```python
import functools

import jax
import jax.numpy as jnp
from jax import lax
from jax.experimental import pallas as pl
from jax.experimental.pallas import tpu as pltpu
from jax.sharding import PartitionSpec as P

TILE = 64
BF = jnp.bfloat16
F32 = jnp.float32
VMEM = pl.BlockSpec(memory_space=pltpu.VMEM)
SMEM = pl.BlockSpec(memory_space=pltpu.SMEM)
HBM = pl.BlockSpec(memory_space=pltpu.HBM)
LIMIT = 10 * 2**20
COL, LOW, HIGH, ROW = range(4)


def kernel_call(body, outs, ins, scratch=(), name=None, out_spec=VMEM, aliases=None):
    return pl.pallas_call(
        body,
        out_shape=outs,
        in_specs=[SMEM] + [VMEM] * (len(ins) - 1),
        out_specs=jax.tree.map(lambda _: out_spec, outs),
        scratch_shapes=scratch,
        compiler_params=pltpu.CompilerParams(vmem_limit_bytes=LIMIT),
        cost_estimate=pl.CostEstimate(flops=0, bytes_accessed=0, transcendentals=0),
        input_output_aliases=aliases or {},
        name=name,
    )(*ins)


def like(shape, dtype):
    return jax.ShapeDtypeStruct(shape, dtype)


class Box:
    def __init__(self, value):
        self.value = value


def tie(*boxes):
    values = lax.optimization_barrier(tuple(box.value for box in boxes))
    for box, value in zip(boxes, values, strict=True):
        box.value = value


def iota(shape, dim):
    return lax.broadcasted_iota(jnp.int32, shape, dim)


def spread(row_tiles, tiles, size):
    count = tiles.shape[0]
    picker = (row_tiles == iota((row_tiles.shape[0], count), 1)).astype(F32).astype(BF)
    wide = (iota((count, size), 1) // TILE == iota((count, size), 0)).astype(F32).astype(BF)
    rows = jnp.dot(picker, tiles.astype(F32).astype(BF), preferred_element_type=F32).astype(BF)
    return jnp.dot(rows, wide, preferred_element_type=F32).astype(BF)


def mask_slab(n_col, ks, ids, tiles, *refs):
    pieces, out = refs[:-1], refs[-1]
    rows, size = pieces[0].shape
    for k, piece in zip(ks, pieces, strict=True):
        owner = ids[COL] ^ k
        row_tiles = ((ids[ROW] * n_col + owner) * rows + iota((rows, 1), 0)) // TILE
        out[owner % 2] = piece[...] * spread(row_tiles, tiles[...], size)


def place_blocks(places, ids, *refs):
    blocks, out = refs[:-1], refs[-1]
    for place, block in zip(places(ids), blocks, strict=True):
        out[place] = block[...]


def masked_block(ids, tiles, piece, group, half, groups, block, size):
    first = ((piece * groups + group) * 2 + half) * block
    return spread((first + iota((block, 1), 0)) // TILE, tiles[...], size)


def place_pieces(ks, ids, tiles, *refs):
    pieces, (other, kept) = refs[: len(ks)], refs[len(ks) :]
    for k, piece in zip(ks, pieces, strict=True):
        aux, groups, _, block, size = piece.shape
        owner = ids[COL] ^ k
        for half, out in ((1 - ids[LOW], other), (ids[LOW], kept)):
            for g in range(groups):
                mask = masked_block(ids, tiles, owner, g, half, groups, block, size)
                for q in range(aux):
                    out[q, owner * groups + g] = piece[q, g, half] * mask


def place_halves(ks, other_half, ids, tiles, *refs):
    pieces, out = refs[: len(ks)], refs[-1]
    half = 1 - ids[LOW] if other_half else ids[LOW]
    for k, piece in zip(ks, pieces, strict=True):
        aux, groups, block, size = piece.shape
        owner = ids[COL] ^ k
        for g in range(groups):
            mask = masked_block(ids, tiles, owner, g, half, groups, block, size)
            for q in range(aux):
                out[q, owner * groups + g] = piece[q, g] * mask


def multiply_rows(factors, inter, carried, first, width):
    value = jnp.dot(carried[...], first[...], preferred_element_type=F32)
    for q in range(factors.shape[0]):
        value += lax.dot_general(
            factors[q],
            inter[pl.ds(q * width, width), :],
            (((1,), (1,)), ((), ())),
            preferred_element_type=F32,
        )
    return value


def runs(segments, block):
    found, to = [], 0
    for piece, start, count in segments:
        end = start + count
        while start < end:
            group, half, at = start // (2 * block), start // block % 2, start % block
            n = min(block - at, end - start)
            found.append((piece, group, half, at, n, to))
            start, to = start + n, to + n
    return found


def pick_rows(segments, width, ids, other, kept, picked):
    aux, n_high, block, _ = other.shape
    groups = max(1, n_high // 4)
    for low in range(2):

        @pl.when(ids[LOW] == low)
        def _():
            for piece, group, half, at, n, to in runs(segments, block):
                source = kept if half == low else other
                for q in range(aux):
                    picked[q * width + to : q * width + to + n, :] = source[
                        q, (ids[COL] ^ piece) * groups + group, at : at + n, :
                    ]


def times_amplitudes(picked, amp, inter, more=None):
    size = amp.shape[1]
    step = 256 if size % 256 == 0 else size
    rows = inter.shape[0]
    for i in range(size // step):
        at = slice(i * step, (i + 1) * step)
        value = jnp.dot(picked[...], amp[:, at], preferred_element_type=F32)
        inter[:, at] = value[:rows].astype(BF)
        if more is not None:
            more[:, at] = value[rows:]


def first_send_part(segments, width, ids, *refs):
    others, kepts, amp, factors, second, first, inter, send, other, kept, picked, rows, turned = refs
    aux = factors.shape[0]
    block = send.shape[1]
    pick_rows(segments, width, ids, others, kepts, picked)
    picked[aux * width :, :] = second[...]
    times_amplitudes(picked, amp, inter, rows)
    u = rows[...]
    high = u.astype(BF).astype(F32)
    turned[...] = jnp.concatenate([high[:aux], (u - high)[:aux]], axis=0).T
    for h in range(send.shape[0]):
        for half, out in ((1 - ids[LOW], other), (ids[LOW], kept)):
            at = pl.ds(pl.multiple_of((2 * h + half) * block, 8), block)
            out[h * block : (h + 1) * block, :] = turned[at, :].astype(BF)
    value = multiply_rows(factors, inter, other, first, width)
    for h in range(send.shape[0]):
        send[h] = value[h * block : (h + 1) * block, :].astype(BF)


def send_part(segments, width, ids, *refs):
    others, kepts, amp, factors, carried, first, inter, send, picked = refs
    block = send.shape[1]
    pick_rows(segments, width, ids, others, kepts, picked)
    times_amplitudes(picked, amp, inter)
    value = multiply_rows(factors, inter, carried, first, width)
    for h in range(send.shape[0]):
        send[h] = value[h * block : (h + 1) * block, :].astype(BF)


def keep_rows(count, width, ids, factors, carried, *refs):
    inter, first, got = refs[:count], refs[count : 2 * count], refs[2 * count : 3 * count]
    total = refs[-1]
    block = got[0].shape[1]
    for c in range(count):
        value = multiply_rows(factors, inter[c], carried, first[c], width)
        for h in range(got[c].shape[0]):
            total[h, :, c * width : (c + 1) * width] = (
                value[h * block : (h + 1) * block, :] + got[c][h].astype(F32)
            )
    return refs[3 * count : -1], total


def keep_direct(count, width, ids, *refs):
    (own, *messages), total = keep_rows(count, width, ids, *refs)
    own[...] = total[ids[HIGH]]
    for k, message in enumerate(messages, 1):
        message[...] = total[ids[HIGH] ^ k].astype(BF)


def keep_halves(count, width, ids, *refs):
    (mine, message), total = keep_rows(count, width, ids, *refs)
    for i in range(mine.shape[0]):
        mine[i] = total[ids[HIGH] ^ (2 * i)]
        message[i] = total[ids[HIGH] ^ (2 * i + 1)].astype(BF)


def add_halves(ids, mine, got, kept, message):
    for i in range(kept.shape[0]):
        kept[i] = mine[2 * i] + got[2 * i].astype(F32)
        message[i] = (mine[2 * i + 1] + got[2 * i + 1].astype(F32)).astype(BF)


def add_up(ids, own, *refs):
    value = own[...]
    for got in refs[:-1]:
        value += got[...].astype(F32)
    refs[-1][...] = value


def finish(places, ids, *refs):
    parts, out, whole, sems = refs[:-3], refs[-3], refs[-2], refs[-1]
    copies = []
    for k in range(whole.shape[0]):
        for (piece, start, count), part in zip(places, parts, strict=True):
            if piece == k:
                whole[k, :, start : start + count] = part[...]
        copy = pltpu.make_async_copy(whole.at[k], out.at[ids[COL] ^ k], sems.at[k])
        copy.start()
        copies.append(copy)
    for copy in copies:
        copy.wait()


def local(n_row, n_col, amplitudes, integrals, occupied, pairs, amp_tiles, int_tiles):
    n_pair, chunk_rows, size = amplitudes.shape
    aux, piece_rows, _ = integrals.shape
    n_high = n_row // 2
    block = size // n_row
    groups = piece_rows // (2 * block)
    half_size = n_high * block
    col, row = lax.axis_index("col"), lax.axis_index("row")
    ids = jnp.stack([col, row % 2, row // 2, row]).astype(jnp.int32)

    def over_col(x, k):
        return lax.ppermute(x, "col", [(i, i ^ k) for i in range(n_col)])

    def over_low(x):
        return lax.ppermute(x, "row", [(i, i ^ 1) for i in range(n_row)])

    def over_high(x, k):
        return lax.ppermute(x, "row", [(i, (i // 2 ^ k) * 2 + i % 2) for i in range(n_row)])

    def up(x):
        return lax.ppermute(x, "row", [(i, (i + 2) % n_row) for i in range(n_row)])

    mine = [lax.dynamic_index_in_dim(amplitudes, col ^ k, 0, keepdims=False) for k in range(n_col)]
    mine = [Box(mine[0])] + [Box(over_col(mine[k], k)) for k in range(1, n_col)]
    split = integrals.reshape(aux, groups, 2, block, size)
    low = row % 2
    other, kept = {}, {}
    send_other = Box(lax.dynamic_index_in_dim(split, 1 - low, 2, keepdims=False))
    send_kept = Box(lax.dynamic_index_in_dim(split, low, 2, keepdims=False))
    split1 = Box(over_col(integrals, 1))
    tie(send_other, send_kept, split1, *mine[1:])
    other[2] = Box(over_col(send_other.value, 2))
    pair_tiles = lax.dynamic_index_in_dim(amp_tiles, col, 0, keepdims=False)

    def half_slab(ks):
        return kernel_call(
            functools.partial(mask_slab, n_col, ks),
            like((2, chunk_rows, size), BF),
            (ids, pair_tiles, *[mine[k].value for k in ks]),
            name="half_slab",
        ).reshape(2 * chunk_rows, size)

    rings = [[Box(half_slab((0, 1)))], [Box(half_slab((2, 3)))]]
    swapped = [[], []]
    for s in range(n_high):
        for r, ring in enumerate(rings):
            if s > 0:
                tie(ring[s], swapped[r][-1])
            if s + 1 < n_high:
                ring.append(Box(up(ring[s].value)))
            swapped[r].append(Box(over_low(ring[s].value)))
    tie(other[2], rings[0][-1], rings[1][-2], swapped[0][-3], swapped[1][-3])
    tie(send_kept, other[2])
    other[3] = Box(over_col(other[2].value, 1))
    kept[2] = Box(over_col(send_kept.value, 2))

    def slab_places(ids):
        highs = [lax.rem(ids[HIGH] + (n_high - s), n_high) for s in range(n_high)]
        side = ids[COL] // 2
        return [
            ((h * 2 + low) * 2) + (side ^ r)
            for low in (ids[LOW], 1 - ids[LOW])
            for r in range(2)
            for h in highs
        ]

    slabs = rings[0] + rings[1] + swapped[0] + swapped[1]
    amp = kernel_call(
        functools.partial(place_blocks, slab_places),
        like((n_row * 2, 2 * chunk_rows, size), BF),
        (ids, *[slab.value for slab in slabs]),
        name="all_rows",
    )
    amp = Box(amp.reshape(size, size))

    shape = like((aux, n_high, block, size), BF)
    all_other, all_kept = kernel_call(
        functools.partial(place_pieces, (0, 1)),
        (shape, shape),
        (ids, int_tiles, split, split1.value.reshape(split.shape)),
        name="place_pieces",
    )

    def place(pieces, into, other_half):
        return kernel_call(
            functools.partial(place_halves, (2, 3), other_half),
            shape,
            (ids, int_tiles, pieces[2].value, pieces[3].value, into),
            aliases={4: 0},
            name="place_halves",
        )

    def flat(x):
        return x.reshape(aux, half_size, size)

    all_other = place(other, all_other, True)
    all_kept = Box(all_kept)

    orbitals = jnp.arange(occupied.shape[1], dtype=jnp.int32)
    picks = (pairs.T.reshape(-1)[:, None] == orbitals[None, :]).astype(BF)
    rows = jnp.einsum("po,qov->pqv", picks, occupied, preferred_element_type=F32).astype(BF)
    first = lax.dynamic_index_in_dim(rows, col, 0, keepdims=False)
    second = lax.dynamic_index_in_dim(rows, col + n_pair, 0, keepdims=False)
    second = jnp.concatenate([second, jnp.zeros((16 - aux, size), BF)], axis=0)
    first = first.reshape(aux, n_col, piece_rows)
    first = [lax.dynamic_index_in_dim(first, col ^ k, 1, keepdims=False) for k in range(n_col)]
    first = [jnp.concatenate([x, x], axis=0) for x in first]

    width = 256 if size % 256 == 0 else piece_rows
    cut = 2 * width - piece_rows
    rest = piece_rows - cut
    order = [(1, 0, piece_rows), (0, 0, cut), (2, 0, piece_rows), (3, 0, cut), (3, cut, rest), (0, cut, rest)]
    chunks, where, at = [], [], 0
    for piece, start, count in order:
        spans = []
        while count:
            if at % width == 0:
                chunks.append([])
            n = min(count, width - at % width)
            chunks[-1].append((piece, start, n))
            spans.append((at // width, at % width, n))
            start, count, at = start + n, count - n, at + n
        where.append(spans)
    first = [jnp.concatenate([first[p][:, s : s + n] for p, s, n in chunk], axis=1) for chunk in chunks]

    inter, got, sums, carried = {}, {}, {}, []

    def send_chunk(c):
        pieces = (all_other, all_kept.value)
        outs = (like((aux * width, size), BF), like((n_high, block, width), BF))
        if not carried:
            extra = second.shape[0]
            x, send, *terms = kernel_call(
                functools.partial(first_send_part, chunks[c], width),
                outs + (like((half_size, 2 * aux), BF),) * 2,
                (ids, *pieces, amp.value, flat(all_other), second, first[c]),
                scratch=[
                    pltpu.VMEM((aux * width + extra, size), BF),
                    pltpu.VMEM((extra, size), F32),
                    pltpu.VMEM((size, 2 * aux), F32),
                ],
                name="send_part",
            )
            carried.extend(terms)
        else:
            x, send = kernel_call(
                functools.partial(send_part, chunks[c], width),
                outs,
                (ids, *pieces, amp.value, flat(all_other), carried[0], first[c]),
                scratch=[pltpu.VMEM((aux * width, size), BF)],
                name="send_part",
            )
        inter[c] = Box(x)
        got[c] = Box(over_low(send))

    def keep_chunks(cs, direct=False):
        n = len(cs)
        wide = n * width
        half = n_high // 2
        if direct:
            body, outs = keep_direct, (like((block, wide), F32),) + (like((block, wide), BF),) * (n_high - 1)
        else:
            body, outs = keep_halves, (like((half, block, wide), F32), like((half, block, wide), BF))
        own, *messages = kernel_call(
            functools.partial(body, n, width),
            outs,
            (ids, flat(all_kept.value), carried[1])
            + tuple(inter[c].value for c in cs)
            + tuple(first[c] for c in cs)
            + tuple(got[c].value for c in cs),
            scratch=[pltpu.VMEM((n_high, block, wide), F32)],
            name="keep_part",
        )
        if direct:
            messages = [Box(over_high(m, k)) for k, m in enumerate(messages, 1)]
        else:
            messages = [Box(over_high(messages[0], 1))]
        return Box(own), messages

    def add_stages(own, messages):
        step = 2
        while own.value.shape[0] > 1:
            half = own.value.shape[0] // 2
            shape = (half,) + own.value.shape[1:]
            mine, message = kernel_call(
                add_halves, (like(shape, F32), like(shape, BF)), (ids, own.value, messages[0].value), name="add_halves"
            )
            own, messages = Box(mine), [Box(over_high(message, step))]
            step *= 2
        return own, messages

    def sum_chunks(cs, own, messages):
        shape = (block, len(cs) * width)
        total = kernel_call(
            add_up,
            like(shape, F32),
            (ids, own.value.reshape(shape), *[m.value.reshape(shape) for m in messages]),
            name="add_up",
        )
        for i, c in enumerate(cs):
            sums[c] = total[:, i * width : (i + 1) * width]
        return Box(total)

    send_chunk(0)
    tie(amp, inter[0])
    send_chunk(1)
    tie(amp, inter[1], kept[2], all_kept)
    kept[3] = Box(over_col(kept[2].value, 1))
    all_kept = Box(place(kept, all_kept.value, False))
    tie(amp, all_kept)
    send_chunk(2)
    stage01 = keep_chunks((0, 1))
    tie(amp, stage01[0])
    send_chunk(3)
    tie(amp, inter[3], got[2])
    send_chunk(4)
    tie(inter[4], stage01[1][0], all_kept)
    stage01 = add_stages(*stage01)
    tie(stage01[0], all_kept)
    stage2 = keep_chunks((2,))
    tie(stage2[0], all_kept)
    stage3 = keep_chunks((3,))
    tie(stage3[0], stage2[1][0])
    stage2 = add_stages(*stage2)
    tie(stage2[0], stage01[1][0])
    total = sum_chunks((0, 1), *stage01)
    tie(stage2[0], all_kept)
    stage4 = keep_chunks((4,), direct=True)
    tie(stage4[0], stage3[1][0])
    stage3 = add_stages(*stage3)
    sum_chunks((2,), *stage2)
    sum_chunks((3,), *stage3)
    sum_chunks((4,), *stage4)
    parts = []
    for (piece, _, _), spans in zip(order, where, strict=True):
        part = jnp.concatenate([sums[c][:, s : s + n] for c, s, n in spans], axis=1)
        parts.append(over_col(part, piece) if piece else part)
    out = kernel_call(
        functools.partial(finish, order),
        like((n_pair, block, piece_rows), F32),
        (ids, *parts),
        scratch=[pltpu.VMEM((n_pair, block, piece_rows), F32), pltpu.SemaphoreType.DMA((n_pair,))],
        name="finish",
        out_spec=HBM,
    )
    return out.transpose(0, 2, 1)


def solution(mesh):
    placed = (
        P(None, ("row", "col"), None),
        P("row", "col", None),
        P("row", None, None),
        P(),
        P(),
        P(),
    )
    return jax.shard_map(
        functools.partial(local, mesh.shape["row"], mesh.shape["col"]),
        mesh=mesh,
        in_specs=placed,
        out_specs=P(None, "col", "row"),
        check_vma=False,
    )
```

time: 362 us -> 155 us (0.43)
  waiting for transfers between devices: 255 us -> 35 us
  Pallas kernels: 0 us -> 59.3 us
  matrix products: 52.6 us -> 0.32 us
  starting transfers between devices: 0.09 us -> 45.7 us
  local copies, waits for them, and re-layouts: 29.2 us -> 12.4 us
  between operations: 13.2 us -> 0.67 us
  other arithmetic: 10.5 us -> 0.36 us
    reduce_scatter x1 -> x0, waiting for transfers between devices: 140 us -> none  [local(): lax.psum_scatter(ladder + cycle, 'row', scatter_dimension=2, tiled=True)]
    all_gather x2 -> x0, waiting for transfers between devices: 115 us -> none  [the longest x1 96.5 us: local(): whole_amp = lax.all_gather(amplitudes, ('row', 'col'), axis=1, tiled=True)]
    pallas_call x0 -> x23, Pallas kernels: none -> 59.3 us  [kernel_call(): pl.pallas_call(body, out_shape=outs, in_specs=[SMEM] + [VMEM] * (len(ins)...]
    dot_general x6 -> x1, matrix products: 52.6 us -> 0.32 us  [local(): jnp.einsum('po,qov->pqv', picks, occupied, preferred_element_type=F32)]
    ppermute x0 -> x40, starting transfers between devices: none -> 45.7 us  [the longest x13 16 us: over_low(): return lax.ppermute(x, 'row', [(i, i ^ 1) for i in range(n_row)])]
    ppermute x0 -> x40, waiting for transfers between devices: none -> 35 us  [the longest x6 10.4 us: up(): return lax.ppermute(x, 'row', [(i, (i + 2) % n_row) for i in range(n_row)])]
    all_gather x1 -> x0, local copies, waits for them, and re-layouts: 21.4 us -> none  [local(): whole_amp = lax.all_gather(amplitudes, ('row', 'col'), axis=1, tiled=True)]
    mul x2 -> x0, other arithmetic: 9.81 us -> none  [the longest x1 6.37 us: mask_rows(): return amp_rows * row_mask.astype(amp_rows.dtype)]
  transfers between devices with their start and end apart: 3 -> 40, of which waited for: 3 -> 17; matrix products, arithmetic and copies ran while one was open for 14% -> 4% of each run, Pallas kernels for 0% -> 38%
where the time goes in v2:
time: 155 us; the launch traced here: 154 us
  Pallas kernels  59.3 us (38%)
  starting transfers between devices  45.7 us (29%)
  waiting for transfers between devices  35 us (23%)
  local copies, waits for them, and re-layouts  12.4 us (8%)
    pallas_call x23, Pallas kernels, kernel_call(): pl.pallas_call(body, out_shape=outs, in_specs=[SMEM] + [VMEM] * (len(ins)...  59.3 us
    ppermute x13, starting transfers between devices, over_low(): return lax.ppermute(x, 'row', [(i, i ^ 1) for i in range(n_row)])  16 us
    ppermute x9, starting transfers between devices, over_high(): lax.ppermute(x, 'row', [(i, (i // 2 ^ k) * 2 + i % 2) for i in range(n_ro...  14.1 us
    ppermute x6, waiting for transfers between devices, up(): return lax.ppermute(x, 'row', [(i, (i + 2) % n_row) for i in range(n_row)])  10.4 us
    ppermute x13, waiting for transfers between devices, over_low(): return lax.ppermute(x, 'row', [(i, i ^ 1) for i in range(n_row)])  9.69 us
    ppermute x6, starting transfers between devices, up(): return lax.ppermute(x, 'row', [(i, (i + 2) % n_row) for i in range(n_row)])  8.12 us
    ppermute x12, waiting for transfers between devices, over_col(): return lax.ppermute(x, 'col', [(i, i ^ k) for i in range(n_col)])  7.52 us
    ppermute x12, starting transfers between devices, over_col(): return lax.ppermute(x, 'col', [(i, i ^ k) for i in range(n_col)])  7.49 us
  transfers between devices with their start and end apart: 40, of which 17 were waited for; matrix products, arithmetic and copies ran while one was open for 4% of the time, Pallas kernels for 38%

profile of v2, /device:TPU:0, one launch (start us, length us, event | category | flops | bytes accessed | tf_op | source)
XLA Modules:
  0.0 153.7 jit_solution(16295631182326481624)
XLA Ops:
  0.5 1.1 dynamic-slice_bitcast_fusion.2
  1.7 2.9 %collective-permute-start.2 = (bf16[40,1280]{1,0:T(8,128)(2,1)S(1)}, bf16[40,1280]{1,0:T(8,128)(2,1)S(1)}, u32[]{:S(2)}, u32[]{:S(2)}) collective-permute-start(bf16[40,1280]{1,0:T(8,128)(2,1)S(1)} %get-tuple-element.176), channel_id=1, source_target_pairs={{0,2},{1,3},{2,0},{3,1},{4,6},{5,7},{6,4},{7,5},{8,10},{9,11},{10,... | collective-permute-start | bytes 307208 | tf_op jit(solution)/shard_map/ppermute | solution.py:250
  4.6 3.3 %dynamic-slice_bitcast_fusion = (bf16[3,1,160,1280]{3,2,1,0:T(8,128)(2,1)}, bf16[3,1,160,1280]{3,2,1,0:T(8,128)(2,1)}) fusion(bf16[3,1,2,160,1280]{4,3,2,1,0:T(8,128)(2,1)} %bitcast.68, s32[]{:T(128)S(6)} %select_n.51, s32[]{:T(128)S(6)} %select_n.50), kind=kLoop, calls=%fused_computation.1 | loop fusion | bytes 4915208 | tf_op jit(solution)/shard_map/jit(dynamic_index_in_dim)/squeeze | solution.py:267
  7.9 1.9 %collective-permute-done.3.refs_1_ = bf16[40,1280]{1,0:T(8,128)(2,1)S(1)} collective-permute-done((bf16[40,1280]{1,0:T(8,128)(2,1)S(1)}, bf16[40,1280]{1,0:T(8,128)(2,1)S(1)}, u32[]{:S(2)}, u32[]{:S(2)}) %collective-permute-start.3) | collective-permute-done | bytes 102432 | tf_op jit(solution)/shard_map/ppermute | solution.py:250
  9.8 1.0 collective-permute-start.8
  12.8 1.6 %collective-permute-start.4 = (bf16[80,1280]{1,0:T(8,128)(2,1)S(1)}, bf16[80,1280]{1,0:T(8,128)(2,1)S(1)}, u32[]{:S(2)}, u32[]{:S(2)}) collective-permute-start(bf16[80,1280]{1,0:T(8,128)(2,1)S(1)} %bitcast.70), channel_id=1, source_target_pairs={{0,8},{4,12},{8,16},{12,20},{16,24},{20,28},{24,0},{28,4},{1,9},{5... | collective-permute-start | bytes 614408 | tf_op jit(solution)/shard_map/ppermute | solution.py:259
  14.4 1.5 collective-permute-start.5
  17.8 1.6 %collective-permute-start.11 = (bf16[80,1280]{1,0:T(8,128)(2,1)S(1)}, bf16[80,1280]{1,0:T(8,128)(2,1)S(1)}, u32[]{:S(2)}, u32[]{:S(2)}) collective-permute-start(bf16[80,1280]{1,0:T(8,128)(2,1)S(1)} %bitcast.73), channel_id=1, source_target_pairs={{0,8},{4,12},{8,16},{12,20},{16,24},{20,28},{24,0},{28,4},{1,9},{5... | collective-permute-start | bytes 614408 | tf_op jit(solution)/shard_map/ppermute | solution.py:259
  19.9 2.1 %collective-permute-done.4.refs_1_ = bf16[80,1280]{1,0:T(8,128)(2,1)S(1)} collective-permute-done((bf16[80,1280]{1,0:T(8,128)(2,1)S(1)}, bf16[80,1280]{1,0:T(8,128)(2,1)S(1)}, u32[]{:S(2)}, u32[]{:S(2)}) %collective-permute-start.4) | collective-permute-done | bytes 204832 | tf_op jit(solution)/shard_map/ppermute | solution.py:259
  23.0 2.4 %collective-permute-start.7 = (bf16[80,1280]{1,0:T(8,128)(2,1)S(1)}, bf16[80,1280]{1,0:T(8,128)(2,1)S(1)}, u32[]{:S(2)}, u32[]{:S(2)}) collective-permute-start(bf16[80,1280]{1,0:T(8,128)(2,1)S(1)} %collective-permute-done.4.refs_1_), channel_id=1, source_target_pairs={{0,4},{4,0},{8,12},{12,8},{16,20},{20,16},{24,28},{28,24},{1,5},{5... | collective-permute-start | bytes 614408 | tf_op jit(solution)/shard_map/ppermute | solution.py:253
  25.4 1.3 collective-permute-done.11.refs_5_
  27.9 1.6 %collective-permute-start.13 = (bf16[80,1280]{1,0:T(8,128)(2,1)S(1)}, bf16[80,1280]{1,0:T(8,128)(2,1)S(1)}, u32[]{:S(2)}, u32[]{:S(2)}) collective-permute-start(bf16[80,1280]{1,0:T(8,128)(2,1)S(1)} %collective-permute-done.11.refs_5_), channel_id=1, source_target_pairs={{0,8},{4,12},{8,16},{12,20},{16,24},{20,28},{24,0},{28,4},{1,9},{5... | collective-permute-start | bytes 614408 | tf_op jit(solution)/shard_map/ppermute | solution.py:259
  29.5 1.0 collective-permute-start.14
  31.8 1.2 collective-permute-start.10
  33.0 1.5 collective-permute-start.9
  35.5 1.8 %collective-permute-done.14.refs_13_ = bf16[80,1280]{1,0:T(8,128)(2,1)S(1)} collective-permute-done((bf16[80,1280]{1,0:T(8,128)(2,1)S(1)}, bf16[80,1280]{1,0:T(8,128)(2,1)S(1)}, u32[]{:S(2)}, u32[]{:S(2)}) %collective-permute-start.14) | collective-permute-done | bytes 204832 | tf_op jit(solution)/shard_map/ppermute | solution.py:253
  38.0 1.7 %collective-permute-done.10.refs_10_ = bf16[80,1280]{1,0:T(8,128)(2,1)S(1)} collective-permute-done((bf16[80,1280]{1,0:T(8,128)(2,1)S(1)}, bf16[80,1280]{1,0:T(8,128)(2,1)S(1)}, u32[]{:S(2)}, u32[]{:S(2)}) %collective-permute-start.10) | collective-permute-done | bytes 204832 | tf_op jit(solution)/shard_map/ppermute | solution.py:253
  43.3 1.4 collective-permute-start.16
  45.3 5.8 %collective-permute-done.15.refs_7_ = bf16[80,1280]{1,0:T(8,128)(2,1)S(1)} collective-permute-done((bf16[80,1280]{1,0:T(8,128)(2,1)}, bf16[80,1280]{1,0:T(8,128)(2,1)S(1)}, u32[]{:S(2)}, u32[]{:S(2)}) %collective-permute-start.15) | collective-permute-done | bytes 204832 | tf_op jit(solution)/shard_map/ppermute | solution.py:259
  51.5 1.4 collective-permute-start.18
  53.0 1.7 %copy-done.1 = bf16[3,320,1280]{2,1,0:T(8,128)(2,1)S(1)} copy-done((bf16[3,320,1280]{2,1,0:T(8,128)(2,1)S(1)}, bf16[3,320,1280]{2,1,0:T(8,128)(2,1)}, u32[]{:S(2)}) %copy-start.1) | copy-done | bytes 2457624
  54.8 2.9 %place_pieces.1 = (bf16[3,4,160,1280]{3,2,1,0:T(8,128)(2,1)S(1)}, bf16[3,4,160,1280]{3,2,1,0:T(8,128)(2,1)S(1)}) custom-call(s32[4]{0:T(128)S(1)} %pad_add_fusion.ids, s32[20,20]{1,0:T(8,128)S(1)} %copy-done.16, bf16[3,1,2,160,1280]{4,3,2,1,0:T(8,128)(2,1)S(1)} %bitcast.69, bf16[3,1,2,160,1280]{4,3,2,1,0:T(8,128)(2,1)} %bitcast.15.refs_1_), custom_call_target="tpu_custom_call" | custom-call | tf_op jit(solution)/shard_map/place_pieces/pallas_call | solution.py:21
  57.7 1.2 collective-permute-done.18.refs_15_
  59.8 1.9 %place_halves.2.refs_0_ = bf16[3,4,160,1280]{3,2,1,0:T(8,128)(2,1)S(1)} custom-call(s32[4]{0:T(128)S(1)} %pad_add_fusion.ids, s32[20,20]{1,0:T(8,128)S(1)} %copy-done.16, bf16[3,1,160,1280]{3,2,1,0:T(8,128)(2,1)S(1)} %collective-permute-done.8.refs_0_, bf16[3,1,160,1280]{3,2,1,0:T(8,128)(2,1)} %collective-permute-done.19.refs_1_, ...), custom_call_target="tpu_custom_call", output_to_operand_aliasing={{}: (4, {})} | custom-call | tf_op jit(solution)/shard_map/place_halves/pallas_call | solution.py:21
  61.7 6.9 %send_part.5 = (bf16[768,1280]{1,0:T(8,128)(2,1)S(1)}, bf16[4,160,256]{2,1,0:T(8,128)(2,1)S(1)}, bf16[640,6]{1,0:T(8,128)(2,1)S(1)}, bf16[640,6]{1,0:T(8,128)(2,1)S(1)}) custom-call(s32[4]{0:T(128)S(1)} %pad_add_fusion.ids, bf16[3,4,160,1280]{3,2,1,0:T(8,128)(2,1)S(1)} %place_halves.2.refs_0_, ...), custom_call_target="tpu_custom_call" | custom-call | tf_op jit(solution)/shard_map/send_part/pallas_call | solution.py:21
  68.6 6.9 %send_part.6 = (bf16[768,1280]{1,0:T(8,128)(2,1)S(1)}, bf16[4,160,256]{2,1,0:T(8,128)(2,1)S(1)}) custom-call(s32[4]{0:T(128)S(1)} %pad_add_fusion.ids, bf16[3,4,160,1280]{3,2,1,0:T(8,128)(2,1)S(1)} %place_halves.2.refs_0_, bf16[3,4,160,1280]{3,2,1,0:T(8,128)(2,1)S(1)} %get-tuple-element.121.refs_1_.refs_2_, bf16[1280,1280]{1,0:T(8,128)(2,1)S(1)} %bitcast.64, ...), custom_call_target="tpu_custom_call" | custom-call | tf_op jit(solution)/shard_map/send_part/pallas_call | solution.py:21
  75.6 1.6 %collective-permute-start.23 = (bf16[4,160,256]{2,1,0:T(8,128)(2,1)S(1)}, bf16[4,160,256]{2,1,0:T(8,128)(2,1)S(1)}, u32[]{:S(2)}, u32[]{:S(2)}) collective-permute-start(bf16[4,160,256]{2,1,0:T(8,128)(2,1)S(1)} %get-tuple-element.128), channel_id=1, source_target_pairs={{0,4},{4,0},{8,12},{12,8},{16,20},{20,16},{24,28},{28,24},{1,5},{5... | collective-permute-start | bytes 983048 | tf_op jit(solution)/shard_map/ppermute | solution.py:253
  78.7 1.9 %place_halves.3.refs_1_ = bf16[3,4,160,1280]{3,2,1,0:T(8,128)(2,1)S(1)} custom-call(s32[4]{0:T(128)S(1)} %pad_add_fusion.ids, s32[20,20]{1,0:T(8,128)S(1)} %copy-done.16, bf16[3,1,160,1280]{3,2,1,0:T(8,128)(2,1)} %collective-permute-done.20.refs_0_, bf16[3,1,160,1280]{3,2,1,0:T(8,128)(2,1)S(1)} %collective-permute-done.21.refs_1_, ...), custom_call_target="tpu_custom_call", output_to_operand_aliasing={{}: (4, {})} | custom-call | tf_op jit(solution)/shard_map/place_halves/pallas_call | solution.py:21
  80.7 6.8 %send_part.8 = (bf16[768,1280]{1,0:T(8,128)(2,1)S(1)}, bf16[4,160,256]{2,1,0:T(8,128)(2,1)S(1)}) custom-call(s32[4]{0:T(128)S(1)} %pad_add_fusion.ids, bf16[3,4,160,1280]{3,2,1,0:T(8,128)(2,1)S(1)} %place_halves.2.refs_0_, bf16[3,4,160,1280]{3,2,1,0:T(8,128)(2,1)S(1)} %place_halves.3.refs_1_, bf16[1280,1280]{1,0:T(8,128)(2,1)S(1)} %bitcast.65, ...), custom_call_target="tpu_custom_call" | custom-call | tf_op jit(solution)/shard_map/send_part/pallas_call | solution.py:21
  87.4 1.6 %collective-permute-start.24 = (bf16[4,160,256]{2,1,0:T(8,128)(2,1)S(1)}, bf16[4,160,256]{2,1,0:T(8,128)(2,1)S(1)}, u32[]{:S(2)}, u32[]{:S(2)}) collective-permute-start(bf16[4,160,256]{2,1,0:T(8,128)(2,1)S(1)} %get-tuple-element.133), channel_id=1, source_target_pairs={{0,4},{4,0},{8,12},{12,8},{16,20},{20,16},{24,28},{28,24},{1,5},{5... | collective-permute-start | bytes 983048 | tf_op jit(solution)/shard_map/ppermute | solution.py:253
  89.0 4.2 %collective-permute-done.22.refs_6_ = bf16[4,160,256]{2,1,0:T(8,128)(2,1)S(1)} collective-permute-done((bf16[4,160,256]{2,1,0:T(8,128)(2,1)S(1)}, bf16[4,160,256]{2,1,0:T(8,128)(2,1)S(1)}, u32[]{:S(2)}, u32[]{:S(2)}) %collective-permute-start.22) | collective-permute-done | bytes 327712 | tf_op jit(solution)/shard_map/ppermute | solution.py:253
  93.2 3.5 %keep_part.4 = (f32[2,160,512]{2,1,0:T(8,128)S(1)}, bf16[2,160,512]{2,1,0:T(8,128)(2,1)S(1)}) custom-call(s32[4]{0:T(128)S(1)} %pad_add_fusion.ids, bf16[3,640,1280]{2,1,0:T(8,128)(2,1)S(1)} %bitcast.59, bf16[640,6]{1,0:T(8,128)(2,1)S(1)} %get-tuple-element.124.refs_1_, bf16[768,1280]{1,0:T(8,128)(2,1)S(1)} %get-tuple-element.125.refs_2_, ...), custom_call_target="tpu_custom_call" | custom-call | tf_op jit(solution)/shard_map/keep_part/pallas_call | solution.py:21
  96.8 1.7 %collective-permute-start.25 = (bf16[2,160,512]{2,1,0:T(8,128)(2,1)S(1)}, bf16[2,160,512]{2,1,0:T(8,128)(2,1)S(1)}, u32[]{:S(2)}, u32[]{:S(2)}) collective-permute-start(bf16[2,160,512]{2,1,0:T(8,128)(2,1)S(1)} %get-tuple-element.136), channel_id=1, source_target_pairs={{0,8},{4,12},{8,0},{12,4},{16,24},{20,28},{24,16},{28,20},{1,9},{5... | collective-permute-start | bytes 983048 | tf_op jit(solution)/shard_map/ppermute | solution.py:256
  98.4 7.0 %send_part.7 = (bf16[768,1280]{1,0:T(8,128)(2,1)S(1)}, bf16[4,160,256]{2,1,0:T(8,128)(2,1)S(1)}) custom-call(s32[4]{0:T(128)S(1)} %pad_add_fusion.ids, bf16[3,4,160,1280]{3,2,1,0:T(8,128)(2,1)S(1)} %place_halves.2.refs_0_, bf16[3,4,160,1280]{3,2,1,0:T(8,128)(2,1)S(1)} %place_halves.3.refs_1_, bf16[1280,1280]{1,0:T(8,128)(2,1)S(1)} %bitcast.66, ...), custom_call_target="tpu_custom_call" | custom-call | tf_op jit(solution)/shard_map/send_part/pallas_call | solution.py:21
  105.4 1.6 %collective-permute-start.26 = (bf16[4,160,256]{2,1,0:T(8,128)(2,1)S(1)}, bf16[4,160,256]{2,1,0:T(8,128)(2,1)S(1)}, u32[]{:S(2)}, u32[]{:S(2)}) collective-permute-start(bf16[4,160,256]{2,1,0:T(8,128)(2,1)S(1)} %get-tuple-element.148), channel_id=1, source_target_pairs={{0,4},{4,0},{8,12},{12,8},{16,20},{20,16},{24,28},{28,24},{1,5},{5... | collective-permute-start | bytes 983048 | tf_op jit(solution)/shard_map/ppermute | solution.py:253
  107.0 6.8 %send_part.9 = (bf16[768,1280]{1,0:T(8,128)(2,1)S(1)}, bf16[4,160,256]{2,1,0:T(8,128)(2,1)S(1)}) custom-call(s32[4]{0:T(128)S(1)} %pad_add_fusion.ids, bf16[3,4,160,1280]{3,2,1,0:T(8,128)(2,1)S(1)} %place_halves.2.refs_0_, bf16[3,4,160,1280]{3,2,1,0:T(8,128)(2,1)S(1)} %place_halves.3.refs_1_, bf16[1280,1280]{1,0:T(8,128)(2,1)S(1)} %bitcast.67, ...), custom_call_target="tpu_custom_call" | custom-call | tf_op jit(solution)/shard_map/send_part/pallas_call | solution.py:21
  115.0 2.1 %keep_part.5 = (f32[2,160,256]{2,1,0:T(8,128)S(1)}, bf16[2,160,256]{2,1,0:T(8,128)(2,1)S(1)}) custom-call(s32[4]{0:T(128)S(1)} %pad_add_fusion.ids, bf16[3,640,1280]{2,1,0:T(8,128)(2,1)S(1)} %bitcast.60, bf16[640,6]{1,0:T(8,128)(2,1)S(1)} %get-tuple-element.124.refs_1_, bf16[768,1280]{1,0:T(8,128)(2,1)S(1)} %get-tuple-element.142.refs_2_, ...), custom_call_target="tpu_custom_call" | custom-call | tf_op jit(solution)/shard_map/keep_part/pallas_call | solution.py:21
  117.6 2.6 %collective-permute-start.28 = (bf16[1,160,512]{2,1,0:T(8,128)(2,1)S(1)}, bf16[1,160,512]{2,1,0:T(8,128)(2,1)S(1)}, u32[]{:S(2)}, u32[]{:S(2)}) collective-permute-start(bf16[1,160,512]{2,1,0:T(8,128)(2,1)S(1)} %get-tuple-element.153), channel_id=1, source_target_pairs={{0,16},{4,20},{8,24},{12,28},{16,0},{20,4},{24,8},{28,12},{1,17},{... | collective-permute-start | bytes 491528 | tf_op jit(solution)/shard_map/ppermute | solution.py:256
  120.2 2.1 %keep_part.6 = (f32[2,160,256]{2,1,0:T(8,128)S(1)}, bf16[2,160,256]{2,1,0:T(8,128)(2,1)S(1)}) custom-call(s32[4]{0:T(128)S(1)} %pad_add_fusion.ids, bf16[3,640,1280]{2,1,0:T(8,128)(2,1)S(1)} %bitcast.61, bf16[640,6]{1,0:T(8,128)(2,1)S(1)} %get-tuple-element.124.refs_1_, bf16[768,1280]{1,0:T(8,128)(2,1)S(1)} %get-tuple-element.147.refs_2_, ...), custom_call_target="tpu_custom_call" | custom-call | tf_op jit(solution)/shard_map/keep_part/pallas_call | solution.py:21
  123.2 2.9 %collective-permute-done.27.got = bf16[2,160,256]{2,1,0:T(8,128)(2,1)S(1)} collective-permute-done((bf16[2,160,256]{2,1,0:T(8,128)(2,1)S(1)}, bf16[2,160,256]{2,1,0:T(8,128)(2,1)S(1)}, u32[]{:S(2)}, u32[]{:S(2)}) %collective-permute-start.27) | collective-permute-done | bytes 163872 | tf_op jit(solution)/shard_map/ppermute | solution.py:256
  126.6 2.6 %collective-permute-start.30 = (bf16[1,160,256]{2,1,0:T(8,128)(2,1)S(1)}, bf16[1,160,256]{2,1,0:T(8,128)(2,1)S(1)}, u32[]{:S(2)}, u32[]{:S(2)}) collective-permute-start(bf16[1,160,256]{2,1,0:T(8,128)(2,1)S(1)} %get-tuple-element.157), channel_id=1, source_target_pairs={{0,16},{4,20},{8,24},{12,28},{16,0},{20,4},{24,8},{28,12},{1,17},{... | collective-permute-start | bytes 245768 | tf_op jit(solution)/shard_map/ppermute | solution.py:256
  129.2 2.1 %keep_part.7 = (f32[160,256]{1,0:T(8,128)S(1)}, bf16[160,256]{1,0:T(8,128)(2,1)S(1)}, bf16[160,256]{1,0:T(8,128)(2,1)S(1)}, bf16[160,256]{1,0:T(8,128)(2,1)S(1)}) custom-call(s32[4]{0:T(128)S(1)} %pad_add_fusion.ids, bf16[3,640,1280]{2,1,0:T(8,128)(2,1)S(1)} %bitcast.62, bf16[640,6]{1,0:T(8,128)(2,1)S(1)} %get-tuple-element.124.refs_1_, ...), custom_call_target="tpu_custom_call" | custom-call | tf_op jit(solution)/shard_map/keep_part/pallas_call | solution.py:21
  133.7 3.0 %collective-permute-start.36 = (bf16[160,256]{1,0:T(8,128)(2,1)S(1)}, bf16[160,256]{1,0:T(8,128)(2,1)S(1)}, u32[]{:S(2)}, u32[]{:S(2)}) collective-permute-start(bf16[160,256]{1,0:T(8,128)(2,1)S(1)} %get-tuple-element.168), channel_id=1, source_target_pairs={{0,8},{4,12},{8,0},{12,4},{16,24},{20,28},{24,16},{28,20},{1,9},{5... | collective-permute-start | bytes 245768 | tf_op jit(solution)/shard_map/ppermute | solution.py:256
  136.7 1.6 %collective-permute-start.37 = (bf16[160,256]{1,0:T(8,128)(2,1)S(1)}, bf16[160,256]{1,0:T(8,128)(2,1)S(1)}, u32[]{:S(2)}, u32[]{:S(2)}) collective-permute-start(bf16[160,256]{1,0:T(8,128)(2,1)S(1)} %get-tuple-element.169), channel_id=1, source_target_pairs={{0,16},{4,20},{8,24},{12,28},{16,0},{20,4},{24,8},{28,12},{1,17},{... | collective-permute-start | bytes 245768 | tf_op jit(solution)/shard_map/ppermute | solution.py:256
  139.9 1.5 collective-permute-start.34
  141.3 4.6 %collective-permute-done.37.refs_1_ = bf16[160,256]{1,0:T(8,128)(2,1)S(1)} collective-permute-done((bf16[160,256]{1,0:T(8,128)(2,1)S(1)}, bf16[160,256]{1,0:T(8,128)(2,1)S(1)}, u32[]{:S(2)}, u32[]{:S(2)}) %collective-permute-start.37) | collective-permute-done | bytes 81952 | tf_op jit(solution)/shard_map/ppermute | solution.py:256
  147.3 4.6 %collective-permute-done.39.refs_4_ = f32[160,128]{1,0:T(8,128)S(1)} collective-permute-done((f32[160,128]{1,0:T(8,128)S(1)}, f32[160,128]{1,0:T(8,128)S(1)}, u32[]{:S(2)}, u32[]{:S(2)}) %collective-permute-start.39) | collective-permute-done | bytes 81952 | tf_op jit(solution)/shard_map/ppermute | solution.py:250
  151.9 1.6 %finish.1 = f32[4,160,320]{2,1,0:T(8,128)} custom-call(s32[4]{0:T(128)S(1)} %pad_add_fusion.ids, f32[160,320]{1,0:T(8,128)S(1)} %collective-permute-done.29.refs_0_, f32[160,192]{1,0:T(8,128)S(1)} %slice.64.refs_1_, f32[160,320]{1,0:T(8,128)S(1)} %collective-permute-done.34.refs_2_, f32[160,192]{1,0:T(8,128)S(1)} %collective-permute-done.35.refs_3_, ...), custom_call_target="tpu_custom_call" | custom-call | tf_op jit(solution)/shard_map/finish/pallas_call | solution.py:21
  (121 shorter events, 25.5 us)
Async XLA Ops:
  0.0 41.9 %copy-start = (bf16[3,160,1280]{2,1,0:T(8,128)(2,1)S(1)}, bf16[3,160,1280]{2,1,0:T(8,128)(2,1)}, u32[]{:S(2)}) copy-start(bf16[3,160,1280]{2,1,0:T(8,128)(2,1)} %param.8) | copy-start | bytes 3686404
  0.0 9.8 %collective-permute-start = (bf16[3,320,1280]{2,1,0:T(8,128)(2,1)}, bf16[3,320,1280]{2,1,0:T(8,128)(2,1)}, u32[]{:S(2)}, u32[]{:S(2)}) collective-permute-start(bf16[3,320,1280]{2,1,0:T(8,128)(2,1)} %param.7), channel_id=1, source_target_pairs={{0,1},{1,0},{2,3},{3,2},{4,5},{5,4},{6,7},{7,6},{8,9},{9,8},{10,11... | collective-permute-start | bytes 7372808 | tf_op jit(solution)/shard_map/ppermute | solution.py:250
  1.5 6.4 %collective-permute-start.1 = (bf16[40,1280]{1,0:T(8,128)(2,1)S(1)}, bf16[40,1280]{1,0:T(8,128)(2,1)S(1)}, u32[]{:S(2)}, u32[]{:S(2)}) collective-permute-start(bf16[40,1280]{1,0:T(8,128)(2,1)S(1)} %get-tuple-element.174), channel_id=1, source_target_pairs={{0,1},{1,0},{2,3},{3,2},{4,5},{5,4},{6,7},{7,6},{8,9},{9,8},{10,11... | collective-permute-start | bytes 307208 | tf_op jit(solution)/shard_map/ppermute | solution.py:250
  1.7 6.1 %collective-permute-start.2 = (bf16[40,1280]{1,0:T(8,128)(2,1)S(1)}, bf16[40,1280]{1,0:T(8,128)(2,1)S(1)}, u32[]{:S(2)}, u32[]{:S(2)}) collective-permute-start(bf16[40,1280]{1,0:T(8,128)(2,1)S(1)} %get-tuple-element.176), channel_id=1, source_target_pairs={{0,2},{1,3},{2,0},{3,1},{4,6},{5,7},{6,4},{7,5},{8,10},{9,11},{10,... | collective-permute-start | bytes 307208 | tf_op jit(solution)/shard_map/ppermute | solution.py:250
  4.6 5.2 %collective-permute-start.3 = (bf16[40,1280]{1,0:T(8,128)(2,1)S(1)}, bf16[40,1280]{1,0:T(8,128)(2,1)S(1)}, u32[]{:S(2)}, u32[]{:S(2)}) collective-permute-start(bf16[40,1280]{1,0:T(8,128)(2,1)S(1)} %get-tuple-element.173), channel_id=1, source_target_pairs={{0,3},{1,2},{2,1},{3,0},{4,7},{5,6},{6,5},{7,4},{8,11},{9,10},{10,... | collective-permute-start | bytes 307208 | tf_op jit(solution)/shard_map/ppermute | solution.py:250
  4.6 37.2 %copy-start.19 = (s32[4,2]{0,1:T(2,128)S(1)}, s32[4,2]{0,1:T(2,128)}, u32[]{:S(2)}) copy-start(s32[4,2]{0,1:T(2,128)} %param.9) | copy-start | bytes 100
  7.9 45.2 %copy-start.16 = (s32[20,20]{1,0:T(8,128)S(1)}, s32[20,20]{1,0:T(8,128)}, u32[]{:S(2)}) copy-start(s32[20,20]{1,0:T(8,128)} %tiles.5) | copy-start | bytes 4804
  9.8 30.7 %collective-permute-start.8 = (bf16[3,1,160,1280]{3,2,1,0:T(8,128)(2,1)}, bf16[3,1,160,1280]{3,2,1,0:T(8,128)(2,1)S(1)}, u32[]{:S(2)}, u32[]{:S(2)}) collective-permute-start(bf16[3,1,160,1280]{3,2,1,0:T(8,128)(2,1)} %get-tuple-element.91), channel_id=1, source_target_pairs={{0,2},{1,3},{2,0},{3,1},{4,6},{5,7},{6,4},{7,5},{8,10},{9,11},{10,... | collective-permute-start | bytes 3686408 | tf_op jit(solution)/shard_map/ppermute | solution.py:250
  12.8 9.3 %collective-permute-start.4 = (bf16[80,1280]{1,0:T(8,128)(2,1)S(1)}, bf16[80,1280]{1,0:T(8,128)(2,1)S(1)}, u32[]{:S(2)}, u32[]{:S(2)}) collective-permute-start(bf16[80,1280]{1,0:T(8,128)(2,1)S(1)} %bitcast.70), channel_id=1, source_target_pairs={{0,8},{4,12},{8,16},{12,20},{16,24},{20,28},{24,0},{28,4},{1,9},{5... | collective-permute-start | bytes 614408 | tf_op jit(solution)/shard_map/ppermute | solution.py:259
  14.4 7.6 %collective-permute-start.5 = (bf16[80,1280]{1,0:T(8,128)(2,1)S(1)}, bf16[80,1280]{1,0:T(8,128)(2,1)S(1)}, u32[]{:S(2)}, u32[]{:S(2)}) collective-permute-start(bf16[80,1280]{1,0:T(8,128)(2,1)S(1)} %bitcast.71), channel_id=1, source_target_pairs={{0,4},{4,0},{8,12},{12,8},{16,20},{20,16},{24,28},{28,24},{1,5},{5... | collective-permute-start | bytes 614408 | tf_op jit(solution)/shard_map/ppermute | solution.py:253
  17.8 9.0 %collective-permute-start.11 = (bf16[80,1280]{1,0:T(8,128)(2,1)S(1)}, bf16[80,1280]{1,0:T(8,128)(2,1)S(1)}, u32[]{:S(2)}, u32[]{:S(2)}) collective-permute-start(bf16[80,1280]{1,0:T(8,128)(2,1)S(1)} %bitcast.73), channel_id=1, source_target_pairs={{0,8},{4,12},{8,16},{12,20},{16,24},{20,28},{24,0},{28,4},{1,9},{5... | collective-permute-start | bytes 614408 | tf_op jit(solution)/shard_map/ppermute | solution.py:259
  19.4 7.8 %collective-permute-start.12 = (bf16[80,1280]{1,0:T(8,128)(2,1)S(1)}, bf16[80,1280]{1,0:T(8,128)(2,1)S(1)}, u32[]{:S(2)}, u32[]{:S(2)}) collective-permute-start(bf16[80,1280]{1,0:T(8,128)(2,1)S(1)} %bitcast.74), channel_id=1, source_target_pairs={{0,4},{4,0},{8,12},{12,8},{16,20},{20,16},{24,28},{28,24},{1,5},{5... | collective-permute-start | bytes 614408 | tf_op jit(solution)/shard_map/ppermute | solution.py:253
  22.0 9.1 %collective-permute-start.6 = (bf16[80,1280]{1,0:T(8,128)(2,1)S(1)}, bf16[80,1280]{1,0:T(8,128)(2,1)S(1)}, u32[]{:S(2)}, u32[]{:S(2)}) collective-permute-start(bf16[80,1280]{1,0:T(8,128)(2,1)S(1)} %collective-permute-done.4.refs_1_), channel_id=1, source_target_pairs={{0,8},{4,12},{8,16},{12,20},{16,24},{20,28},{24,0},{28,4},{1,9},{5... | collective-permute-start | bytes 614408 | tf_op jit(solution)/shard_map/ppermute | solution.py:259
  23.0 8.1 %collective-permute-start.7 = (bf16[80,1280]{1,0:T(8,128)(2,1)S(1)}, bf16[80,1280]{1,0:T(8,128)(2,1)S(1)}, u32[]{:S(2)}, u32[]{:S(2)}) collective-permute-start(bf16[80,1280]{1,0:T(8,128)(2,1)S(1)} %collective-permute-done.4.refs_1_), channel_id=1, source_target_pairs={{0,4},{4,0},{8,12},{12,8},{16,20},{20,16},{24,28},{28,24},{1,5},{5... | collective-permute-start | bytes 614408 | tf_op jit(solution)/shard_map/ppermute | solution.py:253
  27.9 7.6 %collective-permute-start.13 = (bf16[80,1280]{1,0:T(8,128)(2,1)S(1)}, bf16[80,1280]{1,0:T(8,128)(2,1)S(1)}, u32[]{:S(2)}, u32[]{:S(2)}) collective-permute-start(bf16[80,1280]{1,0:T(8,128)(2,1)S(1)} %collective-permute-done.11.refs_5_), channel_id=1, source_target_pairs={{0,8},{4,12},{8,16},{12,20},{16,24},{20,28},{24,0},{28,4},{1,9},{5... | collective-permute-start | bytes 614408 | tf_op jit(solution)/shard_map/ppermute | solution.py:259
  29.5 7.8 %collective-permute-start.14 = (bf16[80,1280]{1,0:T(8,128)(2,1)S(1)}, bf16[80,1280]{1,0:T(8,128)(2,1)S(1)}, u32[]{:S(2)}, u32[]{:S(2)}) collective-permute-start(bf16[80,1280]{1,0:T(8,128)(2,1)S(1)} %collective-permute-done.11.refs_5_), channel_id=1, source_target_pairs={{0,4},{4,0},{8,12},{12,8},{16,20},{20,16},{24,28},{28,24},{1,5},{5... | collective-permute-start | bytes 614408 | tf_op jit(solution)/shard_map/ppermute | solution.py:253
  31.8 7.9 %collective-permute-start.10 = (bf16[80,1280]{1,0:T(8,128)(2,1)S(1)}, bf16[80,1280]{1,0:T(8,128)(2,1)S(1)}, u32[]{:S(2)}, u32[]{:S(2)}) collective-permute-start(bf16[80,1280]{1,0:T(8,128)(2,1)S(1)} %collective-permute-done.6.refs_2_), channel_id=1, source_target_pairs={{0,4},{4,0},{8,12},{12,8},{16,20},{20,16},{24,28},{28,24},{1,5},{5... | collective-permute-start | bytes 614408 | tf_op jit(solution)/shard_map/ppermute | solution.py:253
  33.0 7.6 %collective-permute-start.9 = (bf16[80,1280]{1,0:T(8,128)(2,1)S(1)}, bf16[80,1280]{1,0:T(8,128)(2,1)S(1)}, u32[]{:S(2)}, u32[]{:S(2)}) collective-permute-start(bf16[80,1280]{1,0:T(8,128)(2,1)S(1)} %collective-permute-done.6.refs_2_), channel_id=1, source_target_pairs={{0,8},{4,12},{8,16},{12,20},{16,24},{20,28},{24,0},{28,4},{1,9},{5... | collective-permute-start | bytes 614408 | tf_op jit(solution)/shard_map/ppermute | solution.py:259
  35.5 5.1 %copy-start.8 = (bf16[80,1280]{1,0:T(8,128)(2,1)}, bf16[80,1280]{1,0:T(8,128)(2,1)S(1)}, u32[]{:S(2)}) copy-start(bf16[80,1280]{1,0:T(8,128)(2,1)S(1)} %collective-permute-done.13.refs_6_) | copy-start | bytes 614404
  40.6 19.2 %collective-permute-start.19 = (bf16[3,1,160,1280]{3,2,1,0:T(8,128)(2,1)S(1)}, bf16[3,1,160,1280]{3,2,1,0:T(8,128)(2,1)}, u32[]{:S(2)}, u32[]{:S(2)}) collective-permute-start(bf16[3,1,160,1280]{3,2,1,0:T(8,128)(2,1)S(1)} %collective-permute-done.8.refs_0_), channel_id=1, source_target_pairs={{0,1},{1,0},{2,3},{3,2},{4,5},{5,4},{6,7},{7,6},{8,9},{9,8},{10,11... | collective-permute-start | bytes 3686408 | tf_op jit(solution)/shard_map/ppermute | solution.py:250
  41.3 34.3 %collective-permute-start.20 = (bf16[3,1,160,1280]{3,2,1,0:T(8,128)(2,1)}, bf16[3,1,160,1280]{3,2,1,0:T(8,128)(2,1)}, u32[]{:S(2)}, u32[]{:S(2)}) collective-permute-start(bf16[3,1,160,1280]{3,2,1,0:T(8,128)(2,1)} %get-tuple-element.118), channel_id=1, source_target_pairs={{0,2},{1,3},{2,0},{3,1},{4,6},{5,7},{6,4},{7,5},{8,10},{9,11},{10,... | collective-permute-start | bytes 3686408 | tf_op jit(solution)/shard_map/ppermute | solution.py:250
  42.5 8.7 %collective-permute-start.15 = (bf16[80,1280]{1,0:T(8,128)(2,1)}, bf16[80,1280]{1,0:T(8,128)(2,1)S(1)}, u32[]{:S(2)}, u32[]{:S(2)}) collective-permute-start(bf16[80,1280]{1,0:T(8,128)(2,1)} %copy-done.8), channel_id=1, source_target_pairs={{0,8},{4,12},{8,16},{12,20},{16,24},{20,28},{24,0},{28,4},{1,9},{5... | collective-permute-start | bytes 614408 | tf_op jit(solution)/shard_map/ppermute | solution.py:259
  43.3 8.2 %collective-permute-start.16 = (bf16[80,1280]{1,0:T(8,128)(2,1)}, bf16[80,1280]{1,0:T(8,128)(2,1)S(1)}, u32[]{:S(2)}, u32[]{:S(2)}) collective-permute-start(bf16[80,1280]{1,0:T(8,128)(2,1)} %copy-done.8), channel_id=1, source_target_pairs={{0,4},{4,0},{8,12},{12,8},{16,20},{20,16},{24,28},{28,24},{1,5},{5... | collective-permute-start | bytes 614408 | tf_op jit(solution)/shard_map/ppermute | solution.py:253
  44.8 14.1 %collective-permute-start.17 = (bf16[80,1280]{1,0:T(8,128)(2,1)}, bf16[80,1280]{1,0:T(8,128)(2,1)S(1)}, u32[]{:S(2)}, u32[]{:S(2)}) collective-permute-start(bf16[80,1280]{1,0:T(8,128)(2,1)} %copy-done.14), channel_id=1, source_target_pairs={{0,4},{4,0},{8,12},{12,8},{16,20},{20,16},{24,28},{28,24},{1,5},{5... | collective-permute-start | bytes 614408 | tf_op jit(solution)/shard_map/ppermute | solution.py:253
  51.5 7.4 %collective-permute-start.18 = (bf16[80,1280]{1,0:T(8,128)(2,1)S(1)}, bf16[80,1280]{1,0:T(8,128)(2,1)S(1)}, u32[]{:S(2)}, u32[]{:S(2)}) collective-permute-start(bf16[80,1280]{1,0:T(8,128)(2,1)S(1)} %collective-permute-done.15.refs_7_), channel_id=1, source_target_pairs={{0,4},{4,0},{8,12},{12,8},{16,20},{20,16},{24,28},{28,24},{1,5},{5... | collective-permute-start | bytes 614408 | tf_op jit(solution)/shard_map/ppermute | solution.py:253
  54.7 4.2 %copy-start.9 = (bf16[80,1280]{1,0:T(8,128)(2,1)S(1)}, bf16[80,1280]{1,0:T(8,128)(2,1)}, u32[]{:S(2)}) copy-start(bf16[80,1280]{1,0:T(8,128)(2,1)} %copy-done.8) | copy-start | bytes 614404
  54.7 4.2 %copy-start.11 = (bf16[80,1280]{1,0:T(8,128)(2,1)S(1)}, bf16[80,1280]{1,0:T(8,128)(2,1)}, u32[]{:S(2)}) copy-start(bf16[80,1280]{1,0:T(8,128)(2,1)} %copy-done.10) | copy-start | bytes 614404
  54.8 4.2 %copy-start.13 = (bf16[80,1280]{1,0:T(8,128)(2,1)S(1)}, bf16[80,1280]{1,0:T(8,128)(2,1)}, u32[]{:S(2)}) copy-start(bf16[80,1280]{1,0:T(8,128)(2,1)} %copy-done.12) | copy-start | bytes 614404
  54.8 4.2 %copy-start.15 = (bf16[80,1280]{1,0:T(8,128)(2,1)S(1)}, bf16[80,1280]{1,0:T(8,128)(2,1)}, u32[]{:S(2)}) copy-start(bf16[80,1280]{1,0:T(8,128)(2,1)} %copy-done.14) | copy-start | bytes 614404
  75.5 3.2 %collective-permute-start.21 = (bf16[3,1,160,1280]{3,2,1,0:T(8,128)(2,1)}, bf16[3,1,160,1280]{3,2,1,0:T(8,128)(2,1)S(1)}, u32[]{:S(2)}, u32[]{:S(2)}) collective-permute-start(bf16[3,1,160,1280]{3,2,1,0:T(8,128)(2,1)} %collective-permute-done.20.refs_0_), channel_id=1, source_target_pairs={{0,1},{1,0},{2,3},{3,2},{4,5},{5,4},{6,7},{7,6},{8,9},{9,8},{10,11... | collective-permute-start | bytes 3686408 | tf_op jit(solution)/shard_map/ppermute | solution.py:250
  75.6 13.4 %collective-permute-start.23 = (bf16[4,160,256]{2,1,0:T(8,128)(2,1)S(1)}, bf16[4,160,256]{2,1,0:T(8,128)(2,1)S(1)}, u32[]{:S(2)}, u32[]{:S(2)}) collective-permute-start(bf16[4,160,256]{2,1,0:T(8,128)(2,1)S(1)} %get-tuple-element.128), channel_id=1, source_target_pairs={{0,4},{4,0},{8,12},{12,8},{16,20},{20,16},{24,28},{28,24},{1,5},{5... | collective-permute-start | bytes 983048 | tf_op jit(solution)/shard_map/ppermute | solution.py:253
  77.2 16.0 %collective-permute-start.22 = (bf16[4,160,256]{2,1,0:T(8,128)(2,1)S(1)}, bf16[4,160,256]{2,1,0:T(8,128)(2,1)S(1)}, u32[]{:S(2)}, u32[]{:S(2)}) collective-permute-start(bf16[4,160,256]{2,1,0:T(8,128)(2,1)S(1)} %get-tuple-element.127), channel_id=1, source_target_pairs={{0,4},{4,0},{8,12},{12,8},{16,20},{20,16},{24,28},{28,24},{1,5},{5... | collective-permute-start | bytes 983048 | tf_op jit(solution)/shard_map/ppermute | solution.py:253
  87.4 19.6 %collective-permute-start.24 = (bf16[4,160,256]{2,1,0:T(8,128)(2,1)S(1)}, bf16[4,160,256]{2,1,0:T(8,128)(2,1)S(1)}, u32[]{:S(2)}, u32[]{:S(2)}) collective-permute-start(bf16[4,160,256]{2,1,0:T(8,128)(2,1)S(1)} %get-tuple-element.133), channel_id=1, source_target_pairs={{0,4},{4,0},{8,12},{12,8},{16,20},{20,16},{24,28},{28,24},{1,5},{5... | collective-permute-start | bytes 983048 | tf_op jit(solution)/shard_map/ppermute | solution.py:253
  96.8 17.6 %collective-permute-start.25 = (bf16[2,160,512]{2,1,0:T(8,128)(2,1)S(1)}, bf16[2,160,512]{2,1,0:T(8,128)(2,1)S(1)}, u32[]{:S(2)}, u32[]{:S(2)}) collective-permute-start(bf16[2,160,512]{2,1,0:T(8,128)(2,1)S(1)} %get-tuple-element.136), channel_id=1, source_target_pairs={{0,8},{4,12},{8,0},{12,4},{16,24},{20,28},{24,16},{28,20},{1,9},{5... | collective-permute-start | bytes 983048 | tf_op jit(solution)/shard_map/ppermute | solution.py:256
  105.4 14.9 %collective-permute-start.26 = (bf16[4,160,256]{2,1,0:T(8,128)(2,1)S(1)}, bf16[4,160,256]{2,1,0:T(8,128)(2,1)S(1)}, u32[]{:S(2)}, u32[]{:S(2)}) collective-permute-start(bf16[4,160,256]{2,1,0:T(8,128)(2,1)S(1)} %get-tuple-element.148), channel_id=1, source_target_pairs={{0,4},{4,0},{8,12},{12,8},{16,20},{20,16},{24,28},{28,24},{1,5},{5... | collective-permute-start | bytes 983048 | tf_op jit(solution)/shard_map/ppermute | solution.py:253
  113.8 15.4 %collective-permute-start.31 = (bf16[4,160,256]{2,1,0:T(8,128)(2,1)S(1)}, bf16[4,160,256]{2,1,0:T(8,128)(2,1)S(1)}, u32[]{:S(2)}, u32[]{:S(2)}) collective-permute-start(bf16[4,160,256]{2,1,0:T(8,128)(2,1)S(1)} %get-tuple-element.161), channel_id=1, source_target_pairs={{0,4},{4,0},{8,12},{12,8},{16,20},{20,16},{24,28},{28,24},{1,5},{5... | collective-permute-start | bytes 983048 | tf_op jit(solution)/shard_map/ppermute | solution.py:253
  117.1 8.9 %collective-permute-start.27 = (bf16[2,160,256]{2,1,0:T(8,128)(2,1)S(1)}, bf16[2,160,256]{2,1,0:T(8,128)(2,1)S(1)}, u32[]{:S(2)}, u32[]{:S(2)}) collective-permute-start(bf16[2,160,256]{2,1,0:T(8,128)(2,1)S(1)} %get-tuple-element.150), channel_id=1, source_target_pairs={{0,8},{4,12},{8,0},{12,4},{16,24},{20,28},{24,16},{28,20},{1,9},{5... | collective-permute-start | bytes 491528 | tf_op jit(solution)/shard_map/ppermute | solution.py:256
  117.6 9.0 %collective-permute-start.28 = (bf16[1,160,512]{2,1,0:T(8,128)(2,1)S(1)}, bf16[1,160,512]{2,1,0:T(8,128)(2,1)S(1)}, u32[]{:S(2)}, u32[]{:S(2)}) collective-permute-start(bf16[1,160,512]{2,1,0:T(8,128)(2,1)S(1)} %get-tuple-element.153), channel_id=1, source_target_pairs={{0,16},{4,20},{8,24},{12,28},{16,0},{20,4},{24,8},{28,12},{1,17},{... | collective-permute-start | bytes 491528 | tf_op jit(solution)/shard_map/ppermute | solution.py:256
  122.4 9.0 %collective-permute-start.32 = (bf16[2,160,256]{2,1,0:T(8,128)(2,1)S(1)}, bf16[2,160,256]{2,1,0:T(8,128)(2,1)S(1)}, u32[]{:S(2)}, u32[]{:S(2)}) collective-permute-start(bf16[2,160,256]{2,1,0:T(8,128)(2,1)S(1)} %get-tuple-element.163), channel_id=1, source_target_pairs={{0,8},{4,12},{8,0},{12,4},{16,24},{20,28},{24,16},{28,20},{1,9},{5... | collective-permute-start | bytes 491528 | tf_op jit(solution)/shard_map/ppermute | solution.py:256
  126.6 6.5 %collective-permute-start.30 = (bf16[1,160,256]{2,1,0:T(8,128)(2,1)S(1)}, bf16[1,160,256]{2,1,0:T(8,128)(2,1)S(1)}, u32[]{:S(2)}, u32[]{:S(2)}) collective-permute-start(bf16[1,160,256]{2,1,0:T(8,128)(2,1)S(1)} %get-tuple-element.157), channel_id=1, source_target_pairs={{0,16},{4,20},{8,24},{12,28},{16,0},{20,4},{24,8},{28,12},{1,17},{... | collective-permute-start | bytes 245768 | tf_op jit(solution)/shard_map/ppermute | solution.py:256
  131.9 7.2 %collective-permute-start.33 = (bf16[1,160,256]{2,1,0:T(8,128)(2,1)S(1)}, bf16[1,160,256]{2,1,0:T(8,128)(2,1)S(1)}, u32[]{:S(2)}, u32[]{:S(2)}) collective-permute-start(bf16[1,160,256]{2,1,0:T(8,128)(2,1)S(1)} %get-tuple-element.166), channel_id=1, source_target_pairs={{0,16},{4,20},{8,24},{12,28},{16,0},{20,4},{24,8},{28,12},{1,17},{... | collective-permute-start | bytes 245768 | tf_op jit(solution)/shard_map/ppermute | solution.py:256
  133.0 14.3 %collective-permute-start.29 = (f32[160,320]{1,0:T(8,128)S(1)}, f32[160,320]{1,0:T(8,128)S(1)}, u32[]{:S(2)}, u32[]{:S(2)}) collective-permute-start(f32[160,320]{1,0:T(8,128)S(1)} %concatenate.40), channel_id=1, source_target_pairs={{0,1},{1,0},{2,3},{3,2},{4,5},{5,4},{6,7},{7,6},{8,9},{9,8},{10,11... | collective-permute-start | bytes 614408 | tf_op jit(solution)/shard_map/ppermute | solution.py:250
  133.7 7.7 %collective-permute-start.36 = (bf16[160,256]{1,0:T(8,128)(2,1)S(1)}, bf16[160,256]{1,0:T(8,128)(2,1)S(1)}, u32[]{:S(2)}, u32[]{:S(2)}) collective-permute-start(bf16[160,256]{1,0:T(8,128)(2,1)S(1)} %get-tuple-element.168), channel_id=1, source_target_pairs={{0,8},{4,12},{8,0},{12,4},{16,24},{20,28},{24,16},{28,20},{1,9},{5... | collective-permute-start | bytes 245768 | tf_op jit(solution)/shard_map/ppermute | solution.py:256
  136.7 9.2 %collective-permute-start.37 = (bf16[160,256]{1,0:T(8,128)(2,1)S(1)}, bf16[160,256]{1,0:T(8,128)(2,1)S(1)}, u32[]{:S(2)}, u32[]{:S(2)}) collective-permute-start(bf16[160,256]{1,0:T(8,128)(2,1)S(1)} %get-tuple-element.169), channel_id=1, source_target_pairs={{0,16},{4,20},{8,24},{12,28},{16,0},{20,4},{24,8},{28,12},{1,17},{... | collective-permute-start | bytes 245768 | tf_op jit(solution)/shard_map/ppermute | solution.py:256
  138.3 7.6 %collective-permute-start.38 = (bf16[160,256]{1,0:T(8,128)(2,1)S(1)}, bf16[160,256]{1,0:T(8,128)(2,1)S(1)}, u32[]{:S(2)}, u32[]{:S(2)}) collective-permute-start(bf16[160,256]{1,0:T(8,128)(2,1)S(1)} %get-tuple-element.170), channel_id=1, source_target_pairs={{0,24},{4,28},{8,16},{12,20},{16,8},{20,12},{24,0},{28,4},{1,25},{... | collective-permute-start | bytes 245768 | tf_op jit(solution)/shard_map/ppermute | solution.py:256
  139.9 12.1 %collective-permute-start.34 = (f32[160,320]{1,0:T(8,128)S(1)}, f32[160,320]{1,0:T(8,128)S(1)}, u32[]{:S(2)}, u32[]{:S(2)}) collective-permute-start(f32[160,320]{1,0:T(8,128)S(1)} %pad_maximum_fusion), channel_id=1, source_target_pairs={{0,2},{1,3},{2,0},{3,1},{4,6},{5,7},{6,4},{7,5},{8,10},{9,11},{10,... | collective-permute-start | bytes 614408 | tf_op jit(solution)/shard_map/ppermute | solution.py:250
  141.3 10.6 %collective-permute-start.35 = (f32[160,192]{1,0:T(8,128)S(1)}, f32[160,192]{1,0:T(8,128)S(1)}, u32[]{:S(2)}, u32[]{:S(2)}) collective-permute-start(f32[160,192]{1,0:T(8,128)S(1)} %slice.66), channel_id=1, source_target_pairs={{0,3},{1,2},{2,1},{3,0},{4,7},{5,6},{6,5},{7,4},{8,11},{9,10},{10,... | collective-permute-start | bytes 368648 | tf_op jit(solution)/shard_map/ppermute | solution.py:250
  146.5 5.4 %collective-permute-start.39 = (f32[160,128]{1,0:T(8,128)S(1)}, f32[160,128]{1,0:T(8,128)S(1)}, u32[]{:S(2)}, u32[]{:S(2)}) collective-permute-start(f32[160,128]{1,0:T(8,128)S(1)} %get-tuple-element.178), channel_id=1, source_target_pairs={{0,3},{1,2},{2,1},{3,0},{4,7},{5,6},{6,5},{7,4},{8,11},{9,10},{10,... | collective-permute-start | bytes 245768 | tf_op jit(solution)/shard_map/ppermute | solution.py:250
  (12 other events, 22.2 us)

commit v3 on v2

--- a/solution.py
+++ b/solution.py
@@ -68,9 +68,8 @@
 
 
 def place_blocks(places, ids, *refs):
-    blocks, out = refs[:-1], refs[-1]
-    for place, block in zip(places(ids), blocks, strict=True):
-        out[place] = block[...]
+    for place, block in zip(places, refs, strict=False):
+        refs[-1][place(ids)] = block[...]
 
 
 def masked_block(ids, tiles, piece, group, half, groups, block, size):
@@ -159,51 +158,71 @@
     block = send.shape[1]
     pick_rows(segments, width, ids, others, kepts, picked)
     picked[aux * width :, :] = second[...]
-    times_amplitudes(picked, amp, inter, rows)
-    u = rows[...]
-    high = u.astype(BF).astype(F32)
-    turned[...] = jnp.concatenate([high[:aux], (u - high)[:aux]], axis=0).T
-    for h in range(send.shape[0]):
-        for half, out in ((1 - ids[LOW], other), (ids[LOW], kept)):
-            at = pl.ds(pl.multiple_of((2 * h + half) * block, 8), block)
-            out[h * block : (h + 1) * block, :] = turned[at, :].astype(BF)
-    value = multiply_rows(factors, inter, other, first, width)
-    for h in range(send.shape[0]):
-        send[h] = value[h * block : (h + 1) * block, :].astype(BF)
+
+    @pl.when(ids[LOW] >= 0)
+    def _():
+        times_amplitudes(picked, amp, inter, rows)
+
+    @pl.when(ids[LOW] >= 0)
+    def _():
+        u = rows[...]
+        high = u.astype(BF).astype(F32)
+        turned[...] = jnp.concatenate([high[:aux], (u - high)[:aux]], axis=0).T
+        for h in range(send.shape[0]):
+            for half, out in ((1 - ids[LOW], other), (ids[LOW], kept)):
+                at = pl.ds(pl.multiple_of((2 * h + half) * block, 8), block)
+                out[h * block : (h + 1) * block, :] = turned[at, :].astype(BF)
+
+    @pl.when(ids[LOW] >= 0)
+    def _():
+        value = multiply_rows(factors, inter, other, first, width)
+        for h in range(send.shape[0]):
+            send[h] = value[h * block : (h + 1) * block, :].astype(BF)
 
 
 def send_part(segments, width, ids, *refs):
     others, kepts, amp, factors, carried, first, inter, send, picked = refs
     block = send.shape[1]
     pick_rows(segments, width, ids, others, kepts, picked)
-    times_amplitudes(picked, amp, inter)
-    value = multiply_rows(factors, inter, carried, first, width)
-    for h in range(send.shape[0]):
-        send[h] = value[h * block : (h + 1) * block, :].astype(BF)
-
-
-def keep_rows(count, width, ids, factors, carried, *refs):
+
+    @pl.when(ids[LOW] >= 0)
+    def _():
+        times_amplitudes(picked, amp, inter)
+
+    @pl.when(ids[LOW] >= 0)
+    def _():
+        value = multiply_rows(factors, inter, carried, first, width)
+        for h in range(send.shape[0]):
+            send[h] = value[h * block : (h + 1) * block, :].astype(BF)
+
+
+def keep_rows(widths, ids, factors, carried, *refs):
+    count = len(widths)
     inter, first, got = refs[:count], refs[count : 2 * count], refs[2 * count : 3 * count]
     total = refs[-1]
     block = got[0].shape[1]
-    for c in range(count):
-        value = multiply_rows(factors, inter[c], carried, first[c], width)
-        for h in range(got[c].shape[0]):
-            total[h, :, c * width : (c + 1) * width] = (
-                value[h * block : (h + 1) * block, :] + got[c][h].astype(F32)
-            )
+
+    def part(c, at, width):
+        @pl.when(ids[LOW] >= 0)
+        def _():
+            value = multiply_rows(factors, inter[c], carried, first[c], width)
+            for h in range(got[c].shape[0]):
+                total[h, :, at : at + width] = value[h * block : (h + 1) * block, :] + got[c][h].astype(F32)
+
+    for c, width in enumerate(widths):
+        part(c, sum(widths[:c]), width)
     return refs[3 * count : -1], total
 
 
-def keep_direct(count, width, ids, *refs):
-    (own, *messages), total = keep_rows(count, width, ids, *refs)
+def keep_direct(widths, ids, *refs):
+    (own, *messages), total = keep_rows(widths, ids, *refs)
     own[...] = total[ids[HIGH]]
     for k, message in enumerate(messages, 1):
         message[...] = total[ids[HIGH] ^ k].astype(BF)
 
 
-def keep_halves(count, width, ids, *refs):
-    (mine, message), total = keep_rows(count, width, ids, *refs)
+def keep_halves(widths, ids, *refs):
+    (mine, message), total = keep_rows(widths, ids, *refs)
     for i in range(mine.shape[0]):
         mine[i] = total[ids[HIGH] ^ (2 * i)]
         message[i] = total[ids[HIGH] ^ (2 * i + 1)].astype(BF)
@@ -263,115 +282,139 @@
     split = integrals.reshape(aux, groups, 2, block, size)
     low = row % 2
     other, kept = {}, {}
-    send_other = Box(lax.dynamic_index_in_dim(split, 1 - low, 2, keepdims=False))
-    send_kept = Box(lax.dynamic_index_in_dim(split, low, 2, keepdims=False))
     split1 = Box(over_col(integrals, 1))
-    tie(send_other, send_kept, split1, *mine[1:])
-    other[2] = Box(over_col(send_other.value, 2))
-    pair_tiles = lax.dynamic_index_in_dim(amp_tiles, col, 0, keepdims=False)
+    tie(split1, mine[1])
+    split_other, split_kept = Box(split), Box(split)
+
+    def half_rows(box, half):
+        return Box(lax.dynamic_index_in_dim(box.value, half, 2, keepdims=False))
+
+    is_col = jnp.arange(n_pair, dtype=jnp.int32) == col
+    pair_tiles = Box(jnp.sum(jnp.where(is_col[:, None, None], amp_tiles, 0), axis=0))
+    tie(pair_tiles, mine[1])
+
+    pair = jnp.sum(jnp.where(is_col[:, None], pairs, 0), axis=0)
+    orbitals = jnp.arange(occupied.shape[1], dtype=jnp.int32)
+    picks = (pair[:, None] == orbitals[None, :]).astype(BF)
+    rows = jnp.einsum("po,qov->pqv", picks, occupied, preferred_element_type=F32).astype(BF)
+    first, second = rows[0], rows[1]
+    second = jnp.concatenate([second, jnp.zeros((16 - aux, size), BF)], axis=0)
+    first = first.reshape(aux, n_col, piece_rows)
+    first = [lax.dynamic_index_in_dim(first, col ^ k, 1, keepdims=False) for k in range(n_col)]
+    first = [jnp.concatenate([x, x], axis=0) for x in first]
+
+    step = min(256, piece_rows)
+    widths = [step, 2 * piece_rows - step, 2 * piece_rows - step, step]
+    cut = max(piece_rows - widths[-1], 0)
+    order = [(1, 0, piece_rows), (0, 0, piece_rows), (2, 0, piece_rows), (3, 0, cut), (3, cut, piece_rows - cut)]
+    order = [part for part in order if part[2]]
+    chunks, where = [[] for _ in widths], []
+    at = 0
+    for piece, start, count in order:
+        spans = []
+        while count:
+            done = sum(n for _, _, n in chunks[at])
+            n = min(count, widths[at] - done)
+            chunks[at].append((piece, start, n))
+            spans.append((at, done, n))
+            start, count = start + n, count - n
+            at += done + n == widths[at]
+        where.append(spans)
+    first = [jnp.concatenate([first[p][:, s : s + n] for p, s, n in chunk], axis=1) for chunk in chunks]
+
+    second, first = Box(second), [Box(x) for x in first]
 
     def half_slab(ks):
         return kernel_call(
             functools.partial(mask_slab, n_col, ks),
             like((2, chunk_rows, size), BF),
-            (ids, pair_tiles, *[mine[k].value for k in ks]),
+            (ids, pair_tiles.value, *[mine[k].value for k in ks]),
             name="half_slab",
         ).reshape(2 * chunk_rows, size)
 
-    rings = [[Box(half_slab((0, 1)))], [Box(half_slab((2, 3)))]]
+    shape = like((aux, n_high, block, size), BF)
+    all_other, all_kept = map(
+        Box,
+        kernel_call(
+            functools.partial(place_pieces, (0, 1)),
+            (shape, shape),
+            (ids, int_tiles, split, split1.value.reshape(split.shape)),
+            name="place_pieces",
+        ),
+    )
+
+    def place(pieces, k, into, other_half):
+        return kernel_call(
+            functools.partial(place_halves, (k,), other_half),
+            shape,
+            (ids, int_tiles, pieces[k].value, into.value),
+            aliases={3: 0},
+            name="place_halves",
+        )
+
+    def flat(x):
+        return x.reshape(aux, half_size, size)
+
+    def slab_place(step, other_low, side, ids):
+        h = lax.rem(ids[HIGH] + (n_high - step), n_high)
+        low = 1 - ids[LOW] if other_low else ids[LOW]
+        return (h * 2 + low) * 2 + (ids[COL] // 2 ^ side)
+
+    def place_slabs(found):
+        places = [functools.partial(slab_place, *place) for _, place in found]
+        return kernel_call(
+            functools.partial(place_blocks, places),
+            like((n_row * 2, 2 * chunk_rows, size), BF),
+            (ids, *[slab.value for slab, _ in found]),
+            name="place_rows",
+        )
+
+    rings = [[Box(half_slab((0, 1)))]]
+    tie(split_other, rings[0][0])
+    send_other = half_rows(split_other, 1 - low)
+    other[2] = Box(over_col(send_other.value, 2))
     swapped = [[], []]
-    for s in range(n_high):
-        for r, ring in enumerate(rings):
-            if s > 0:
-                tie(ring[s], swapped[r][-1])
-            if s + 1 < n_high:
-                ring.append(Box(up(ring[s].value)))
-            swapped[r].append(Box(over_low(ring[s].value)))
-    tie(other[2], rings[0][-1], rings[1][-2], swapped[0][-3], swapped[1][-3])
-    tie(send_kept, other[2])
+
+    def hop(r, s):
+        ring = rings[r]
+        if s > 0:
+            tie(ring[s], swapped[r][-1])
+        if s + 1 < n_high:
+            ring.append(Box(up(ring[s].value)))
+        swapped[r].append(Box(over_low(ring[s].value)))
+
+    tie(rings[0][0], mine[2], mine[3])
+    rings.append([Box(half_slab((2, 3)))])
+    hop(0, 0)
+    hop(1, 0)
+    tie(rings[0][1], second, *first)
+    tie(rings[0][1], split_kept)
+    send_kept = half_rows(split_kept, low)
+    tie(rings[0][1], send_kept)
+    tie(rings[1][1], all_other, all_kept)
+    for s in range(1, n_high):
+        hop(0, s)
+        hop(1, s)
+    tie(other[2], rings[0][-1], rings[1][-1])
     other[3] = Box(over_col(other[2].value, 1))
     kept[2] = Box(over_col(send_kept.value, 2))
-
-    def slab_places(ids):
-        highs = [lax.rem(ids[HIGH] + (n_high - s), n_high) for s in range(n_high)]
-        side = ids[COL] // 2
-        return [
-            ((h * 2 + low) * 2) + (side ^ r)
-            for low in (ids[LOW], 1 - ids[LOW])
-            for r in range(2)
-            for h in highs
-        ]
-
-    slabs = rings[0] + rings[1] + swapped[0] + swapped[1]
-    amp = kernel_call(
-        functools.partial(place_blocks, slab_places),
-        like((n_row * 2, 2 * chunk_rows, size), BF),
-        (ids, *[slab.value for slab in slabs]),
-        name="all_rows",
-    )
-    amp = Box(amp.reshape(size, size))
-
-    shape = like((aux, n_high, block, size), BF)
-    all_other, all_kept = kernel_call(
-        functools.partial(place_pieces, (0, 1)),
-        (shape, shape),
-        (ids, int_tiles, split, split1.value.reshape(split.shape)),
-        name="place_pieces",
-    )
-
-    def place(pieces, into, other_half):
-        return kernel_call(
-            functools.partial(place_halves, (2, 3), other_half),
-            shape,
-            (ids, int_tiles, pieces[2].value, pieces[3].value, into),
-            aliases={4: 0},
-            name="place_halves",
-        )
-
-    def flat(x):
-        return x.reshape(aux, half_size, size)
-
-    all_other = place(other, all_other, True)
-    all_kept = Box(all_kept)
-
-    orbitals = jnp.arange(occupied.shape[1], dtype=jnp.int32)
-    picks = (pairs.T.reshape(-1)[:, None] == orbitals[None, :]).astype(BF)
-    rows = jnp.einsum("po,qov->pqv", picks, occupied, preferred_element_type=F32).astype(BF)
-    first = lax.dynamic_index_in_dim(rows, col, 0, keepdims=False)
-    second = lax.dynamic_index_in_dim(rows, col + n_pair, 0, keepdims=False)
-    second = jnp.concatenate([second, jnp.zeros((16 - aux, size), BF)], axis=0)
-    first = first.reshape(aux, n_col, piece_rows)
-    first = [lax.dynamic_index_in_dim(first, col ^ k, 1, keepdims=False) for k in range(n_col)]
-    first = [jnp.concatenate([x, x], axis=0) for x in first]
-
-    width = 256 if size % 256 == 0 else piece_rows
-    cut = 2 * width - piece_rows
-    rest = piece_rows - cut
-    order = [(1, 0, piece_rows), (0, 0, cut), (2, 0, piece_rows), (3, 0, cut), (3, cut, rest), (0, cut, rest)]
-    chunks, where, at = [], [], 0
-    for piece, start, count in order:
-        spans = []
-        while count:
-            if at % width == 0:
-                chunks.append([])
-            n = min(count, width - at % width)
-            chunks[-1].append((piece, start, n))
-            spans.append((at // width, at % width, n))
-            start, count, at = start + n, count - n, at + n
-        where.append(spans)
-    first = [jnp.concatenate([first[p][:, s : s + n] for p, s, n in chunk], axis=1) for chunk in chunks]
+    all_other = Box(place(other, 2, all_other, True))
+    found = [(slab, (s, low, r)) for low, side in enumerate((rings, swapped)) for r in range(2) for s, slab in enumerate(side[r])]
+    amp = Box(place_slabs(found).reshape(size, size))
+    all_other = Box(place(other, 3, all_other, True))
 
     inter, got, sums, carried = {}, {}, {}, []
 
     def send_chunk(c):
-        pieces = (all_other, all_kept.value)
+        pieces = (all_other.value, all_kept.value)
+        width = widths[c]
         outs = (like((aux * width, size), BF), like((n_high, block, width), BF))
         if not carried:
-            extra = second.shape[0]
+            extra = second.value.shape[0]
             x, send, *terms = kernel_call(
                 functools.partial(first_send_part, chunks[c], width),
                 outs + (like((half_size, 2 * aux), BF),) * 2,
-                (ids, *pieces, amp.value, flat(all_other), second, first[c]),
+                (ids, *pieces, amp.value, flat(all_other.value), second.value, first[c].value),
                 scratch=[
                     pltpu.VMEM((aux * width + extra, size), BF),
                     pltpu.VMEM((extra, size), F32),
@@ -384,7 +427,7 @@
             x, send = kernel_call(
                 functools.partial(send_part, chunks[c], width),
                 outs,
-                (ids, *pieces, amp.value, flat(all_other), carried[0], first[c]),
+                (ids, *pieces, amp.value, flat(all_other.value), carried[0], first[c].value),
                 scratch=[pltpu.VMEM((aux * width, size), BF)],
                 name="send_part",
             )
@@ -392,19 +435,19 @@
         got[c] = Box(over_low(send))
 
     def keep_chunks(cs, direct=False):
-        n = len(cs)
-        wide = n * width
+        own_widths = tuple(widths[c] for c in cs)
+        wide = sum(own_widths)
         half = n_high // 2
         if direct:
             body, outs = keep_direct, (like((block, wide), F32),) + (like((block, wide), BF),) * (n_high - 1)
         else:
             body, outs = keep_halves, (like((half, block, wide), F32), like((half, block, wide), BF))
         own, *messages = kernel_call(
-            functools.partial(body, n, width),
+            functools.partial(body, own_widths),
             outs,
             (ids, flat(all_kept.value), carried[1])
             + tuple(inter[c].value for c in cs)
-            + tuple(first[c] for c in cs)
+            + tuple(first[c].value for c in cs)
             + tuple(got[c].value for c in cs),
             scratch=[pltpu.VMEM((n_high, block, wide), F32)],
             name="keep_part",
@@ -428,50 +471,74 @@
         return own, messages
 
     def sum_chunks(cs, own, messages):
-        shape = (block, len(cs) * width)
+        shape = (block, sum(widths[c] for c in cs))
         total = kernel_call(
             add_up,
             like(shape, F32),
             (ids, own.value.reshape(shape), *[m.value.reshape(shape) for m in messages]),
             name="add_up",
         )
-        for i, c in enumerate(cs):
-            sums[c] = total[:, i * width : (i + 1) * width]
-        return Box(total)
-
-    send_chunk(0)
-    tie(amp, inter[0])
-    send_chunk(1)
-    tie(amp, inter[1], kept[2], all_kept)
+        total = Box(total)
+        at = 0
+        for c in cs:
+            sums[c] = (total, at)
+            at += widths[c]
+        return total
+
+    stages = {}
+    last = amp
+
+    def send_step(c):
+        nonlocal last
+        if c:
+            tie(amp, last)
+        send_chunk(c)
+        last = inter[c]
+
+    def place_step(k):
+        nonlocal last, all_kept
+        tie(all_kept, last)
+        all_kept = Box(place(kept, k, all_kept, False))
+        last = all_kept
+
+    def keep_step(cs):
+        nonlocal last
+        tie(inter[cs[-1]], last)
+        stages[cs] = keep_chunks(cs, direct=cs == (3,))
+        last = stages[cs][0]
+
+    def add_step(cs):
+        nonlocal last
+        tie(stages[cs][0], last)
+        stages[cs] = add_stages(*stages[cs])
+        last = stages[cs][0]
+
+    def sum_step(cs):
+        nonlocal last
+        tie(stages[cs][0], last)
+        last = sum_chunks(cs, *stages[cs])
+
+    send_step(0)
+    send_step(1)
+    tie(last, got[0])
+    tie(kept[2], last)
     kept[3] = Box(over_col(kept[2].value, 1))
-    all_kept = Box(place(kept, all_kept.value, False))
-    tie(amp, all_kept)
-    send_chunk(2)
-    stage01 = keep_chunks((0, 1))
-    tie(amp, stage01[0])
-    send_chunk(3)
-    tie(amp, inter[3], got[2])
-    send_chunk(4)
-    tie(inter[4], stage01[1][0], all_kept)
-    stage01 = add_stages(*stage01)
-    tie(stage01[0], all_kept)
-    stage2 = keep_chunks((2,))
-    tie(stage2[0], all_kept)
-    stage3 = keep_chunks((3,))
-    tie(stage3[0], stage2[1][0])
-    stage2 = add_stages(*stage2)
-    tie(stage2[0], stage01[1][0])
-    total = sum_chunks((0, 1), *stage01)
-    tie(stage2[0], all_kept)
-    stage4 = keep_chunks((4,), direct=True)
-    tie(stage4[0], stage3[1][0])
-    stage3 = add_stages(*stage3)
-    sum_chunks((2,), *stage2)
-    sum_chunks((3,), *stage3)
-    sum_chunks((4,), *stage4)
+    place_step(2)
+    place_step(3)
+    send_step(2)
+    keep_step((0, 1))
+    send_step(3)
+    keep_step((2,))
+    add_step((0, 1))
+    add_step((2,))
+    keep_step((3,))
+    sum_step((0, 1))
+    sum_step((2,))
+    sum_step((3,))
     parts = []
     for (piece, _, _), spans in zip(order, where, strict=True):
-        part = jnp.concatenate([sums[c][:, s : s + n] for c, s, n in spans], axis=1)
+        spans = [(sums[c][0].value, sums[c][1] + s, n) for c, s, n in spans]
+        part = jnp.concatenate([total[:, s : s + n] for total, s, n in spans], axis=1)
         parts.append(over_col(part, piece) if piece else part)
     out = kernel_call(
         functools.partial(finish, order),

time: 155 us -> 141 us (0.910)
  waiting for transfers between devices: 35 us -> 49.5 us
  starting transfers between devices: 45.7 us -> 34.8 us
  local copies, waits for them, and re-layouts: 12.4 us -> 2.91 us
  Pallas kernels: 59.3 us -> 50.1 us
    pallas_call x23 -> x21, Pallas kernels: 59.3 us -> 50.1 us  [kernel_call(): pl.pallas_call(body, out_shape=outs, in_specs=[SMEM] + [VMEM] * (len(ins)...]
    unnamed x45 -> x8, local copies, waits for them, and re-layouts: 6.7 us -> 0.02 us
    ppermute x9 -> x7, waiting for transfers between devices: 7.42 us -> 13.7 us  [over_high(): lax.ppermute(x, 'row', [(i, (i // 2 ^ k) * 2 + i % 2) for i in range(n_ro...]
    ppermute x9 -> x7, starting transfers between devices: 14.1 us -> 7.92 us  [over_high(): lax.ppermute(x, 'row', [(i, (i // 2 ^ k) * 2 + i % 2) for i in range(n_ro...]
    ppermute x13 -> x12, starting transfers between devices: 16 us -> 10.7 us  [over_low(): return lax.ppermute(x, 'row', [(i, i ^ 1) for i in range(n_row)])]
    ppermute x13 -> x12, waiting for transfers between devices: 9.69 us -> 13.8 us  [over_low(): return lax.ppermute(x, 'row', [(i, i ^ 1) for i in range(n_row)])]
    ppermute x6, waiting for transfers between devices: 10.4 us -> 12.5 us  [up(): return lax.ppermute(x, 'row', [(i, (i + 2) % n_row) for i in range(n_row)])]
    ppermute x12, waiting for transfers between devices: 7.52 us -> 9.52 us  [over_col(): return lax.ppermute(x, 'col', [(i, i ^ k) for i in range(n_col)])]
  transfers between devices with their start and end apart: 40 -> 37, of which waited for: 17 -> 19; matrix products, arithmetic and copies ran while one was open for 4% -> 3% of each run, Pallas kernels for 38% -> 34%
where the time goes in v3:
time: 141 us; the launch traced here: 139 us
  Pallas kernels  50.1 us (36%)
  waiting for transfers between devices  49.5 us (35%)
  starting transfers between devices  34.8 us (25%)
  local copies, waits for them, and re-layouts  2.91 us (2%)
    pallas_call x21, Pallas kernels, kernel_call(): pl.pallas_call(body, out_shape=outs, in_specs=[SMEM] + [VMEM] * (len(ins)...  50.1 us
    ppermute x12, waiting for transfers between devices, over_low(): return lax.ppermute(x, 'row', [(i, i ^ 1) for i in range(n_row)])  13.8 us
    ppermute x7, waiting for transfers between devices, over_high(): lax.ppermute(x, 'row', [(i, (i // 2 ^ k) * 2 + i % 2) for i in range(n_ro...  13.7 us
    ppermute x6, waiting for transfers between devices, up(): return lax.ppermute(x, 'row', [(i, (i + 2) % n_row) for i in range(n_row)])  12.5 us
    ppermute x12, starting transfers between devices, over_low(): return lax.ppermute(x, 'row', [(i, i ^ 1) for i in range(n_row)])  10.7 us
    ppermute x12, waiting for transfers between devices, over_col(): return lax.ppermute(x, 'col', [(i, i ^ k) for i in range(n_col)])  9.52 us
    ppermute x12, starting transfers between devices, over_col(): return lax.ppermute(x, 'col', [(i, i ^ k) for i in range(n_col)])  8.29 us
    ppermute x7, starting transfers between devices, over_high(): lax.ppermute(x, 'row', [(i, (i // 2 ^ k) * 2 + i % 2) for i in range(n_ro...  7.92 us
  transfers between devices with their start and end apart: 37, of which 19 were waited for; matrix products, arithmetic and copies ran while one was open for 3% of the time, Pallas kernels for 34%

profile of v3, /device:TPU:0, one launch (start us, length us, event | category | flops | bytes accessed | tf_op | source)
XLA Modules:
  0.0 139.4 jit_solution(6774273467314486300)
XLA Ops:
  0.5 1.1 dynamic-slice_bitcast_fusion.2
  1.7 2.9 %collective-permute-start.2 = (bf16[40,1280]{1,0:T(8,128)(2,1)S(1)}, bf16[40,1280]{1,0:T(8,128)(2,1)S(1)}, u32[]{:S(2)}, u32[]{:S(2)}) collective-permute-start(bf16[40,1280]{1,0:T(8,128)(2,1)S(1)} %get-tuple-element.188), channel_id=1, source_target_pairs={{0,2},{1,3},{2,0},{3,1},{4,6},{5,7},{6,4},{7,5},{8,10},{9,11},{10,... | collective-permute-start | bytes 307208 | tf_op jit(solution)/shard_map/ppermute | solution.py:269
  6.3 1.0 half_slab.2
  7.2 1.4 dynamic-slice_bitcast_fusion
  8.6 1.8 %collective-permute-start.7 = (bf16[3,1,160,1280]{3,2,1,0:T(8,128)(2,1)S(1)}, bf16[3,1,160,1280]{3,2,1,0:T(8,128)(2,1)S(1)}, u32[]{:S(2)}, u32[]{:S(2)}) collective-permute-start(bf16[3,1,160,1280]{3,2,1,0:T(8,128)(2,1)S(1)} %dynamic-slice_bitcast_fusion), channel_id=1, source_target_pairs={{0,2},{1,3},{2,0},{3,1},{4,6},{5,7},{6,4},{7,5},{8,10},{9,11},{10,... | collective-permute-start | bytes 3686408 | tf_op jit(solution)/shard_map/ppermute | solution.py:269
  10.5 1.0 half_slab.3
  11.5 1.6 %collective-permute-start.4 = (bf16[80,1280]{1,0:T(8,128)(2,1)S(1)}, bf16[80,1280]{1,0:T(8,128)(2,1)S(1)}, u32[]{:S(2)}, u32[]{:S(2)}) collective-permute-start(bf16[80,1280]{1,0:T(8,128)(2,1)S(1)} %bitcast.60), channel_id=1, source_target_pairs={{0,8},{4,12},{8,16},{12,20},{16,24},{20,28},{24,0},{28,4},{1,9},{5... | collective-permute-start | bytes 614408 | tf_op jit(solution)/shard_map/ppermute | solution.py:278
  13.1 1.5 %collective-permute-start.13 = (bf16[80,1280]{1,0:T(8,128)(2,1)S(1)}, bf16[80,1280]{1,0:T(8,128)(2,1)S(1)}, u32[]{:S(2)}, u32[]{:S(2)}) collective-permute-start(bf16[80,1280]{1,0:T(8,128)(2,1)S(1)} %bitcast.61), channel_id=1, source_target_pairs={{0,4},{4,0},{8,12},{12,8},{16,20},{20,16},{24,28},{28,24},{1,5},{5... | collective-permute-start | bytes 614408 | tf_op jit(solution)/shard_map/ppermute | solution.py:272
  14.6 1.6 %collective-permute-start.5 = (bf16[80,1280]{1,0:T(8,128)(2,1)S(1)}, bf16[80,1280]{1,0:T(8,128)(2,1)S(1)}, u32[]{:S(2)}, u32[]{:S(2)}) collective-permute-start(bf16[80,1280]{1,0:T(8,128)(2,1)S(1)} %bitcast.57), channel_id=1, source_target_pairs={{0,8},{4,12},{8,16},{12,20},{16,24},{20,28},{24,0},{28,4},{1,9},{5... | collective-permute-start | bytes 614408 | tf_op jit(solution)/shard_map/ppermute | solution.py:278
  16.8 2.8 %place_pieces.1 = (bf16[3,4,160,1280]{3,2,1,0:T(8,128)(2,1)S(1)}, bf16[3,4,160,1280]{3,2,1,0:T(8,128)(2,1)S(1)}) custom-call(s32[4]{0:T(128)S(1)} %pad_add_fusion.ids, s32[20,20]{1,0:T(8,128)S(1)} %copy-done.2, bf16[3,1,2,160,1280]{4,3,2,1,0:T(8,128)(2,1)S(1)} %bitcast.55, bf16[3,1,2,160,1280]{4,3,2,1,0:T(8,128)(2,1)} %bitcast.11.refs_1_), custom_call_target="tpu_custom_call" | custom-call | tf_op jit(solution)/shard_map/place_pieces/pallas_call | solution.py:21
  19.6 1.6 %collective-permute-done.4.refs_5_ = bf16[80,1280]{1,0:T(8,128)(2,1)S(1)} collective-permute-done((bf16[80,1280]{1,0:T(8,128)(2,1)S(1)}, bf16[80,1280]{1,0:T(8,128)(2,1)S(1)}, u32[]{:S(2)}, u32[]{:S(2)}) %collective-permute-start.4) | collective-permute-done | bytes 204832 | tf_op jit(solution)/shard_map/ppermute | solution.py:278
  21.2 1.4 %collective-permute-start.14 = (bf16[80,1280]{1,0:T(8,128)(2,1)S(1)}, bf16[80,1280]{1,0:T(8,128)(2,1)S(1)}, u32[]{:S(2)}, u32[]{:S(2)}) collective-permute-start(bf16[80,1280]{1,0:T(8,128)(2,1)S(1)} %collective-permute-done.4.refs_5_), channel_id=1, source_target_pairs={{0,8},{4,12},{8,16},{12,20},{16,24},{20,28},{24,0},{28,4},{1,9},{5... | collective-permute-start | bytes 614408 | tf_op jit(solution)/shard_map/ppermute | solution.py:278
  22.6 1.5 %collective-permute-start.15 = (bf16[80,1280]{1,0:T(8,128)(2,1)S(1)}, bf16[80,1280]{1,0:T(8,128)(2,1)S(1)}, u32[]{:S(2)}, u32[]{:S(2)}) collective-permute-start(bf16[80,1280]{1,0:T(8,128)(2,1)S(1)} %collective-permute-done.4.refs_5_), channel_id=1, source_target_pairs={{0,4},{4,0},{8,12},{12,8},{16,20},{20,16},{24,28},{28,24},{1,5},{5... | collective-permute-start | bytes 614408 | tf_op jit(solution)/shard_map/ppermute | solution.py:272
  24.2 1.3 collective-permute-done.5.refs_1_
  25.5 1.6 %collective-permute-start.10 = (bf16[80,1280]{1,0:T(8,128)(2,1)S(1)}, bf16[80,1280]{1,0:T(8,128)(2,1)S(1)}, u32[]{:S(2)}, u32[]{:S(2)}) collective-permute-start(bf16[80,1280]{1,0:T(8,128)(2,1)S(1)} %collective-permute-done.5.refs_1_), channel_id=1, source_target_pairs={{0,4},{4,0},{8,12},{12,8},{16,20},{20,16},{24,28},{28,24},{1,5},{5... | collective-permute-start | bytes 614408 | tf_op jit(solution)/shard_map/ppermute | solution.py:272
  27.1 1.4 %collective-permute-start.9 = (bf16[80,1280]{1,0:T(8,128)(2,1)S(1)}, bf16[80,1280]{1,0:T(8,128)(2,1)S(1)}, u32[]{:S(2)}, u32[]{:S(2)}) collective-permute-start(bf16[80,1280]{1,0:T(8,128)(2,1)S(1)} %collective-permute-done.5.refs_1_), channel_id=1, source_target_pairs={{0,8},{4,12},{8,16},{12,20},{16,24},{20,28},{24,0},{28,4},{1,9},{5... | collective-permute-start | bytes 614408 | tf_op jit(solution)/shard_map/ppermute | solution.py:278
  29.3 1.1 collective-permute-done.15.refs_13_
  30.4 1.8 %collective-permute-start.16 = (bf16[80,1280]{1,0:T(8,128)(2,1)S(1)}, bf16[80,1280]{1,0:T(8,128)(2,1)S(1)}, u32[]{:S(2)}, u32[]{:S(2)}) collective-permute-start(bf16[80,1280]{1,0:T(8,128)(2,1)S(1)} %collective-permute-done.14.refs_6_), channel_id=1, source_target_pairs={{0,8},{4,12},{8,16},{12,20},{16,24},{20,28},{24,0},{28,4},{1,9},{5... | collective-permute-start | bytes 614408 | tf_op jit(solution)/shard_map/ppermute | solution.py:278
  32.2 1.5 %collective-permute-start.17 = (bf16[80,1280]{1,0:T(8,128)(2,1)S(1)}, bf16[80,1280]{1,0:T(8,128)(2,1)S(1)}, u32[]{:S(2)}, u32[]{:S(2)}) collective-permute-start(bf16[80,1280]{1,0:T(8,128)(2,1)S(1)} %collective-permute-done.14.refs_6_), channel_id=1, source_target_pairs={{0,4},{4,0},{8,12},{12,8},{16,20},{20,16},{24,28},{28,24},{1,5},{5... | collective-permute-start | bytes 614408 | tf_op jit(solution)/shard_map/ppermute | solution.py:272
  33.8 1.0 collective-permute-done.10.refs_9_
  34.8 2.1 %collective-permute-done.9.refs_2_ = bf16[80,1280]{1,0:T(8,128)(2,1)S(1)} collective-permute-done((bf16[80,1280]{1,0:T(8,128)(2,1)S(1)}, bf16[80,1280]{1,0:T(8,128)(2,1)S(1)}, u32[]{:S(2)}, u32[]{:S(2)}) %collective-permute-start.9) | collective-permute-done | bytes 204832 | tf_op jit(solution)/shard_map/ppermute | solution.py:278
  37.7 3.5 %collective-permute-done.16.refs_7_ = bf16[80,1280]{1,0:T(8,128)(2,1)S(1)} collective-permute-done((bf16[80,1280]{1,0:T(8,128)(2,1)S(1)}, bf16[80,1280]{1,0:T(8,128)(2,1)S(1)}, u32[]{:S(2)}, u32[]{:S(2)}) %collective-permute-start.16) | collective-permute-done | bytes 204832 | tf_op jit(solution)/shard_map/ppermute | solution.py:278
  41.1 3.3 %collective-permute-done.11.refs_3_ = bf16[80,1280]{1,0:T(8,128)(2,1)S(1)} collective-permute-done((bf16[80,1280]{1,0:T(8,128)(2,1)S(1)}, bf16[80,1280]{1,0:T(8,128)(2,1)S(1)}, u32[]{:S(2)}, u32[]{:S(2)}) %collective-permute-start.11) | collective-permute-done | bytes 204832 | tf_op jit(solution)/shard_map/ppermute | solution.py:278
  45.4 1.7 %collective-permute-start.19 = (bf16[80,1280]{1,0:T(8,128)(2,1)S(1)}, bf16[80,1280]{1,0:T(8,128)(2,1)S(1)}, u32[]{:S(2)}, u32[]{:S(2)}) collective-permute-start(bf16[80,1280]{1,0:T(8,128)(2,1)S(1)} %collective-permute-done.11.refs_3_), channel_id=1, source_target_pairs={{0,4},{4,0},{8,12},{12,8},{16,20},{20,16},{24,28},{28,24},{1,5},{5... | collective-permute-start | bytes 614408 | tf_op jit(solution)/shard_map/ppermute | solution.py:272
  48.0 5.0 %collective-permute-done.20.refs_15_ = bf16[80,1280]{1,0:T(8,128)(2,1)S(1)} collective-permute-done((bf16[80,1280]{1,0:T(8,128)(2,1)S(1)}, bf16[80,1280]{1,0:T(8,128)(2,1)S(1)}, u32[]{:S(2)}, u32[]{:S(2)}) %collective-permute-start.20) | collective-permute-done | bytes 204832 | tf_op jit(solution)/shard_map/ppermute | solution.py:272
  53.0 3.6 %collective-permute-done.19.refs_11_ = bf16[80,1280]{1,0:T(8,128)(2,1)S(1)} collective-permute-done((bf16[80,1280]{1,0:T(8,128)(2,1)S(1)}, bf16[80,1280]{1,0:T(8,128)(2,1)S(1)}, u32[]{:S(2)}, u32[]{:S(2)}) %collective-permute-start.19) | collective-permute-done | bytes 204832 | tf_op jit(solution)/shard_map/ppermute | solution.py:272
  57.4 0.9 place_halves.5.refs_0_
  58.3 5.3 %send_part.4 = (bf16[768,1280]{1,0:T(8,128)(2,1)S(1)}, bf16[4,160,256]{2,1,0:T(8,128)(2,1)S(1)}, bf16[640,6]{1,0:T(8,128)(2,1)S(1)}, bf16[640,6]{1,0:T(8,128)(2,1)S(1)}) custom-call(s32[4]{0:T(128)S(1)} %pad_add_fusion.ids, bf16[3,4,160,1280]{3,2,1,0:T(8,128)(2,1)S(1)} %place_halves.5.refs_0_, bf16[3,4,160,1280]{3,2,1,0:T(8,128)(2,1)S(1)} %get-tuple-element.140.refs_1_, ...), custom_call_target="tpu_custom_call" | custom-call | tf_op jit(solution)/shard_map/send_part/pallas_call | solution.py:21
  64.0 7.8 %send_part.5 = (bf16[1152,1280]{1,0:T(8,128)(2,1)S(1)}, bf16[4,160,384]{2,1,0:T(8,128)(2,1)S(1)}) custom-call(s32[4]{0:T(128)S(1)} %pad_add_fusion.ids, bf16[3,4,160,1280]{3,2,1,0:T(8,128)(2,1)S(1)} %place_halves.5.refs_0_, bf16[3,4,160,1280]{3,2,1,0:T(8,128)(2,1)S(1)} %get-tuple-element.140.refs_1_, bf16[1280,1280]{1,0:T(8,128)(2,1)S(1)} %bitcast.51, ...), custom_call_target="tpu_custom_call" | custom-call | tf_op jit(solution)/shard_map/send_part/pallas_call | solution.py:21
  72.6 1.2 collective-permute-done.6.refs_0_
  73.9 0.9 place_halves.6.refs_1_
  74.8 1.9 %collective-permute-done.22.refs_0_ = bf16[3,1,160,1280]{3,2,1,0:T(8,128)(2,1)S(1)} collective-permute-done((bf16[3,1,160,1280]{3,2,1,0:T(8,128)(2,1)S(1)}, bf16[3,1,160,1280]{3,2,1,0:T(8,128)(2,1)S(1)}, u32[]{:S(2)}, u32[]{:S(2)}) %collective-permute-start.22) | collective-permute-done | bytes 1228832 | tf_op jit(solution)/shard_map/ppermute | solution.py:269
  76.8 0.9 place_halves.7.refs_1_
  77.7 7.6 %send_part.6 = (bf16[1152,1280]{1,0:T(8,128)(2,1)S(1)}, bf16[4,160,384]{2,1,0:T(8,128)(2,1)S(1)}) custom-call(s32[4]{0:T(128)S(1)} %pad_add_fusion.ids, bf16[3,4,160,1280]{3,2,1,0:T(8,128)(2,1)S(1)} %place_halves.5.refs_0_, bf16[3,4,160,1280]{3,2,1,0:T(8,128)(2,1)S(1)} %place_halves.7.refs_1_, bf16[1280,1280]{1,0:T(8,128)(2,1)S(1)} %bitcast.52, ...), custom_call_target="tpu_custom_call" | custom-call | tf_op jit(solution)/shard_map/send_part/pallas_call | solution.py:21
  85.4 2.1 %collective-permute-done.23.refs_7_ = bf16[4,160,384]{2,1,0:T(8,128)(2,1)S(1)} collective-permute-done((bf16[4,160,384]{2,1,0:T(8,128)(2,1)S(1)}, bf16[4,160,384]{2,1,0:T(8,128)(2,1)S(1)}, u32[]{:S(2)}, u32[]{:S(2)}) %collective-permute-start.23) | collective-permute-done | bytes 491552 | tf_op jit(solution)/shard_map/ppermute | solution.py:272
  87.5 5.0 %keep_part.3 = (f32[2,160,640]{2,1,0:T(8,128)S(1)}, bf16[2,160,640]{2,1,0:T(8,128)(2,1)S(1)}) custom-call(s32[4]{0:T(128)S(1)} %pad_add_fusion.ids, bf16[3,640,1280]{2,1,0:T(8,128)(2,1)S(1)} %bitcast.47, bf16[640,6]{1,0:T(8,128)(2,1)S(1)} %get-tuple-element.146.refs_1_, bf16[768,1280]{1,0:T(8,128)(2,1)S(1)} %get-tuple-element.147.refs_2_, ...), custom_call_target="tpu_custom_call" | custom-call | tf_op jit(solution)/shard_map/keep_part/pallas_call | solution.py:21
  92.6 5.1 %send_part.7 = (bf16[768,1280]{1,0:T(8,128)(2,1)S(1)}, bf16[4,160,256]{2,1,0:T(8,128)(2,1)S(1)}) custom-call(s32[4]{0:T(128)S(1)} %pad_add_fusion.ids, bf16[3,4,160,1280]{3,2,1,0:T(8,128)(2,1)S(1)} %place_halves.5.refs_0_, bf16[3,4,160,1280]{3,2,1,0:T(8,128)(2,1)S(1)} %place_halves.7.refs_1_, bf16[1280,1280]{1,0:T(8,128)(2,1)S(1)} %bitcast.53, ...), custom_call_target="tpu_custom_call" | custom-call | tf_op jit(solution)/shard_map/send_part/pallas_call | solution.py:21
  98.6 3.5 %keep_part.4 = (f32[2,160,384]{2,1,0:T(8,128)S(1)}, bf16[2,160,384]{2,1,0:T(8,128)(2,1)S(1)}) custom-call(s32[4]{0:T(128)S(1)} %pad_add_fusion.ids, bf16[3,640,1280]{2,1,0:T(8,128)(2,1)S(1)} %bitcast.48, bf16[640,6]{1,0:T(8,128)(2,1)S(1)} %get-tuple-element.146.refs_1_, bf16[1152,1280]{1,0:T(8,128)(2,1)S(1)} %get-tuple-element.157.refs_2_, ...), custom_call_target="tpu_custom_call" | custom-call | tf_op jit(solution)/shard_map/keep_part/pallas_call | solution.py:21
  102.1 1.5 %collective-permute-start.26 = (bf16[2,160,384]{2,1,0:T(8,128)(2,1)S(1)}, bf16[2,160,384]{2,1,0:T(8,128)(2,1)S(1)}, u32[]{:S(2)}, u32[]{:S(2)}) collective-permute-start(bf16[2,160,384]{2,1,0:T(8,128)(2,1)S(1)} %get-tuple-element.165), channel_id=1, source_target_pairs={{0,8},{4,12},{8,0},{12,4},{16,24},{20,28},{24,16},{28,20},{1,9},{5... | collective-permute-start | bytes 737288 | tf_op jit(solution)/shard_map/ppermute | solution.py:275
  104.3 1.4 collective-permute-start.28
  105.7 7.6 %collective-permute-done.26.got = bf16[2,160,384]{2,1,0:T(8,128)(2,1)S(1)} collective-permute-done((bf16[2,160,384]{2,1,0:T(8,128)(2,1)S(1)}, bf16[2,160,384]{2,1,0:T(8,128)(2,1)S(1)}, u32[]{:S(2)}, u32[]{:S(2)}) %collective-permute-start.26) | collective-permute-done | bytes 245792 | tf_op jit(solution)/shard_map/ppermute | solution.py:275
  113.9 2.1 %keep_part.5 = (f32[160,256]{1,0:T(8,128)S(1)}, bf16[160,256]{1,0:T(8,128)(2,1)S(1)}, bf16[160,256]{1,0:T(8,128)(2,1)S(1)}, bf16[160,256]{1,0:T(8,128)(2,1)S(1)}) custom-call(s32[4]{0:T(128)S(1)} %pad_add_fusion.ids, bf16[3,640,1280]{2,1,0:T(8,128)(2,1)S(1)} %bitcast.49, bf16[640,6]{1,0:T(8,128)(2,1)S(1)} %get-tuple-element.146.refs_1_, ...), custom_call_target="tpu_custom_call" | custom-call | tf_op jit(solution)/shard_map/keep_part/pallas_call | solution.py:21
  116.9 2.3 %collective-permute-start.33 = (bf16[160,256]{1,0:T(8,128)(2,1)S(1)}, bf16[160,256]{1,0:T(8,128)(2,1)S(1)}, u32[]{:S(2)}, u32[]{:S(2)}) collective-permute-start(bf16[160,256]{1,0:T(8,128)(2,1)S(1)} %get-tuple-element.180), channel_id=1, source_target_pairs={{0,8},{4,12},{8,0},{12,4},{16,24},{20,28},{24,16},{28,20},{1,9},{5... | collective-permute-start | bytes 245768 | tf_op jit(solution)/shard_map/ppermute | solution.py:275
  119.6 1.9 %collective-permute-start.35 = (bf16[160,256]{1,0:T(8,128)(2,1)S(1)}, bf16[160,256]{1,0:T(8,128)(2,1)S(1)}, u32[]{:S(2)}, u32[]{:S(2)}) collective-permute-start(bf16[160,256]{1,0:T(8,128)(2,1)S(1)} %get-tuple-element.182), channel_id=1, source_target_pairs={{0,24},{4,28},{8,16},{12,20},{16,8},{20,12},{24,0},{28,4},{1,25},{... | collective-permute-start | bytes 245768 | tf_op jit(solution)/shard_map/ppermute | solution.py:275
  121.8 5.9 %collective-permute-done.30 = bf16[1,160,384]{2,1,0:T(8,128)(2,1)S(1)} collective-permute-done((bf16[1,160,384]{2,1,0:T(8,128)(2,1)S(1)}, bf16[1,160,384]{2,1,0:T(8,128)(2,1)S(1)}, u32[]{:S(2)}, u32[]{:S(2)}) %collective-permute-start.30) | collective-permute-done | bytes 122912 | tf_op jit(solution)/shard_map/ppermute | solution.py:275
  129.5 1.8 %collective-permute-start.32 = (f32[160,64]{1,0:T(8,128)S(1)}, f32[160,64]{1,0:T(8,128)S(1)}, u32[]{:S(2)}, u32[]{:S(2)}) collective-permute-start(f32[160,64]{1,0:T(8,128)S(1)} %slice.38), channel_id=1, source_target_pairs={{0,3},{1,2},{2,1},{3,0},{4,7},{5,6},{6,5},{7,4},{8,11},{9,10},{10,... | collective-permute-start | bytes 122888 | tf_op jit(solution)/shard_map/ppermute | solution.py:269
  131.3 6.3 %collective-permute-done.32.refs_3_ = f32[160,64]{1,0:T(8,128)S(1)} collective-permute-done((f32[160,64]{1,0:T(8,128)S(1)}, f32[160,64]{1,0:T(8,128)S(1)}, u32[]{:S(2)}, u32[]{:S(2)}) %collective-permute-start.32) | collective-permute-done | bytes 40992 | tf_op jit(solution)/shard_map/ppermute | solution.py:269
  137.7 1.5 %finish.1 = f32[4,160,320]{2,1,0:T(8,128)} custom-call(s32[4]{0:T(128)S(1)} %pad_add_fusion.ids, f32[160,320]{1,0:T(8,128)S(1)} %collective-permute-done.29.refs_0_, f32[160,320]{1,0:T(8,128)S(1)} %get-tuple-element.183.refs_1_, f32[160,320]{1,0:T(8,128)S(1)} %collective-permute-done.31.refs_2_, f32[160,64]{1,0:T(8,128)S(1)} %collective-permute-done.32.refs_3_, ...), custom_call_target="tpu_custom_call" | custom-call | tf_op jit(solution)/shard_map/finish/pallas_call | solution.py:21
  (76 shorter events, 14.2 us)
Async XLA Ops:
  0.0 5.4 %copy-start = (bf16[3,160,1280]{2,1,0:T(8,128)(2,1)S(1)}, bf16[3,160,1280]{2,1,0:T(8,128)(2,1)}, u32[]{:S(2)}) copy-start(bf16[3,160,1280]{2,1,0:T(8,128)(2,1)} %param.8) | copy-start | bytes 3686404
  0.0 6.1 %copy-start.3 = (s32[4,20,20]{2,0,1:T(4,128)S(1)}, s32[4,20,20]{2,0,1:T(4,128)}, u32[]{:S(2)}) copy-start(s32[4,20,20]{2,0,1:T(4,128)} %param.10) | copy-start | bytes 19204
  0.0 6.2 %collective-permute-start = (bf16[3,320,1280]{2,1,0:T(8,128)(2,1)}, bf16[3,320,1280]{2,1,0:T(8,128)(2,1)}, u32[]{:S(2)}, u32[]{:S(2)}) collective-permute-start(bf16[3,320,1280]{2,1,0:T(8,128)(2,1)} %param.7), channel_id=1, source_target_pairs={{0,1},{1,0},{2,3},{3,2},{4,5},{5,4},{6,7},{7,6},{8,9},{9,8},{10,11... | collective-permute-start | bytes 7372808 | tf_op jit(solution)/shard_map/ppermute | solution.py:269
  1.5 4.7 %collective-permute-start.1 = (bf16[40,1280]{1,0:T(8,128)(2,1)S(1)}, bf16[40,1280]{1,0:T(8,128)(2,1)S(1)}, u32[]{:S(2)}, u32[]{:S(2)}) collective-permute-start(bf16[40,1280]{1,0:T(8,128)(2,1)S(1)} %get-tuple-element.187), channel_id=1, source_target_pairs={{0,1},{1,0},{2,3},{3,2},{4,5},{5,4},{6,7},{7,6},{8,9},{9,8},{10,11... | collective-permute-start | bytes 307208 | tf_op jit(solution)/shard_map/ppermute | solution.py:269
  1.7 8.7 %collective-permute-start.2 = (bf16[40,1280]{1,0:T(8,128)(2,1)S(1)}, bf16[40,1280]{1,0:T(8,128)(2,1)S(1)}, u32[]{:S(2)}, u32[]{:S(2)}) collective-permute-start(bf16[40,1280]{1,0:T(8,128)(2,1)S(1)} %get-tuple-element.188), channel_id=1, source_target_pairs={{0,2},{1,3},{2,0},{3,1},{4,6},{5,7},{6,4},{7,5},{8,10},{9,11},{10,... | collective-permute-start | bytes 307208 | tf_op jit(solution)/shard_map/ppermute | solution.py:269
  4.6 5.9 %collective-permute-start.3 = (bf16[40,1280]{1,0:T(8,128)(2,1)S(1)}, bf16[40,1280]{1,0:T(8,128)(2,1)S(1)}, u32[]{:S(2)}, u32[]{:S(2)}) collective-permute-start(bf16[40,1280]{1,0:T(8,128)(2,1)S(1)} %get-tuple-element.185), channel_id=1, source_target_pairs={{0,3},{1,2},{2,1},{3,0},{4,7},{5,6},{6,5},{7,4},{8,11},{9,10},{10,... | collective-permute-start | bytes 307208 | tf_op jit(solution)/shard_map/ppermute | solution.py:269
  5.7 11.1 %copy-start.2 = (s32[20,20]{1,0:T(8,128)S(1)}, s32[20,20]{1,0:T(8,128)}, u32[]{:S(2)}) copy-start(s32[20,20]{1,0:T(8,128)} %tiles.9) | copy-start | bytes 4804
  5.9 10.9 %copy-start.1 = (bf16[3,320,1280]{2,1,0:T(8,128)(2,1)S(1)}, bf16[3,320,1280]{2,1,0:T(8,128)(2,1)}, u32[]{:S(2)}) copy-start(bf16[3,320,1280]{2,1,0:T(8,128)(2,1)} %param.7) | copy-start | bytes 7372804
  8.6 35.8 %collective-permute-start.7 = (bf16[3,1,160,1280]{3,2,1,0:T(8,128)(2,1)S(1)}, bf16[3,1,160,1280]{3,2,1,0:T(8,128)(2,1)S(1)}, u32[]{:S(2)}, u32[]{:S(2)}) collective-permute-start(bf16[3,1,160,1280]{3,2,1,0:T(8,128)(2,1)S(1)} %dynamic-slice_bitcast_fusion), channel_id=1, source_target_pairs={{0,2},{1,3},{2,0},{3,1},{4,6},{5,7},{6,4},{7,5},{8,10},{9,11},{10,... | collective-permute-start | bytes 3686408 | tf_op jit(solution)/shard_map/ppermute | solution.py:269
  11.5 9.8 %collective-permute-start.4 = (bf16[80,1280]{1,0:T(8,128)(2,1)S(1)}, bf16[80,1280]{1,0:T(8,128)(2,1)S(1)}, u32[]{:S(2)}, u32[]{:S(2)}) collective-permute-start(bf16[80,1280]{1,0:T(8,128)(2,1)S(1)} %bitcast.60), channel_id=1, source_target_pairs={{0,8},{4,12},{8,16},{12,20},{16,24},{20,28},{24,0},{28,4},{1,9},{5... | collective-permute-start | bytes 614408 | tf_op jit(solution)/shard_map/ppermute | solution.py:278
  13.1 8.1 %collective-permute-start.13 = (bf16[80,1280]{1,0:T(8,128)(2,1)S(1)}, bf16[80,1280]{1,0:T(8,128)(2,1)S(1)}, u32[]{:S(2)}, u32[]{:S(2)}) collective-permute-start(bf16[80,1280]{1,0:T(8,128)(2,1)S(1)} %bitcast.61), channel_id=1, source_target_pairs={{0,4},{4,0},{8,12},{12,8},{16,20},{20,16},{24,28},{28,24},{1,5},{5... | collective-permute-start | bytes 614408 | tf_op jit(solution)/shard_map/ppermute | solution.py:272
  14.6 10.8 %collective-permute-start.5 = (bf16[80,1280]{1,0:T(8,128)(2,1)S(1)}, bf16[80,1280]{1,0:T(8,128)(2,1)S(1)}, u32[]{:S(2)}, u32[]{:S(2)}) collective-permute-start(bf16[80,1280]{1,0:T(8,128)(2,1)S(1)} %bitcast.57), channel_id=1, source_target_pairs={{0,8},{4,12},{8,16},{12,20},{16,24},{20,28},{24,0},{28,4},{1,9},{5... | collective-permute-start | bytes 614408 | tf_op jit(solution)/shard_map/ppermute | solution.py:278
  16.3 9.2 %collective-permute-start.8 = (bf16[80,1280]{1,0:T(8,128)(2,1)S(1)}, bf16[80,1280]{1,0:T(8,128)(2,1)S(1)}, u32[]{:S(2)}, u32[]{:S(2)}) collective-permute-start(bf16[80,1280]{1,0:T(8,128)(2,1)S(1)} %bitcast.58), channel_id=1, source_target_pairs={{0,4},{4,0},{8,12},{12,8},{16,20},{20,16},{24,28},{28,24},{1,5},{5... | collective-permute-start | bytes 614408 | tf_op jit(solution)/shard_map/ppermute | solution.py:272
  21.2 8.1 %collective-permute-start.14 = (bf16[80,1280]{1,0:T(8,128)(2,1)S(1)}, bf16[80,1280]{1,0:T(8,128)(2,1)S(1)}, u32[]{:S(2)}, u32[]{:S(2)}) collective-permute-start(bf16[80,1280]{1,0:T(8,128)(2,1)S(1)} %collective-permute-done.4.refs_5_), channel_id=1, source_target_pairs={{0,8},{4,12},{8,16},{12,20},{16,24},{20,28},{24,0},{28,4},{1,9},{5... | collective-permute-start | bytes 614408 | tf_op jit(solution)/shard_map/ppermute | solution.py:278
  22.6 7.8 %collective-permute-start.15 = (bf16[80,1280]{1,0:T(8,128)(2,1)S(1)}, bf16[80,1280]{1,0:T(8,128)(2,1)S(1)}, u32[]{:S(2)}, u32[]{:S(2)}) collective-permute-start(bf16[80,1280]{1,0:T(8,128)(2,1)S(1)} %collective-permute-done.4.refs_5_), channel_id=1, source_target_pairs={{0,4},{4,0},{8,12},{12,8},{16,20},{20,16},{24,28},{28,24},{1,5},{5... | collective-permute-start | bytes 614408 | tf_op jit(solution)/shard_map/ppermute | solution.py:272
  25.5 9.3 %collective-permute-start.10 = (bf16[80,1280]{1,0:T(8,128)(2,1)S(1)}, bf16[80,1280]{1,0:T(8,128)(2,1)S(1)}, u32[]{:S(2)}, u32[]{:S(2)}) collective-permute-start(bf16[80,1280]{1,0:T(8,128)(2,1)S(1)} %collective-permute-done.5.refs_1_), channel_id=1, source_target_pairs={{0,4},{4,0},{8,12},{12,8},{16,20},{20,16},{24,28},{28,24},{1,5},{5... | collective-permute-start | bytes 614408 | tf_op jit(solution)/shard_map/ppermute | solution.py:272
  27.1 9.7 %collective-permute-start.9 = (bf16[80,1280]{1,0:T(8,128)(2,1)S(1)}, bf16[80,1280]{1,0:T(8,128)(2,1)S(1)}, u32[]{:S(2)}, u32[]{:S(2)}) collective-permute-start(bf16[80,1280]{1,0:T(8,128)(2,1)S(1)} %collective-permute-done.5.refs_1_), channel_id=1, source_target_pairs={{0,8},{4,12},{8,16},{12,20},{16,24},{20,28},{24,0},{28,4},{1,9},{5... | collective-permute-start | bytes 614408 | tf_op jit(solution)/shard_map/ppermute | solution.py:278
  30.4 10.7 %collective-permute-start.16 = (bf16[80,1280]{1,0:T(8,128)(2,1)S(1)}, bf16[80,1280]{1,0:T(8,128)(2,1)S(1)}, u32[]{:S(2)}, u32[]{:S(2)}) collective-permute-start(bf16[80,1280]{1,0:T(8,128)(2,1)S(1)} %collective-permute-done.14.refs_6_), channel_id=1, source_target_pairs={{0,8},{4,12},{8,16},{12,20},{16,24},{20,28},{24,0},{28,4},{1,9},{5... | collective-permute-start | bytes 614408 | tf_op jit(solution)/shard_map/ppermute | solution.py:278
  32.2 8.9 %collective-permute-start.17 = (bf16[80,1280]{1,0:T(8,128)(2,1)S(1)}, bf16[80,1280]{1,0:T(8,128)(2,1)S(1)}, u32[]{:S(2)}, u32[]{:S(2)}) collective-permute-start(bf16[80,1280]{1,0:T(8,128)(2,1)S(1)} %collective-permute-done.14.refs_6_), channel_id=1, source_target_pairs={{0,4},{4,0},{8,12},{12,8},{16,20},{20,16},{24,28},{28,24},{1,5},{5... | collective-permute-start | bytes 614408 | tf_op jit(solution)/shard_map/ppermute | solution.py:272
  36.9 7.6 %collective-permute-start.11 = (bf16[80,1280]{1,0:T(8,128)(2,1)S(1)}, bf16[80,1280]{1,0:T(8,128)(2,1)S(1)}, u32[]{:S(2)}, u32[]{:S(2)}) collective-permute-start(bf16[80,1280]{1,0:T(8,128)(2,1)S(1)} %collective-permute-done.9.refs_2_), channel_id=1, source_target_pairs={{0,8},{4,12},{8,16},{12,20},{16,24},{20,28},{24,0},{28,4},{1,9},{5... | collective-permute-start | bytes 614408 | tf_op jit(solution)/shard_map/ppermute | solution.py:278
  36.9 7.6 %collective-permute-start.12 = (bf16[80,1280]{1,0:T(8,128)(2,1)S(1)}, bf16[80,1280]{1,0:T(8,128)(2,1)S(1)}, u32[]{:S(2)}, u32[]{:S(2)}) collective-permute-start(bf16[80,1280]{1,0:T(8,128)(2,1)S(1)} %collective-permute-done.9.refs_2_), channel_id=1, source_target_pairs={{0,4},{4,0},{8,12},{12,8},{16,20},{20,16},{24,28},{28,24},{1,5},{5... | collective-permute-start | bytes 614408 | tf_op jit(solution)/shard_map/ppermute | solution.py:272
  44.4 13.0 %collective-permute-start.18 = (bf16[3,1,160,1280]{3,2,1,0:T(8,128)(2,1)S(1)}, bf16[3,1,160,1280]{3,2,1,0:T(8,128)(2,1)S(1)}, u32[]{:S(2)}, u32[]{:S(2)}) collective-permute-start(bf16[3,1,160,1280]{3,2,1,0:T(8,128)(2,1)S(1)} %collective-permute-done.7.refs_0_), channel_id=1, source_target_pairs={{0,1},{1,0},{2,3},{3,2},{4,5},{5,4},{6,7},{7,6},{8,9},{9,8},{10,11... | collective-permute-start | bytes 3686408 | tf_op jit(solution)/shard_map/ppermute | solution.py:269
  44.4 29.4 %collective-permute-start.6 = (bf16[3,1,160,1280]{3,2,1,0:T(8,128)(2,1)S(1)}, bf16[3,1,160,1280]{3,2,1,0:T(8,128)(2,1)S(1)}, u32[]{:S(2)}, u32[]{:S(2)}) collective-permute-start(bf16[3,1,160,1280]{3,2,1,0:T(8,128)(2,1)S(1)} %dynamic-slice_bitcast_fusion.1), channel_id=1, source_target_pairs={{0,2},{1,3},{2,0},{3,1},{4,6},{5,7},{6,4},{7,5},{8,10},{9,11},{10,... | collective-permute-start | bytes 3686408 | tf_op jit(solution)/shard_map/ppermute | solution.py:269
  45.1 7.9 %collective-permute-start.20 = (bf16[80,1280]{1,0:T(8,128)(2,1)S(1)}, bf16[80,1280]{1,0:T(8,128)(2,1)S(1)}, u32[]{:S(2)}, u32[]{:S(2)}) collective-permute-start(bf16[80,1280]{1,0:T(8,128)(2,1)S(1)} %collective-permute-done.16.refs_7_), channel_id=1, source_target_pairs={{0,4},{4,0},{8,12},{12,8},{16,20},{20,16},{24,28},{28,24},{1,5},{5... | collective-permute-start | bytes 614408 | tf_op jit(solution)/shard_map/ppermute | solution.py:272
  45.4 11.2 %collective-permute-start.19 = (bf16[80,1280]{1,0:T(8,128)(2,1)S(1)}, bf16[80,1280]{1,0:T(8,128)(2,1)S(1)}, u32[]{:S(2)}, u32[]{:S(2)}) collective-permute-start(bf16[80,1280]{1,0:T(8,128)(2,1)S(1)} %collective-permute-done.11.refs_3_), channel_id=1, source_target_pairs={{0,4},{4,0},{8,12},{12,8},{16,20},{20,16},{24,28},{28,24},{1,5},{5... | collective-permute-start | bytes 614408 | tf_op jit(solution)/shard_map/ppermute | solution.py:272
  63.6 9.0 %collective-permute-start.21 = (bf16[4,160,256]{2,1,0:T(8,128)(2,1)S(1)}, bf16[4,160,256]{2,1,0:T(8,128)(2,1)S(1)}, u32[]{:S(2)}, u32[]{:S(2)}) collective-permute-start(bf16[4,160,256]{2,1,0:T(8,128)(2,1)S(1)} %get-tuple-element.135), channel_id=1, source_target_pairs={{0,4},{4,0},{8,12},{12,8},{16,20},{20,16},{24,28},{28,24},{1,5},{5... | collective-permute-start | bytes 983048 | tf_op jit(solution)/shard_map/ppermute | solution.py:272
  73.9 2.9 %collective-permute-start.22 = (bf16[3,1,160,1280]{3,2,1,0:T(8,128)(2,1)S(1)}, bf16[3,1,160,1280]{3,2,1,0:T(8,128)(2,1)S(1)}, u32[]{:S(2)}, u32[]{:S(2)}) collective-permute-start(bf16[3,1,160,1280]{3,2,1,0:T(8,128)(2,1)S(1)} %collective-permute-done.6.refs_0_), channel_id=1, source_target_pairs={{0,1},{1,0},{2,3},{3,2},{4,5},{5,4},{6,7},{7,6},{8,9},{9,8},{10,11... | collective-permute-start | bytes 3686408 | tf_op jit(solution)/shard_map/ppermute | solution.py:269
  73.9 13.6 %collective-permute-start.23 = (bf16[4,160,384]{2,1,0:T(8,128)(2,1)S(1)}, bf16[4,160,384]{2,1,0:T(8,128)(2,1)S(1)}, u32[]{:S(2)}, u32[]{:S(2)}) collective-permute-start(bf16[4,160,384]{2,1,0:T(8,128)(2,1)S(1)} %get-tuple-element.150), channel_id=1, source_target_pairs={{0,4},{4,0},{8,12},{12,8},{16,20},{20,16},{24,28},{28,24},{1,5},{5... | collective-permute-start | bytes 1474568 | tf_op jit(solution)/shard_map/ppermute | solution.py:272
  85.3 13.3 %collective-permute-start.24 = (bf16[4,160,384]{2,1,0:T(8,128)(2,1)S(1)}, bf16[4,160,384]{2,1,0:T(8,128)(2,1)S(1)}, u32[]{:S(2)}, u32[]{:S(2)}) collective-permute-start(bf16[4,160,384]{2,1,0:T(8,128)(2,1)S(1)} %get-tuple-element.158), channel_id=1, source_target_pairs={{0,4},{4,0},{8,12},{12,8},{16,20},{20,16},{24,28},{28,24},{1,5},{5... | collective-permute-start | bytes 1474568 | tf_op jit(solution)/shard_map/ppermute | solution.py:272
  92.5 11.2 %collective-permute-start.25 = (bf16[2,160,640]{2,1,0:T(8,128)(2,1)S(1)}, bf16[2,160,640]{2,1,0:T(8,128)(2,1)S(1)}, u32[]{:S(2)}, u32[]{:S(2)}) collective-permute-start(bf16[2,160,640]{2,1,0:T(8,128)(2,1)S(1)} %get-tuple-element.162), channel_id=1, source_target_pairs={{0,8},{4,12},{8,0},{12,4},{16,24},{20,28},{24,16},{28,20},{1,9},{5... | collective-permute-start | bytes 1228808 | tf_op jit(solution)/shard_map/ppermute | solution.py:275
  97.8 16.1 %collective-permute-start.27 = (bf16[4,160,256]{2,1,0:T(8,128)(2,1)S(1)}, bf16[4,160,256]{2,1,0:T(8,128)(2,1)S(1)}, u32[]{:S(2)}, u32[]{:S(2)}) collective-permute-start(bf16[4,160,256]{2,1,0:T(8,128)(2,1)S(1)} %get-tuple-element.170), channel_id=1, source_target_pairs={{0,4},{4,0},{8,12},{12,8},{16,20},{20,16},{24,28},{28,24},{1,5},{5... | collective-permute-start | bytes 983048 | tf_op jit(solution)/shard_map/ppermute | solution.py:272
  102.1 11.2 %collective-permute-start.26 = (bf16[2,160,384]{2,1,0:T(8,128)(2,1)S(1)}, bf16[2,160,384]{2,1,0:T(8,128)(2,1)S(1)}, u32[]{:S(2)}, u32[]{:S(2)}) collective-permute-start(bf16[2,160,384]{2,1,0:T(8,128)(2,1)S(1)} %get-tuple-element.165), channel_id=1, source_target_pairs={{0,8},{4,12},{8,0},{12,4},{16,24},{20,28},{24,16},{28,20},{1,9},{5... | collective-permute-start | bytes 737288 | tf_op jit(solution)/shard_map/ppermute | solution.py:275
  104.3 11.7 %collective-permute-start.28 = (bf16[1,160,640]{2,1,0:T(8,128)(2,1)S(1)}, bf16[1,160,640]{2,1,0:T(8,128)(2,1)S(1)}, u32[]{:S(2)}, u32[]{:S(2)}) collective-permute-start(bf16[1,160,640]{2,1,0:T(8,128)(2,1)S(1)} %get-tuple-element.173), channel_id=1, source_target_pairs={{0,16},{4,20},{8,24},{12,28},{16,0},{20,4},{24,8},{28,12},{1,17},{... | collective-permute-start | bytes 614408 | tf_op jit(solution)/shard_map/ppermute | solution.py:275
  116.6 11.0 %collective-permute-start.30 = (bf16[1,160,384]{2,1,0:T(8,128)(2,1)S(1)}, bf16[1,160,384]{2,1,0:T(8,128)(2,1)S(1)}, u32[]{:S(2)}, u32[]{:S(2)}) collective-permute-start(bf16[1,160,384]{2,1,0:T(8,128)(2,1)S(1)} %get-tuple-element.177), channel_id=1, source_target_pairs={{0,16},{4,20},{8,24},{12,28},{16,0},{20,4},{24,8},{28,12},{1,17},{... | collective-permute-start | bytes 368648 | tf_op jit(solution)/shard_map/ppermute | solution.py:275
  116.9 11.8 %collective-permute-start.33 = (bf16[160,256]{1,0:T(8,128)(2,1)S(1)}, bf16[160,256]{1,0:T(8,128)(2,1)S(1)}, u32[]{:S(2)}, u32[]{:S(2)}) collective-permute-start(bf16[160,256]{1,0:T(8,128)(2,1)S(1)} %get-tuple-element.180), channel_id=1, source_target_pairs={{0,8},{4,12},{8,0},{12,4},{16,24},{20,28},{24,16},{28,20},{1,9},{5... | collective-permute-start | bytes 245768 | tf_op jit(solution)/shard_map/ppermute | solution.py:275
  119.2 9.6 %collective-permute-start.34 = (bf16[160,256]{1,0:T(8,128)(2,1)S(1)}, bf16[160,256]{1,0:T(8,128)(2,1)S(1)}, u32[]{:S(2)}, u32[]{:S(2)}) collective-permute-start(bf16[160,256]{1,0:T(8,128)(2,1)S(1)} %get-tuple-element.181), channel_id=1, source_target_pairs={{0,16},{4,20},{8,24},{12,28},{16,0},{20,4},{24,8},{28,12},{1,17},{... | collective-permute-start | bytes 245768 | tf_op jit(solution)/shard_map/ppermute | solution.py:275
  119.6 9.2 %collective-permute-start.35 = (bf16[160,256]{1,0:T(8,128)(2,1)S(1)}, bf16[160,256]{1,0:T(8,128)(2,1)S(1)}, u32[]{:S(2)}, u32[]{:S(2)}) collective-permute-start(bf16[160,256]{1,0:T(8,128)(2,1)S(1)} %get-tuple-element.182), channel_id=1, source_target_pairs={{0,24},{4,28},{8,16},{12,20},{16,8},{20,12},{24,0},{28,4},{1,25},{... | collective-permute-start | bytes 245768 | tf_op jit(solution)/shard_map/ppermute | solution.py:275
  121.7 16.0 %collective-permute-start.29 = (f32[160,320]{1,0:T(8,128)S(1)}, f32[160,320]{1,0:T(8,128)S(1)}, u32[]{:S(2)}, u32[]{:S(2)}) collective-permute-start(f32[160,320]{1,0:T(8,128)S(1)} %get-tuple-element.184), channel_id=1, source_target_pairs={{0,1},{1,0},{2,3},{3,2},{4,5},{5,4},{6,7},{7,6},{8,9},{9,8},{10,11... | collective-permute-start | bytes 614408 | tf_op jit(solution)/shard_map/ppermute | solution.py:269
  128.2 9.4 %collective-permute-start.31 = (f32[160,320]{1,0:T(8,128)S(1)}, f32[160,320]{1,0:T(8,128)S(1)}, u32[]{:S(2)}, u32[]{:S(2)}) collective-permute-start(f32[160,320]{1,0:T(8,128)S(1)} %bitcast.63), channel_id=1, source_target_pairs={{0,2},{1,3},{2,0},{3,1},{4,6},{5,7},{6,4},{7,5},{8,10},{9,11},{10,... | collective-permute-start | bytes 614408 | tf_op jit(solution)/shard_map/ppermute | solution.py:269
  129.4 8.3 %collective-permute-start.36 = (f32[160,256]{1,0:T(8,128)S(1)}, f32[160,256]{1,0:T(8,128)S(1)}, u32[]{:S(2)}, u32[]{:S(2)}) collective-permute-start(f32[160,256]{1,0:T(8,128)S(1)} %add_up.5), channel_id=1, source_target_pairs={{0,3},{1,2},{2,1},{3,0},{4,7},{5,6},{6,5},{7,4},{8,11},{9,10},{10,... | collective-permute-start | bytes 491528 | tf_op jit(solution)/shard_map/ppermute | solution.py:269
  129.5 8.1 %collective-permute-start.32 = (f32[160,64]{1,0:T(8,128)S(1)}, f32[160,64]{1,0:T(8,128)S(1)}, u32[]{:S(2)}, u32[]{:S(2)}) collective-permute-start(f32[160,64]{1,0:T(8,128)S(1)} %slice.38), channel_id=1, source_target_pairs={{0,3},{1,2},{2,1},{3,0},{4,7},{5,6},{6,5},{7,4},{8,11},{9,10},{10,... | collective-permute-start | bytes 122888 | tf_op jit(solution)/shard_map/ppermute | solution.py:269

commit v4 on v3

--- a/solution.py
+++ b/solution.py
@@ -15,6 +15,25 @@
 HBM = pl.BlockSpec(memory_space=pltpu.HBM)
 LIMIT = 10 * 2**20
 COL, LOW, HIGH, ROW = range(4)
+ROWS_AT, PIECES_AT, KEPT_AT = (1, 0), (1, 1), (1, 0)
+STEPS = (
+    ("s", 0),
+    ("s", 1),
+    ("g", 0),
+    ("f", 0),
+    ("p", 2),
+    ("p", 3),
+    ("s", 2),
+    ("k", (0, 1)),
+    ("s", 3),
+    ("k", (2,)),
+    ("a", (0, 1)),
+    ("a", (2,)),
+    ("k", (3,)),
+    ("u", (0, 1)),
+    ("u", (2,)),
+    ("u", (3,)),
+)
 
 
 def kernel_call(body, outs, ins, scratch=(), name=None, out_spec=VMEM, aliases=None):
@@ -247,7 +266,7 @@
     for k in range(whole.shape[0]):
         for (piece, start, count), part in zip(places, parts, strict=True):
             if piece == k:
-                whole[k, :, start : start + count] = part[...]
+                whole[k, :, start : start + count] = part[:, :count]
         copy = pltpu.make_async_copy(whole.at[k], out.at[ids[COL] ^ k], sems.at[k])
         copy.start()
         copies.append(copy)
@@ -376,26 +395,32 @@
     swapped = [[], []]
 
     def hop(r, s):
+        nonlocal send_kept
         ring = rings[r]
-        if s > 0:
+        if s > 0 and not (s == n_high - 1 and r == 1):
             tie(ring[s], swapped[r][-1])
+        if (s, r) == ROWS_AT:
+            tie(ring[s], second, *first)
+        if (s, r) == PIECES_AT:
+            tie(ring[s], all_other, all_kept)
+        if (s, r) == KEPT_AT:
+            tie(ring[s], split_kept)
+            send_kept = half_rows(split_kept, low)
+            tie(ring[s], send_kept)
         if s + 1 < n_high:
             ring.append(Box(up(ring[s].value)))
-        swapped[r].append(Box(over_low(ring[s].value)))
-
+        if s == n_high - 1 and r == 1:
+            swapped[r].append(Box(up(swapped[r][-1].value)))
+        else:
+            swapped[r].append(Box(over_low(ring[s].value)))
+
+    send_kept = None
     tie(rings[0][0], mine[2], mine[3])
     rings.append([Box(half_slab((2, 3)))])
-    hop(0, 0)
-    hop(1, 0)
-    tie(rings[0][1], second, *first)
-    tie(rings[0][1], split_kept)
-    send_kept = half_rows(split_kept, low)
-    tie(rings[0][1], send_kept)
-    tie(rings[1][1], all_other, all_kept)
-    for s in range(1, n_high):
+    for s in range(n_high):
         hop(0, s)
         hop(1, s)
-    tie(other[2], rings[0][-1], rings[1][-1])
+    tie(other[2], rings[0][-1], rings[1][-1], swapped[1][-2])
     other[3] = Box(over_col(other[2].value, 1))
     kept[2] = Box(over_col(send_kept.value, 2))
     all_other = Box(place(other, 2, all_other, True))
@@ -432,7 +457,9 @@
                 name="send_part",
             )
         inter[c] = Box(x)
-        got[c] = Box(over_low(send))
+        send = Box(send)
+        tie(send)
+        got[c] = Box(over_low(send.value))
 
     def keep_chunks(cs, direct=False):
         own_widths = tuple(widths[c] for c in cs)
@@ -518,30 +545,39 @@
         tie(stages[cs][0], last)
         last = sum_chunks(cs, *stages[cs])
 
-    send_step(0)
-    send_step(1)
-    tie(last, got[0])
-    tie(kept[2], last)
-    kept[3] = Box(over_col(kept[2].value, 1))
-    place_step(2)
-    place_step(3)
-    send_step(2)
-    keep_step((0, 1))
-    send_step(3)
-    keep_step((2,))
-    add_step((0, 1))
-    add_step((2,))
-    keep_step((3,))
-    sum_step((0, 1))
-    sum_step((2,))
-    sum_step((3,))
-    parts = []
-    for (piece, _, _), spans in zip(order, where, strict=True):
-        spans = [(sums[c][0].value, sums[c][1] + s, n) for c, s, n in spans]
-        part = jnp.concatenate([total[:, s : s + n] for total, s, n in spans], axis=1)
-        parts.append(over_col(part, piece) if piece else part)
+    def got_step(c):
+        nonlocal last
+        tie(last, got[c])
+
+    def forward_step(c):
+        tie(kept[2], last)
+        kept[3] = Box(over_col(kept[2].value, 1))
+
+    steps = {
+        "s": send_step,
+        "p": place_step,
+        "k": keep_step,
+        "a": add_step,
+        "u": sum_step,
+        "g": got_step,
+        "f": forward_step,
+    }
+    for kind, what in STEPS:
+        steps[kind](what)
+    parts, places = [], []
+    for (piece, start, count), spans in zip(order, where, strict=True):
+        if spans[0][0] == 2 and piece == 3:
+            part = over_col(parts[-1][:, widths[2] - count :], 1)
+        elif spans[0][0] == 2:
+            part = over_col(sums[2][0].value, piece)
+        else:
+            spans = [(sums[c][0].value, sums[c][1] + s, n) for c, s, n in spans]
+            part = jnp.concatenate([total[:, s : s + n] for total, s, n in spans], axis=1)
+            part = over_col(part, piece) if piece else part
+        parts.append(part)
+        places.append((piece, start, count))
     out = kernel_call(
-        functools.partial(finish, order),
+        functools.partial(finish, places),
         like((n_pair, block, piece_rows), F32),
         (ids, *parts),
         scratch=[pltpu.VMEM((n_pair, block, piece_rows), F32), pltpu.SemaphoreType.DMA((n_pair,))],

time: 141 us -> 136 us (0.965)
  waiting for transfers between devices: 49.5 us -> 37.9 us
  starting transfers between devices: 34.8 us -> 42.7 us
    ppermute x12 -> x11, waiting for transfers between devices: 13.8 us -> 1.34 us  [over_low(): return lax.ppermute(x, 'row', [(i, i ^ 1) for i in range(n_row)])]
    ppermute x12 -> x11, starting transfers between devices: 10.7 us -> 16.3 us  [over_low(): return lax.ppermute(x, 'row', [(i, i ^ 1) for i in range(n_row)])]
    ppermute x6 -> x7, waiting for transfers between devices: 12.5 us -> 14.7 us  [up(): return lax.ppermute(x, 'row', [(i, (i + 2) % n_row) for i in range(n_row)])]
    ppermute x6 -> x7, starting transfers between devices: 7.87 us -> 9.72 us  [up(): return lax.ppermute(x, 'row', [(i, (i + 2) % n_row) for i in range(n_row)])]
    ppermute x7, starting transfers between devices: 7.92 us -> 9.58 us  [over_high(): lax.ppermute(x, 'row', [(i, (i // 2 ^ k) * 2 + i % 2) for i in range(n_ro...]
  transfers between devices with their start and end apart: 37 -> 37, of which waited for: 19 -> 18; matrix products, arithmetic and copies ran while one was open for 3% -> 3% of each run, Pallas kernels for 34% -> 36%
where the time goes in v4:
time: 136 us
  Pallas kernels  50.1 us (37%)
  starting transfers between devices  42.7 us (31%)
  waiting for transfers between devices  37.9 us (28%)
  local copies, waits for them, and re-layouts  2.91 us (2%)
    pallas_call x21, Pallas kernels, kernel_call(): pl.pallas_call(body, out_shape=outs, in_specs=[SMEM] + [VMEM] * (len(ins)...  50.1 us
    ppermute x11, starting transfers between devices, over_low(): return lax.ppermute(x, 'row', [(i, i ^ 1) for i in range(n_row)])  16.3 us
    ppermute x7, waiting for transfers between devices, up(): return lax.ppermute(x, 'row', [(i, (i + 2) % n_row) for i in range(n_row)])  14.7 us
    ppermute x7, waiting for transfers between devices, over_high(): lax.ppermute(x, 'row', [(i, (i // 2 ^ k) * 2 + i % 2) for i in range(n_ro...  12.3 us
    ppermute x7, starting transfers between devices, up(): return lax.ppermute(x, 'row', [(i, (i + 2) % n_row) for i in range(n_row)])  9.72 us
    ppermute x7, starting transfers between devices, over_high(): lax.ppermute(x, 'row', [(i, (i // 2 ^ k) * 2 + i % 2) for i in range(n_ro...  9.58 us
    ppermute x12, waiting for transfers between devices, over_col(): return lax.ppermute(x, 'col', [(i, i ^ k) for i in range(n_col)])  9.55 us
    ppermute x12, starting transfers between devices, over_col(): return lax.ppermute(x, 'col', [(i, i ^ k) for i in range(n_col)])  7.06 us
  transfers between devices with their start and end apart: 37, of which 18 were waited for; matrix products, arithmetic and copies ran while one was open for 3% of the time, Pallas kernels for 36%

profile of v4, /device:TPU:0, one launch (start us, length us, event | category | flops | bytes accessed | tf_op | source)
XLA Modules:
  0.0 135.7 jit_solution(444559095793904306)
XLA Ops:
  0.5 1.1 dynamic-slice_bitcast_fusion.2
  1.7 2.9 %collective-permute-start.2 = (bf16[40,1280]{1,0:T(8,128)(2,1)S(1)}, bf16[40,1280]{1,0:T(8,128)(2,1)S(1)}, u32[]{:S(2)}, u32[]{:S(2)}) collective-permute-start(bf16[40,1280]{1,0:T(8,128)(2,1)S(1)} %get-tuple-element.186), channel_id=1, source_target_pairs={{0,2},{1,3},{2,0},{3,1},{4,6},{5,7},{6,4},{7,5},{8,10},{9,11},{10,... | collective-permute-start | bytes 307208 | tf_op jit(solution)/shard_map/ppermute | solution.py:288
  6.3 1.0 half_slab.2
  7.2 1.4 %dynamic-slice_bitcast_fusion = bf16[3,1,160,1280]{3,2,1,0:T(8,128)(2,1)S(1)} fusion(bf16[3,1,2,160,1280]{4,3,2,1,0:T(8,128)(2,1)} %bitcast.53, s32[]{:T(128)S(6)} %select_n.55), kind=kLoop, calls=%fused_computation | loop fusion | bytes 2457604 | tf_op jit(solution)/shard_map/jit(dynamic_index_in_dim)/squeeze | solution.py:309
  8.6 1.8 %collective-permute-start.9 = (bf16[3,1,160,1280]{3,2,1,0:T(8,128)(2,1)S(1)}, bf16[3,1,160,1280]{3,2,1,0:T(8,128)(2,1)S(1)}, u32[]{:S(2)}, u32[]{:S(2)}) collective-permute-start(bf16[3,1,160,1280]{3,2,1,0:T(8,128)(2,1)S(1)} %dynamic-slice_bitcast_fusion), channel_id=1, source_target_pairs={{0,2},{1,3},{2,0},{3,1},{4,6},{5,7},{6,4},{7,5},{8,10},{9,11},{10,... | collective-permute-start | bytes 3686408 | tf_op jit(solution)/shard_map/ppermute | solution.py:288
  10.5 1.6 %collective-permute-start.6 = (bf16[80,1280]{1,0:T(8,128)(2,1)S(1)}, bf16[80,1280]{1,0:T(8,128)(2,1)S(1)}, u32[]{:S(2)}, u32[]{:S(2)}) collective-permute-start(bf16[80,1280]{1,0:T(8,128)(2,1)S(1)} %bitcast.56), channel_id=1, source_target_pairs={{0,8},{4,12},{8,16},{12,20},{16,24},{20,28},{24,0},{28,4},{1,9},{5... | collective-permute-start | bytes 614408 | tf_op jit(solution)/shard_map/ppermute | solution.py:297
  12.1 1.5 %collective-permute-start.7 = (bf16[80,1280]{1,0:T(8,128)(2,1)S(1)}, bf16[80,1280]{1,0:T(8,128)(2,1)S(1)}, u32[]{:S(2)}, u32[]{:S(2)}) collective-permute-start(bf16[80,1280]{1,0:T(8,128)(2,1)S(1)} %bitcast.57), channel_id=1, source_target_pairs={{0,4},{4,0},{8,12},{12,8},{16,20},{20,16},{24,28},{28,24},{1,5},{5... | collective-permute-start | bytes 614408 | tf_op jit(solution)/shard_map/ppermute | solution.py:291
  13.7 1.0 half_slab.3
  14.7 1.6 %collective-permute-start.4 = (bf16[80,1280]{1,0:T(8,128)(2,1)S(1)}, bf16[80,1280]{1,0:T(8,128)(2,1)S(1)}, u32[]{:S(2)}, u32[]{:S(2)}) collective-permute-start(bf16[80,1280]{1,0:T(8,128)(2,1)S(1)} %bitcast.59), channel_id=1, source_target_pairs={{0,8},{4,12},{8,16},{12,20},{16,24},{20,28},{24,0},{28,4},{1,9},{5... | collective-permute-start | bytes 614408 | tf_op jit(solution)/shard_map/ppermute | solution.py:297
  16.9 2.8 %place_pieces.1 = (bf16[3,4,160,1280]{3,2,1,0:T(8,128)(2,1)S(1)}, bf16[3,4,160,1280]{3,2,1,0:T(8,128)(2,1)S(1)}) custom-call(s32[4]{0:T(128)S(1)} %pad_add_fusion.ids, s32[20,20]{1,0:T(8,128)S(1)} %copy-done.2, bf16[3,1,2,160,1280]{4,3,2,1,0:T(8,128)(2,1)S(1)} %bitcast.54, bf16[3,1,2,160,1280]{4,3,2,1,0:T(8,128)(2,1)} %bitcast.11.refs_1_), custom_call_target="tpu_custom_call" | custom-call | tf_op jit(solution)/shard_map/place_pieces/pallas_call | solution.py:40
  20.3 1.1 collective-permute-start.10
  21.4 1.9 %collective-permute-start.11 = (bf16[80,1280]{1,0:T(8,128)(2,1)S(1)}, bf16[80,1280]{1,0:T(8,128)(2,1)S(1)}, u32[]{:S(2)}, u32[]{:S(2)}) collective-permute-start(bf16[80,1280]{1,0:T(8,128)(2,1)S(1)} %collective-permute-done.6.refs_1_), channel_id=1, source_target_pairs={{0,4},{4,0},{8,12},{12,8},{16,20},{20,16},{24,28},{28,24},{1,5},{5... | collective-permute-start | bytes 614408 | tf_op jit(solution)/shard_map/ppermute | solution.py:291
  23.3 1.0 collective-permute-done.4.refs_5_
  24.3 1.6 %collective-permute-start.14 = (bf16[80,1280]{1,0:T(8,128)(2,1)S(1)}, bf16[80,1280]{1,0:T(8,128)(2,1)S(1)}, u32[]{:S(2)}, u32[]{:S(2)}) collective-permute-start(bf16[80,1280]{1,0:T(8,128)(2,1)S(1)} %collective-permute-done.4.refs_5_), channel_id=1, source_target_pairs={{0,8},{4,12},{8,16},{12,20},{16,24},{20,28},{24,0},{28,4},{1,9},{5... | collective-permute-start | bytes 614408 | tf_op jit(solution)/shard_map/ppermute | solution.py:297
  25.9 1.6 %collective-permute-start.15 = (bf16[80,1280]{1,0:T(8,128)(2,1)S(1)}, bf16[80,1280]{1,0:T(8,128)(2,1)S(1)}, u32[]{:S(2)}, u32[]{:S(2)}) collective-permute-start(bf16[80,1280]{1,0:T(8,128)(2,1)S(1)} %collective-permute-done.4.refs_5_), channel_id=1, source_target_pairs={{0,4},{4,0},{8,12},{12,8},{16,20},{20,16},{24,28},{28,24},{1,5},{5... | collective-permute-start | bytes 614408 | tf_op jit(solution)/shard_map/ppermute | solution.py:291
  27.6 1.3 collective-permute-done.10.refs_2_
  29.1 1.7 %collective-permute-start.12 = (bf16[80,1280]{1,0:T(8,128)(2,1)S(1)}, bf16[80,1280]{1,0:T(8,128)(2,1)S(1)}, u32[]{:S(2)}, u32[]{:S(2)}) collective-permute-start(bf16[80,1280]{1,0:T(8,128)(2,1)S(1)} %collective-permute-done.10.refs_2_), channel_id=1, source_target_pairs={{0,8},{4,12},{8,16},{12,20},{16,24},{20,28},{24,0},{28,4},{1,9},{5... | collective-permute-start | bytes 614408 | tf_op jit(solution)/shard_map/ppermute | solution.py:297
  30.8 1.5 %collective-permute-start.13 = (bf16[80,1280]{1,0:T(8,128)(2,1)S(1)}, bf16[80,1280]{1,0:T(8,128)(2,1)S(1)}, u32[]{:S(2)}, u32[]{:S(2)}) collective-permute-start(bf16[80,1280]{1,0:T(8,128)(2,1)S(1)} %collective-permute-done.10.refs_2_), channel_id=1, source_target_pairs={{0,4},{4,0},{8,12},{12,8},{16,20},{20,16},{24,28},{28,24},{1,5},{5... | collective-permute-start | bytes 614408 | tf_op jit(solution)/shard_map/ppermute | solution.py:291
  32.3 1.8 %collective-permute-done.14.refs_6_ = bf16[80,1280]{1,0:T(8,128)(2,1)S(1)} collective-permute-done((bf16[80,1280]{1,0:T(8,128)(2,1)S(1)}, bf16[80,1280]{1,0:T(8,128)(2,1)S(1)}, u32[]{:S(2)}, u32[]{:S(2)}) %collective-permute-start.14) | collective-permute-done | bytes 204832 | tf_op jit(solution)/shard_map/ppermute | solution.py:297
  34.1 1.1 collective-permute-start.16
  35.2 1.5 %collective-permute-start.17 = (bf16[80,1280]{1,0:T(8,128)(2,1)S(1)}, bf16[80,1280]{1,0:T(8,128)(2,1)S(1)}, u32[]{:S(2)}, u32[]{:S(2)}) collective-permute-start(bf16[80,1280]{1,0:T(8,128)(2,1)S(1)} %collective-permute-done.14.refs_6_), channel_id=1, source_target_pairs={{0,4},{4,0},{8,12},{12,8},{16,20},{20,16},{24,28},{28,24},{1,5},{5... | collective-permute-start | bytes 614408 | tf_op jit(solution)/shard_map/ppermute | solution.py:291
  36.7 1.6 %collective-permute-done.12.refs_3_ = bf16[80,1280]{1,0:T(8,128)(2,1)S(1)} collective-permute-done((bf16[80,1280]{1,0:T(8,128)(2,1)S(1)}, bf16[80,1280]{1,0:T(8,128)(2,1)S(1)}, u32[]{:S(2)}, u32[]{:S(2)}) %collective-permute-start.12) | collective-permute-done | bytes 204832 | tf_op jit(solution)/shard_map/ppermute | solution.py:297
  38.8 2.9 %collective-permute-done.16.refs_7_ = bf16[80,1280]{1,0:T(8,128)(2,1)S(1)} collective-permute-done((bf16[80,1280]{1,0:T(8,128)(2,1)S(1)}, bf16[80,1280]{1,0:T(8,128)(2,1)S(1)}, u32[]{:S(2)}, u32[]{:S(2)}) %collective-permute-start.16) | collective-permute-done | bytes 204832 | tf_op jit(solution)/shard_map/ppermute | solution.py:297
  43.3 1.5 %collective-permute-start.19 = (bf16[80,1280]{1,0:T(8,128)(2,1)S(1)}, bf16[80,1280]{1,0:T(8,128)(2,1)S(1)}, u32[]{:S(2)}, u32[]{:S(2)}) collective-permute-start(bf16[80,1280]{1,0:T(8,128)(2,1)S(1)} %collective-permute-done.12.refs_3_), channel_id=1, source_target_pairs={{0,4},{4,0},{8,12},{12,8},{16,20},{20,16},{24,28},{28,24},{1,5},{5... | collective-permute-start | bytes 614408 | tf_op jit(solution)/shard_map/ppermute | solution.py:291
  45.8 5.5 %collective-permute-done.20.refs_15_ = bf16[80,1280]{1,0:T(8,128)(2,1)S(1)} collective-permute-done((bf16[80,1280]{1,0:T(8,128)(2,1)S(1)}, bf16[80,1280]{1,0:T(8,128)(2,1)S(1)}, u32[]{:S(2)}, u32[]{:S(2)}) %collective-permute-start.20) | collective-permute-done | bytes 204832 | tf_op jit(solution)/shard_map/ppermute | solution.py:297
  53.1 5.3 %send_part.4 = (bf16[768,1280]{1,0:T(8,128)(2,1)S(1)}, bf16[4,160,256]{2,1,0:T(8,128)(2,1)S(1)}, bf16[640,6]{1,0:T(8,128)(2,1)S(1)}, bf16[640,6]{1,0:T(8,128)(2,1)S(1)}) custom-call(s32[4]{0:T(128)S(1)} %pad_add_fusion.ids, bf16[3,4,160,1280]{3,2,1,0:T(8,128)(2,1)S(1)} %place_halves.5.refs_0_, bf16[3,4,160,1280]{3,2,1,0:T(8,128)(2,1)S(1)} %get-tuple-element.138.refs_1_, ...), custom_call_target="tpu_custom_call" | custom-call | tf_op jit(solution)/shard_map/send_part/pallas_call | solution.py:40
  58.3 1.6 %collective-permute-start.21 = (bf16[4,160,256]{2,1,0:T(8,128)(2,1)S(1)}, bf16[4,160,256]{2,1,0:T(8,128)(2,1)S(1)}, u32[]{:S(2)}, u32[]{:S(2)}) collective-permute-start(bf16[4,160,256]{2,1,0:T(8,128)(2,1)S(1)} %get-tuple-element.133), channel_id=1, source_target_pairs={{0,4},{4,0},{8,12},{12,8},{16,20},{20,16},{24,28},{28,24},{1,5},{5... | collective-permute-start | bytes 983048 | tf_op jit(solution)/shard_map/ppermute | solution.py:291
  59.9 7.8 %send_part.5 = (bf16[1152,1280]{1,0:T(8,128)(2,1)S(1)}, bf16[4,160,384]{2,1,0:T(8,128)(2,1)S(1)}) custom-call(s32[4]{0:T(128)S(1)} %pad_add_fusion.ids, bf16[3,4,160,1280]{3,2,1,0:T(8,128)(2,1)S(1)} %place_halves.5.refs_0_, bf16[3,4,160,1280]{3,2,1,0:T(8,128)(2,1)S(1)} %get-tuple-element.138.refs_1_, bf16[1280,1280]{1,0:T(8,128)(2,1)S(1)} %bitcast.50, ...), custom_call_target="tpu_custom_call" | custom-call | tf_op jit(solution)/shard_map/send_part/pallas_call | solution.py:40
  67.7 3.4 %collective-permute-done.8.refs_0_ = bf16[3,1,160,1280]{3,2,1,0:T(8,128)(2,1)S(1)} collective-permute-done((bf16[3,1,160,1280]{3,2,1,0:T(8,128)(2,1)S(1)}, bf16[3,1,160,1280]{3,2,1,0:T(8,128)(2,1)S(1)}, u32[]{:S(2)}, u32[]{:S(2)}) %collective-permute-start.8) | collective-permute-done | bytes 1228832 | tf_op jit(solution)/shard_map/ppermute | solution.py:288
  71.1 1.5 %collective-permute-start.23 = (bf16[4,160,384]{2,1,0:T(8,128)(2,1)S(1)}, bf16[4,160,384]{2,1,0:T(8,128)(2,1)S(1)}, u32[]{:S(2)}, u32[]{:S(2)}) collective-permute-start(bf16[4,160,384]{2,1,0:T(8,128)(2,1)S(1)} %get-tuple-element.148), channel_id=1, source_target_pairs={{0,4},{4,0},{8,12},{12,8},{16,20},{20,16},{24,28},{28,24},{1,5},{5... | collective-permute-start | bytes 1474568 | tf_op jit(solution)/shard_map/ppermute | solution.py:291
  75.0 7.6 %send_part.6 = (bf16[1152,1280]{1,0:T(8,128)(2,1)S(1)}, bf16[4,160,384]{2,1,0:T(8,128)(2,1)S(1)}) custom-call(s32[4]{0:T(128)S(1)} %pad_add_fusion.ids, bf16[3,4,160,1280]{3,2,1,0:T(8,128)(2,1)S(1)} %place_halves.5.refs_0_, bf16[3,4,160,1280]{3,2,1,0:T(8,128)(2,1)S(1)} %place_halves.7.refs_1_, bf16[1280,1280]{1,0:T(8,128)(2,1)S(1)} %bitcast.51, ...), custom_call_target="tpu_custom_call" | custom-call | tf_op jit(solution)/shard_map/send_part/pallas_call | solution.py:40
  82.6 1.6 %collective-permute-start.24 = (bf16[4,160,384]{2,1,0:T(8,128)(2,1)S(1)}, bf16[4,160,384]{2,1,0:T(8,128)(2,1)S(1)}, u32[]{:S(2)}, u32[]{:S(2)}) collective-permute-start(bf16[4,160,384]{2,1,0:T(8,128)(2,1)S(1)} %get-tuple-element.156), channel_id=1, source_target_pairs={{0,4},{4,0},{8,12},{12,8},{16,20},{20,16},{24,28},{28,24},{1,5},{5... | collective-permute-start | bytes 1474568 | tf_op jit(solution)/shard_map/ppermute | solution.py:291
  84.8 5.0 %keep_part.3 = (f32[2,160,640]{2,1,0:T(8,128)S(1)}, bf16[2,160,640]{2,1,0:T(8,128)(2,1)S(1)}) custom-call(s32[4]{0:T(128)S(1)} %pad_add_fusion.ids, bf16[3,640,1280]{2,1,0:T(8,128)(2,1)S(1)} %bitcast.46, bf16[640,6]{1,0:T(8,128)(2,1)S(1)} %get-tuple-element.144.refs_1_, bf16[768,1280]{1,0:T(8,128)(2,1)S(1)} %get-tuple-element.145.refs_2_, ...), custom_call_target="tpu_custom_call" | custom-call | tf_op jit(solution)/shard_map/keep_part/pallas_call | solution.py:40
  90.7 5.1 %send_part.7 = (bf16[768,1280]{1,0:T(8,128)(2,1)S(1)}, bf16[4,160,256]{2,1,0:T(8,128)(2,1)S(1)}) custom-call(s32[4]{0:T(128)S(1)} %pad_add_fusion.ids, bf16[3,4,160,1280]{3,2,1,0:T(8,128)(2,1)S(1)} %place_halves.5.refs_0_, bf16[3,4,160,1280]{3,2,1,0:T(8,128)(2,1)S(1)} %place_halves.7.refs_1_, bf16[1280,1280]{1,0:T(8,128)(2,1)S(1)} %bitcast.52, ...), custom_call_target="tpu_custom_call" | custom-call | tf_op jit(solution)/shard_map/send_part/pallas_call | solution.py:40
  95.9 3.5 %keep_part.4 = (f32[2,160,384]{2,1,0:T(8,128)S(1)}, bf16[2,160,384]{2,1,0:T(8,128)(2,1)S(1)}) custom-call(s32[4]{0:T(128)S(1)} %pad_add_fusion.ids, bf16[3,640,1280]{2,1,0:T(8,128)(2,1)S(1)} %bitcast.47, bf16[640,6]{1,0:T(8,128)(2,1)S(1)} %get-tuple-element.144.refs_1_, bf16[1152,1280]{1,0:T(8,128)(2,1)S(1)} %get-tuple-element.155.refs_2_, ...), custom_call_target="tpu_custom_call" | custom-call | tf_op jit(solution)/shard_map/keep_part/pallas_call | solution.py:40
  99.4 1.2 collective-permute-start.26
  100.6 1.5 %collective-permute-start.27 = (bf16[4,160,256]{2,1,0:T(8,128)(2,1)S(1)}, bf16[4,160,256]{2,1,0:T(8,128)(2,1)S(1)}, u32[]{:S(2)}, u32[]{:S(2)}) collective-permute-start(bf16[4,160,256]{2,1,0:T(8,128)(2,1)S(1)} %get-tuple-element.168), channel_id=1, source_target_pairs={{0,4},{4,0},{8,12},{12,8},{16,20},{20,16},{24,28},{28,24},{1,5},{5... | collective-permute-start | bytes 983048 | tf_op jit(solution)/shard_map/ppermute | solution.py:291
  102.8 1.9 %collective-permute-start.28 = (bf16[1,160,640]{2,1,0:T(8,128)(2,1)S(1)}, bf16[1,160,640]{2,1,0:T(8,128)(2,1)S(1)}, u32[]{:S(2)}, u32[]{:S(2)}) collective-permute-start(bf16[1,160,640]{2,1,0:T(8,128)(2,1)S(1)} %get-tuple-element.171), channel_id=1, source_target_pairs={{0,16},{4,20},{8,24},{12,28},{16,0},{20,4},{24,8},{28,12},{1,17},{... | collective-permute-start | bytes 614408 | tf_op jit(solution)/shard_map/ppermute | solution.py:294
  104.7 4.5 %collective-permute-done.26.got = bf16[2,160,384]{2,1,0:T(8,128)(2,1)S(1)} collective-permute-done((bf16[2,160,384]{2,1,0:T(8,128)(2,1)S(1)}, bf16[2,160,384]{2,1,0:T(8,128)(2,1)S(1)}, u32[]{:S(2)}, u32[]{:S(2)}) %collective-permute-start.26) | collective-permute-done | bytes 245792 | tf_op jit(solution)/shard_map/ppermute | solution.py:294
  109.7 1.1 collective-permute-start.30
  110.8 2.1 %keep_part.5 = (f32[160,256]{1,0:T(8,128)S(1)}, bf16[160,256]{1,0:T(8,128)(2,1)S(1)}, bf16[160,256]{1,0:T(8,128)(2,1)S(1)}, bf16[160,256]{1,0:T(8,128)(2,1)S(1)}) custom-call(s32[4]{0:T(128)S(1)} %pad_add_fusion.ids, bf16[3,640,1280]{2,1,0:T(8,128)(2,1)S(1)} %bitcast.48, bf16[640,6]{1,0:T(8,128)(2,1)S(1)} %get-tuple-element.144.refs_1_, ...), custom_call_target="tpu_custom_call" | custom-call | tf_op jit(solution)/shard_map/keep_part/pallas_call | solution.py:40
  113.0 5.1 %collective-permute-done.28 = bf16[1,160,640]{2,1,0:T(8,128)(2,1)S(1)} collective-permute-done((bf16[1,160,640]{2,1,0:T(8,128)(2,1)S(1)}, bf16[1,160,640]{2,1,0:T(8,128)(2,1)S(1)}, u32[]{:S(2)}, u32[]{:S(2)}) %collective-permute-start.28) | collective-permute-done | bytes 204832 | tf_op jit(solution)/shard_map/ppermute | solution.py:294
  118.7 2.6 %collective-permute-start.34 = (bf16[160,256]{1,0:T(8,128)(2,1)S(1)}, bf16[160,256]{1,0:T(8,128)(2,1)S(1)}, u32[]{:S(2)}, u32[]{:S(2)}) collective-permute-start(bf16[160,256]{1,0:T(8,128)(2,1)S(1)} %get-tuple-element.179), channel_id=1, source_target_pairs={{0,16},{4,20},{8,24},{12,28},{16,0},{20,4},{24,8},{28,12},{1,17},{... | collective-permute-start | bytes 245768 | tf_op jit(solution)/shard_map/ppermute | solution.py:294
  121.3 1.8 %collective-permute-start.35 = (bf16[160,256]{1,0:T(8,128)(2,1)S(1)}, bf16[160,256]{1,0:T(8,128)(2,1)S(1)}, u32[]{:S(2)}, u32[]{:S(2)}) collective-permute-start(bf16[160,256]{1,0:T(8,128)(2,1)S(1)} %get-tuple-element.180), channel_id=1, source_target_pairs={{0,24},{4,28},{8,16},{12,20},{16,8},{20,12},{24,0},{28,4},{1,25},{... | collective-permute-start | bytes 245768 | tf_op jit(solution)/shard_map/ppermute | solution.py:294
  124.7 2.8 %collective-permute-done.35.refs_2_ = bf16[160,256]{1,0:T(8,128)(2,1)S(1)} collective-permute-done((bf16[160,256]{1,0:T(8,128)(2,1)S(1)}, bf16[160,256]{1,0:T(8,128)(2,1)S(1)}, u32[]{:S(2)}, u32[]{:S(2)}) %collective-permute-start.35) | collective-permute-done | bytes 81952 | tf_op jit(solution)/shard_map/ppermute | solution.py:294
  128.2 1.8 %collective-permute-done.31.refs_2_ = f32[160,384]{1,0:T(8,128)S(1)} collective-permute-done((f32[160,384]{1,0:T(8,128)S(1)}, f32[160,384]{1,0:T(8,128)S(1)}, u32[]{:S(2)}, u32[]{:S(2)}) %collective-permute-start.31) | collective-permute-done | bytes 245792 | tf_op jit(solution)/shard_map/ppermute | solution.py:288
  130.1 3.9 %collective-permute-done.36.refs_4_ = f32[160,256]{1,0:T(8,128)S(1)} collective-permute-done((f32[160,256]{1,0:T(8,128)S(1)}, f32[160,256]{1,0:T(8,128)S(1)}, u32[]{:S(2)}, u32[]{:S(2)}) %collective-permute-start.36) | collective-permute-done | bytes 163872 | tf_op jit(solution)/shard_map/ppermute | solution.py:288
  134.0 1.5 %finish.1 = f32[4,160,320]{2,1,0:T(8,128)} custom-call(s32[4]{0:T(128)S(1)} %pad_add_fusion.ids, f32[160,320]{1,0:T(8,128)S(1)} %collective-permute-done.29.refs_0_, f32[160,320]{1,0:T(8,128)S(1)} %get-tuple-element.181.refs_1_, f32[160,384]{1,0:T(8,128)S(1)} %collective-permute-done.31.refs_2_, f32[160,64]{1,0:T(8,128)S(1)} %collective-permute-done.32.refs_3_, ...), custom_call_target="tpu_custom_call" | custom-call | tf_op jit(solution)/shard_map/finish/pallas_call | solution.py:40
  (76 shorter events, 16.7 us)
Async XLA Ops:
  0.0 5.4 %copy-start = (bf16[3,160,1280]{2,1,0:T(8,128)(2,1)S(1)}, bf16[3,160,1280]{2,1,0:T(8,128)(2,1)}, u32[]{:S(2)}) copy-start(bf16[3,160,1280]{2,1,0:T(8,128)(2,1)} %param.8) | copy-start | bytes 3686404
  0.0 6.1 %copy-start.3 = (s32[4,20,20]{2,0,1:T(4,128)S(1)}, s32[4,20,20]{2,0,1:T(4,128)}, u32[]{:S(2)}) copy-start(s32[4,20,20]{2,0,1:T(4,128)} %param.10) | copy-start | bytes 19204
  0.0 6.2 %collective-permute-start = (bf16[3,320,1280]{2,1,0:T(8,128)(2,1)}, bf16[3,320,1280]{2,1,0:T(8,128)(2,1)}, u32[]{:S(2)}, u32[]{:S(2)}) collective-permute-start(bf16[3,320,1280]{2,1,0:T(8,128)(2,1)} %param.7), channel_id=1, source_target_pairs={{0,1},{1,0},{2,3},{3,2},{4,5},{5,4},{6,7},{7,6},{8,9},{9,8},{10,11... | collective-permute-start | bytes 7372808 | tf_op jit(solution)/shard_map/ppermute | solution.py:288
  1.5 4.7 %collective-permute-start.1 = (bf16[40,1280]{1,0:T(8,128)(2,1)S(1)}, bf16[40,1280]{1,0:T(8,128)(2,1)S(1)}, u32[]{:S(2)}, u32[]{:S(2)}) collective-permute-start(bf16[40,1280]{1,0:T(8,128)(2,1)S(1)} %get-tuple-element.185), channel_id=1, source_target_pairs={{0,1},{1,0},{2,3},{3,2},{4,5},{5,4},{6,7},{7,6},{8,9},{9,8},{10,11... | collective-permute-start | bytes 307208 | tf_op jit(solution)/shard_map/ppermute | solution.py:288
  1.7 8.7 %collective-permute-start.2 = (bf16[40,1280]{1,0:T(8,128)(2,1)S(1)}, bf16[40,1280]{1,0:T(8,128)(2,1)S(1)}, u32[]{:S(2)}, u32[]{:S(2)}) collective-permute-start(bf16[40,1280]{1,0:T(8,128)(2,1)S(1)} %get-tuple-element.186), channel_id=1, source_target_pairs={{0,2},{1,3},{2,0},{3,1},{4,6},{5,7},{6,4},{7,5},{8,10},{9,11},{10,... | collective-permute-start | bytes 307208 | tf_op jit(solution)/shard_map/ppermute | solution.py:288
  4.6 5.9 %collective-permute-start.3 = (bf16[40,1280]{1,0:T(8,128)(2,1)S(1)}, bf16[40,1280]{1,0:T(8,128)(2,1)S(1)}, u32[]{:S(2)}, u32[]{:S(2)}) collective-permute-start(bf16[40,1280]{1,0:T(8,128)(2,1)S(1)} %get-tuple-element.183), channel_id=1, source_target_pairs={{0,3},{1,2},{2,1},{3,0},{4,7},{5,6},{6,5},{7,4},{8,11},{9,10},{10,... | collective-permute-start | bytes 307208 | tf_op jit(solution)/shard_map/ppermute | solution.py:288
  5.7 11.1 %copy-start.2 = (s32[20,20]{1,0:T(8,128)S(1)}, s32[20,20]{1,0:T(8,128)}, u32[]{:S(2)}) copy-start(s32[20,20]{1,0:T(8,128)} %tiles.9) | copy-start | bytes 4804
  5.9 11.0 %copy-start.1 = (bf16[3,320,1280]{2,1,0:T(8,128)(2,1)S(1)}, bf16[3,320,1280]{2,1,0:T(8,128)(2,1)}, u32[]{:S(2)}) copy-start(bf16[3,320,1280]{2,1,0:T(8,128)(2,1)} %param.7) | copy-start | bytes 7372804
  8.6 33.1 %collective-permute-start.9 = (bf16[3,1,160,1280]{3,2,1,0:T(8,128)(2,1)S(1)}, bf16[3,1,160,1280]{3,2,1,0:T(8,128)(2,1)S(1)}, u32[]{:S(2)}, u32[]{:S(2)}) collective-permute-start(bf16[3,1,160,1280]{3,2,1,0:T(8,128)(2,1)S(1)} %dynamic-slice_bitcast_fusion), channel_id=1, source_target_pairs={{0,2},{1,3},{2,0},{3,1},{4,6},{5,7},{6,4},{7,5},{8,10},{9,11},{10,... | collective-permute-start | bytes 3686408 | tf_op jit(solution)/shard_map/ppermute | solution.py:288
  10.5 9.8 %collective-permute-start.6 = (bf16[80,1280]{1,0:T(8,128)(2,1)S(1)}, bf16[80,1280]{1,0:T(8,128)(2,1)S(1)}, u32[]{:S(2)}, u32[]{:S(2)}) collective-permute-start(bf16[80,1280]{1,0:T(8,128)(2,1)S(1)} %bitcast.56), channel_id=1, source_target_pairs={{0,8},{4,12},{8,16},{12,20},{16,24},{20,28},{24,0},{28,4},{1,9},{5... | collective-permute-start | bytes 614408 | tf_op jit(solution)/shard_map/ppermute | solution.py:297
  12.1 8.1 %collective-permute-start.7 = (bf16[80,1280]{1,0:T(8,128)(2,1)S(1)}, bf16[80,1280]{1,0:T(8,128)(2,1)S(1)}, u32[]{:S(2)}, u32[]{:S(2)}) collective-permute-start(bf16[80,1280]{1,0:T(8,128)(2,1)S(1)} %bitcast.57), channel_id=1, source_target_pairs={{0,4},{4,0},{8,12},{12,8},{16,20},{20,16},{24,28},{28,24},{1,5},{5... | collective-permute-start | bytes 614408 | tf_op jit(solution)/shard_map/ppermute | solution.py:291
  14.7 9.6 %collective-permute-start.4 = (bf16[80,1280]{1,0:T(8,128)(2,1)S(1)}, bf16[80,1280]{1,0:T(8,128)(2,1)S(1)}, u32[]{:S(2)}, u32[]{:S(2)}) collective-permute-start(bf16[80,1280]{1,0:T(8,128)(2,1)S(1)} %bitcast.59), channel_id=1, source_target_pairs={{0,8},{4,12},{8,16},{12,20},{16,24},{20,28},{24,0},{28,4},{1,9},{5... | collective-permute-start | bytes 614408 | tf_op jit(solution)/shard_map/ppermute | solution.py:297
  16.3 8.0 %collective-permute-start.5 = (bf16[80,1280]{1,0:T(8,128)(2,1)S(1)}, bf16[80,1280]{1,0:T(8,128)(2,1)S(1)}, u32[]{:S(2)}, u32[]{:S(2)}) collective-permute-start(bf16[80,1280]{1,0:T(8,128)(2,1)S(1)} %bitcast.60), channel_id=1, source_target_pairs={{0,4},{4,0},{8,12},{12,8},{16,20},{20,16},{24,28},{28,24},{1,5},{5... | collective-permute-start | bytes 614408 | tf_op jit(solution)/shard_map/ppermute | solution.py:291
  20.3 8.5 %collective-permute-start.10 = (bf16[80,1280]{1,0:T(8,128)(2,1)S(1)}, bf16[80,1280]{1,0:T(8,128)(2,1)S(1)}, u32[]{:S(2)}, u32[]{:S(2)}) collective-permute-start(bf16[80,1280]{1,0:T(8,128)(2,1)S(1)} %collective-permute-done.6.refs_1_), channel_id=1, source_target_pairs={{0,8},{4,12},{8,16},{12,20},{16,24},{20,28},{24,0},{28,4},{1,9},{5... | collective-permute-start | bytes 614408 | tf_op jit(solution)/shard_map/ppermute | solution.py:297
  21.4 7.7 %collective-permute-start.11 = (bf16[80,1280]{1,0:T(8,128)(2,1)S(1)}, bf16[80,1280]{1,0:T(8,128)(2,1)S(1)}, u32[]{:S(2)}, u32[]{:S(2)}) collective-permute-start(bf16[80,1280]{1,0:T(8,128)(2,1)S(1)} %collective-permute-done.6.refs_1_), channel_id=1, source_target_pairs={{0,4},{4,0},{8,12},{12,8},{16,20},{20,16},{24,28},{28,24},{1,5},{5... | collective-permute-start | bytes 614408 | tf_op jit(solution)/shard_map/ppermute | solution.py:291
  24.3 9.8 %collective-permute-start.14 = (bf16[80,1280]{1,0:T(8,128)(2,1)S(1)}, bf16[80,1280]{1,0:T(8,128)(2,1)S(1)}, u32[]{:S(2)}, u32[]{:S(2)}) collective-permute-start(bf16[80,1280]{1,0:T(8,128)(2,1)S(1)} %collective-permute-done.4.refs_5_), channel_id=1, source_target_pairs={{0,8},{4,12},{8,16},{12,20},{16,24},{20,28},{24,0},{28,4},{1,9},{5... | collective-permute-start | bytes 614408 | tf_op jit(solution)/shard_map/ppermute | solution.py:297
  25.9 8.2 %collective-permute-start.15 = (bf16[80,1280]{1,0:T(8,128)(2,1)S(1)}, bf16[80,1280]{1,0:T(8,128)(2,1)S(1)}, u32[]{:S(2)}, u32[]{:S(2)}) collective-permute-start(bf16[80,1280]{1,0:T(8,128)(2,1)S(1)} %collective-permute-done.4.refs_5_), channel_id=1, source_target_pairs={{0,4},{4,0},{8,12},{12,8},{16,20},{20,16},{24,28},{28,24},{1,5},{5... | collective-permute-start | bytes 614408 | tf_op jit(solution)/shard_map/ppermute | solution.py:291
  29.1 9.2 %collective-permute-start.12 = (bf16[80,1280]{1,0:T(8,128)(2,1)S(1)}, bf16[80,1280]{1,0:T(8,128)(2,1)S(1)}, u32[]{:S(2)}, u32[]{:S(2)}) collective-permute-start(bf16[80,1280]{1,0:T(8,128)(2,1)S(1)} %collective-permute-done.10.refs_2_), channel_id=1, source_target_pairs={{0,8},{4,12},{8,16},{12,20},{16,24},{20,28},{24,0},{28,4},{1,9},{5... | collective-permute-start | bytes 614408 | tf_op jit(solution)/shard_map/ppermute | solution.py:297
  30.8 7.9 %collective-permute-start.13 = (bf16[80,1280]{1,0:T(8,128)(2,1)S(1)}, bf16[80,1280]{1,0:T(8,128)(2,1)S(1)}, u32[]{:S(2)}, u32[]{:S(2)}) collective-permute-start(bf16[80,1280]{1,0:T(8,128)(2,1)S(1)} %collective-permute-done.10.refs_2_), channel_id=1, source_target_pairs={{0,4},{4,0},{8,12},{12,8},{16,20},{20,16},{24,28},{28,24},{1,5},{5... | collective-permute-start | bytes 614408 | tf_op jit(solution)/shard_map/ppermute | solution.py:291
  34.1 7.6 %collective-permute-start.16 = (bf16[80,1280]{1,0:T(8,128)(2,1)S(1)}, bf16[80,1280]{1,0:T(8,128)(2,1)S(1)}, u32[]{:S(2)}, u32[]{:S(2)}) collective-permute-start(bf16[80,1280]{1,0:T(8,128)(2,1)S(1)} %collective-permute-done.14.refs_6_), channel_id=1, source_target_pairs={{0,8},{4,12},{8,16},{12,20},{16,24},{20,28},{24,0},{28,4},{1,9},{5... | collective-permute-start | bytes 614408 | tf_op jit(solution)/shard_map/ppermute | solution.py:297
  35.2 6.5 %collective-permute-start.17 = (bf16[80,1280]{1,0:T(8,128)(2,1)S(1)}, bf16[80,1280]{1,0:T(8,128)(2,1)S(1)}, u32[]{:S(2)}, u32[]{:S(2)}) collective-permute-start(bf16[80,1280]{1,0:T(8,128)(2,1)S(1)} %collective-permute-done.14.refs_6_), channel_id=1, source_target_pairs={{0,4},{4,0},{8,12},{12,8},{16,20},{20,16},{24,28},{28,24},{1,5},{5... | collective-permute-start | bytes 614408 | tf_op jit(solution)/shard_map/ppermute | solution.py:291
  41.7 10.4 %collective-permute-start.18 = (bf16[3,1,160,1280]{3,2,1,0:T(8,128)(2,1)S(1)}, bf16[3,1,160,1280]{3,2,1,0:T(8,128)(2,1)S(1)}, u32[]{:S(2)}, u32[]{:S(2)}) collective-permute-start(bf16[3,1,160,1280]{3,2,1,0:T(8,128)(2,1)S(1)} %collective-permute-done.9.refs_0_), channel_id=1, source_target_pairs={{0,1},{1,0},{2,3},{3,2},{4,5},{5,4},{6,7},{7,6},{8,9},{9,8},{10,11... | collective-permute-start | bytes 3686408 | tf_op jit(solution)/shard_map/ppermute | solution.py:288
  41.7 29.4 %collective-permute-start.8 = (bf16[3,1,160,1280]{3,2,1,0:T(8,128)(2,1)S(1)}, bf16[3,1,160,1280]{3,2,1,0:T(8,128)(2,1)S(1)}, u32[]{:S(2)}, u32[]{:S(2)}) collective-permute-start(bf16[3,1,160,1280]{3,2,1,0:T(8,128)(2,1)S(1)} %dynamic-slice_bitcast_fusion.1), channel_id=1, source_target_pairs={{0,2},{1,3},{2,0},{3,1},{4,6},{5,7},{6,4},{7,5},{8,10},{9,11},{10,... | collective-permute-start | bytes 3686408 | tf_op jit(solution)/shard_map/ppermute | solution.py:288
  42.4 8.9 %collective-permute-start.20 = (bf16[80,1280]{1,0:T(8,128)(2,1)S(1)}, bf16[80,1280]{1,0:T(8,128)(2,1)S(1)}, u32[]{:S(2)}, u32[]{:S(2)}) collective-permute-start(bf16[80,1280]{1,0:T(8,128)(2,1)S(1)} %collective-permute-done.17.refs_14_), channel_id=1, source_target_pairs={{0,8},{4,12},{8,16},{12,20},{16,24},{20,28},{24,0},{28,4},{1,9},{5... | collective-permute-start | bytes 614408 | tf_op jit(solution)/shard_map/ppermute | solution.py:297
  43.3 8.0 %collective-permute-start.19 = (bf16[80,1280]{1,0:T(8,128)(2,1)S(1)}, bf16[80,1280]{1,0:T(8,128)(2,1)S(1)}, u32[]{:S(2)}, u32[]{:S(2)}) collective-permute-start(bf16[80,1280]{1,0:T(8,128)(2,1)S(1)} %collective-permute-done.12.refs_3_), channel_id=1, source_target_pairs={{0,4},{4,0},{8,12},{12,8},{16,20},{20,16},{24,28},{28,24},{1,5},{5... | collective-permute-start | bytes 614408 | tf_op jit(solution)/shard_map/ppermute | solution.py:291
  58.3 9.4 %collective-permute-start.21 = (bf16[4,160,256]{2,1,0:T(8,128)(2,1)S(1)}, bf16[4,160,256]{2,1,0:T(8,128)(2,1)S(1)}, u32[]{:S(2)}, u32[]{:S(2)}) collective-permute-start(bf16[4,160,256]{2,1,0:T(8,128)(2,1)S(1)} %get-tuple-element.133), channel_id=1, source_target_pairs={{0,4},{4,0},{8,12},{12,8},{16,20},{20,16},{24,28},{28,24},{1,5},{5... | collective-permute-start | bytes 983048 | tf_op jit(solution)/shard_map/ppermute | solution.py:291
  71.1 2.9 %collective-permute-start.22 = (bf16[3,1,160,1280]{3,2,1,0:T(8,128)(2,1)S(1)}, bf16[3,1,160,1280]{3,2,1,0:T(8,128)(2,1)S(1)}, u32[]{:S(2)}, u32[]{:S(2)}) collective-permute-start(bf16[3,1,160,1280]{3,2,1,0:T(8,128)(2,1)S(1)} %collective-permute-done.8.refs_0_), channel_id=1, source_target_pairs={{0,1},{1,0},{2,3},{3,2},{4,5},{5,4},{6,7},{7,6},{8,9},{9,8},{10,11... | collective-permute-start | bytes 3686408 | tf_op jit(solution)/shard_map/ppermute | solution.py:288
  71.1 13.6 %collective-permute-start.23 = (bf16[4,160,384]{2,1,0:T(8,128)(2,1)S(1)}, bf16[4,160,384]{2,1,0:T(8,128)(2,1)S(1)}, u32[]{:S(2)}, u32[]{:S(2)}) collective-permute-start(bf16[4,160,384]{2,1,0:T(8,128)(2,1)S(1)} %get-tuple-element.148), channel_id=1, source_target_pairs={{0,4},{4,0},{8,12},{12,8},{16,20},{20,16},{24,28},{28,24},{1,5},{5... | collective-permute-start | bytes 1474568 | tf_op jit(solution)/shard_map/ppermute | solution.py:291
  82.6 13.3 %collective-permute-start.24 = (bf16[4,160,384]{2,1,0:T(8,128)(2,1)S(1)}, bf16[4,160,384]{2,1,0:T(8,128)(2,1)S(1)}, u32[]{:S(2)}, u32[]{:S(2)}) collective-permute-start(bf16[4,160,384]{2,1,0:T(8,128)(2,1)S(1)} %get-tuple-element.156), channel_id=1, source_target_pairs={{0,4},{4,0},{8,12},{12,8},{16,20},{20,16},{24,28},{28,24},{1,5},{5... | collective-permute-start | bytes 1474568 | tf_op jit(solution)/shard_map/ppermute | solution.py:291
  89.8 12.3 %collective-permute-start.25 = (bf16[2,160,640]{2,1,0:T(8,128)(2,1)S(1)}, bf16[2,160,640]{2,1,0:T(8,128)(2,1)S(1)}, u32[]{:S(2)}, u32[]{:S(2)}) collective-permute-start(bf16[2,160,640]{2,1,0:T(8,128)(2,1)S(1)} %get-tuple-element.160), channel_id=1, source_target_pairs={{0,8},{4,12},{8,0},{12,4},{16,24},{20,28},{24,16},{28,20},{1,9},{5... | collective-permute-start | bytes 1228808 | tf_op jit(solution)/shard_map/ppermute | solution.py:294
  99.4 9.7 %collective-permute-start.26 = (bf16[2,160,384]{2,1,0:T(8,128)(2,1)S(1)}, bf16[2,160,384]{2,1,0:T(8,128)(2,1)S(1)}, u32[]{:S(2)}, u32[]{:S(2)}) collective-permute-start(bf16[2,160,384]{2,1,0:T(8,128)(2,1)S(1)} %get-tuple-element.163), channel_id=1, source_target_pairs={{0,8},{4,12},{8,0},{12,4},{16,24},{20,28},{24,16},{28,20},{1,9},{5... | collective-permute-start | bytes 737288 | tf_op jit(solution)/shard_map/ppermute | solution.py:294
  100.6 10.3 %collective-permute-start.27 = (bf16[4,160,256]{2,1,0:T(8,128)(2,1)S(1)}, bf16[4,160,256]{2,1,0:T(8,128)(2,1)S(1)}, u32[]{:S(2)}, u32[]{:S(2)}) collective-permute-start(bf16[4,160,256]{2,1,0:T(8,128)(2,1)S(1)} %get-tuple-element.168), channel_id=1, source_target_pairs={{0,4},{4,0},{8,12},{12,8},{16,20},{20,16},{24,28},{28,24},{1,5},{5... | collective-permute-start | bytes 983048 | tf_op jit(solution)/shard_map/ppermute | solution.py:291
  102.8 15.3 %collective-permute-start.28 = (bf16[1,160,640]{2,1,0:T(8,128)(2,1)S(1)}, bf16[1,160,640]{2,1,0:T(8,128)(2,1)S(1)}, u32[]{:S(2)}, u32[]{:S(2)}) collective-permute-start(bf16[1,160,640]{2,1,0:T(8,128)(2,1)S(1)} %get-tuple-element.171), channel_id=1, source_target_pairs={{0,16},{4,20},{8,24},{12,28},{16,0},{20,4},{24,8},{28,12},{1,17},{... | collective-permute-start | bytes 614408 | tf_op jit(solution)/shard_map/ppermute | solution.py:294
  109.7 13.4 %collective-permute-start.30 = (bf16[1,160,384]{2,1,0:T(8,128)(2,1)S(1)}, bf16[1,160,384]{2,1,0:T(8,128)(2,1)S(1)}, u32[]{:S(2)}, u32[]{:S(2)}) collective-permute-start(bf16[1,160,384]{2,1,0:T(8,128)(2,1)S(1)} %get-tuple-element.175), channel_id=1, source_target_pairs={{0,16},{4,20},{8,24},{12,28},{16,0},{20,4},{24,8},{28,12},{1,17},{... | collective-permute-start | bytes 368648 | tf_op jit(solution)/shard_map/ppermute | solution.py:294
  118.6 6.1 %collective-permute-start.33 = (bf16[160,256]{1,0:T(8,128)(2,1)S(1)}, bf16[160,256]{1,0:T(8,128)(2,1)S(1)}, u32[]{:S(2)}, u32[]{:S(2)}) collective-permute-start(bf16[160,256]{1,0:T(8,128)(2,1)S(1)} %get-tuple-element.178), channel_id=1, source_target_pairs={{0,8},{4,12},{8,0},{12,4},{16,24},{20,28},{24,16},{28,20},{1,9},{5... | collective-permute-start | bytes 245768 | tf_op jit(solution)/shard_map/ppermute | solution.py:294
  118.7 6.0 %collective-permute-start.34 = (bf16[160,256]{1,0:T(8,128)(2,1)S(1)}, bf16[160,256]{1,0:T(8,128)(2,1)S(1)}, u32[]{:S(2)}, u32[]{:S(2)}) collective-permute-start(bf16[160,256]{1,0:T(8,128)(2,1)S(1)} %get-tuple-element.179), channel_id=1, source_target_pairs={{0,16},{4,20},{8,24},{12,28},{16,0},{20,4},{24,8},{28,12},{1,17},{... | collective-permute-start | bytes 245768 | tf_op jit(solution)/shard_map/ppermute | solution.py:294
  121.3 6.2 %collective-permute-start.35 = (bf16[160,256]{1,0:T(8,128)(2,1)S(1)}, bf16[160,256]{1,0:T(8,128)(2,1)S(1)}, u32[]{:S(2)}, u32[]{:S(2)}) collective-permute-start(bf16[160,256]{1,0:T(8,128)(2,1)S(1)} %get-tuple-element.180), channel_id=1, source_target_pairs={{0,24},{4,28},{8,16},{12,20},{16,8},{20,12},{24,0},{28,4},{1,25},{... | collective-permute-start | bytes 245768 | tf_op jit(solution)/shard_map/ppermute | solution.py:294
  123.7 6.3 %collective-permute-start.31 = (f32[160,384]{1,0:T(8,128)S(1)}, f32[160,384]{1,0:T(8,128)S(1)}, u32[]{:S(2)}, u32[]{:S(2)}) collective-permute-start(f32[160,384]{1,0:T(8,128)S(1)} %add_up.4), channel_id=1, source_target_pairs={{0,2},{1,3},{2,0},{3,1},{4,6},{5,7},{6,4},{7,5},{8,10},{9,11},{10,... | collective-permute-start | bytes 737288 | tf_op jit(solution)/shard_map/ppermute | solution.py:288
  124.6 5.4 %collective-permute-start.29 = (f32[160,320]{1,0:T(8,128)S(1)}, f32[160,320]{1,0:T(8,128)S(1)}, u32[]{:S(2)}, u32[]{:S(2)}) collective-permute-start(f32[160,320]{1,0:T(8,128)S(1)} %get-tuple-element.182), channel_id=1, source_target_pairs={{0,1},{1,0},{2,3},{3,2},{4,5},{5,4},{6,7},{7,6},{8,9},{9,8},{10,11... | collective-permute-start | bytes 614408 | tf_op jit(solution)/shard_map/ppermute | solution.py:288
  128.1 5.9 %collective-permute-start.36 = (f32[160,256]{1,0:T(8,128)S(1)}, f32[160,256]{1,0:T(8,128)S(1)}, u32[]{:S(2)}, u32[]{:S(2)}) collective-permute-start(f32[160,256]{1,0:T(8,128)S(1)} %add_up.5), channel_id=1, source_target_pairs={{0,3},{1,2},{2,1},{3,0},{4,7},{5,6},{6,5},{7,4},{8,11},{9,10},{10,... | collective-permute-start | bytes 491528 | tf_op jit(solution)/shard_map/ppermute | solution.py:288
  130.0 4.0 %collective-permute-start.32 = (f32[160,64]{1,0:T(8,128)S(1)}, f32[160,64]{1,0:T(8,128)S(1)}, u32[]{:S(2)}, u32[]{:S(2)}) collective-permute-start(f32[160,64]{1,0:T(8,128)S(1)} %slice.39), channel_id=1, source_target_pairs={{0,1},{1,0},{2,3},{3,2},{4,5},{5,4},{6,7},{7,6},{8,9},{9,8},{10,11... | collective-permute-start | bytes 122888 | tf_op jit(solution)/shard_map/ppermute | solution.py:288

commit v5 on v4

--- a/solution.py
+++ b/solution.py
@@ -120,6 +120,17 @@
                 out[q, owner * groups + g] = piece[q, g] * mask
 
 
+def place_parts(k, ids, tiles, *refs):
+    out = refs[-1]
+    pieces = refs[: out.shape[0]]
+    owner = ids[COL] ^ k
+    _, groups, block, size = pieces[0].shape
+    for g in range(groups):
+        mask = masked_block(ids, tiles, owner, g, 1 - ids[LOW], groups, block, size)
+        for q, piece in enumerate(pieces):
+            out[q, owner * groups + g] = piece[0, g] * mask
+
+
 def multiply_rows(factors, inter, carried, first, width):
     value = jnp.dot(carried[...], first[...], preferred_element_type=F32)
     for q in range(factors.shape[0]):
@@ -421,12 +432,20 @@
         hop(0, s)
         hop(1, s)
     tie(other[2], rings[0][-1], rings[1][-1], swapped[1][-2])
-    other[3] = Box(over_col(other[2].value, 1))
+    other[3] = [over_col(other[2].value[q : q + 1], 1) for q in range(aux)]
     kept[2] = Box(over_col(send_kept.value, 2))
     all_other = Box(place(other, 2, all_other, True))
     found = [(slab, (s, low, r)) for low, side in enumerate((rings, swapped)) for r in range(2) for s, slab in enumerate(side[r])]
     amp = Box(place_slabs(found).reshape(size, size))
-    all_other = Box(place(other, 3, all_other, True))
+    all_other = Box(
+        kernel_call(
+            functools.partial(place_parts, 3),
+            shape,
+            (ids, int_tiles, *other[3], all_other.value),
+            aliases={2 + aux: 0},
+            name="place_parts",
+        )
+    )
 
     inter, got, sums, carried = {}, {}, {}, []
 

time: 136 us -> 133 us (0.978)
  starting transfers between devices: 42.7 us -> 39.3 us
    ppermute x11, waiting for transfers between devices: 1.34 us -> 9.07 us  [over_low(): return lax.ppermute(x, 'row', [(i, i ^ 1) for i in range(n_row)])]
    ppermute x7, waiting for transfers between devices: 14.7 us -> 10.2 us  [up(): return lax.ppermute(x, 'row', [(i, (i + 2) % n_row) for i in range(n_row)])]
    ppermute x11, starting transfers between devices: 16.3 us -> 13.3 us  [over_low(): return lax.ppermute(x, 'row', [(i, i ^ 1) for i in range(n_row)])]
    ppermute x12 -> x14, waiting for transfers between devices: 9.55 us -> 7.53 us  [over_col(): return lax.ppermute(x, 'col', [(i, i ^ k) for i in range(n_col)])]
    ppermute x7, starting transfers between devices: 9.58 us -> 8.06 us  [over_high(): lax.ppermute(x, 'row', [(i, (i // 2 ^ k) * 2 + i % 2) for i in range(n_ro...]
    ppermute x12 -> x14, starting transfers between devices: 7.06 us -> 7.57 us  [over_col(): return lax.ppermute(x, 'col', [(i, i ^ k) for i in range(n_col)])]
  transfers between devices with their start and end apart: 37 -> 39, of which waited for: 18 -> 19; matrix products, arithmetic and copies ran while one was open for 3% -> 3% of each run, Pallas kernels for 36% -> 37%
where the time goes in v5:
time: 133 us
  Pallas kernels  50.1 us (38%)
  starting transfers between devices  39.3 us (30%)
  waiting for transfers between devices  38.5 us (29%)
  local copies, waits for them, and re-layouts  2.99 us (2%)
    pallas_call x21, Pallas kernels, kernel_call(): pl.pallas_call(body, out_shape=outs, in_specs=[SMEM] + [VMEM] * (len(ins)...  50.1 us
    ppermute x11, starting transfers between devices, over_low(): return lax.ppermute(x, 'row', [(i, i ^ 1) for i in range(n_row)])  13.3 us
    ppermute x7, waiting for transfers between devices, over_high(): lax.ppermute(x, 'row', [(i, (i // 2 ^ k) * 2 + i % 2) for i in range(n_ro...  11.6 us
    ppermute x7, starting transfers between devices, up(): return lax.ppermute(x, 'row', [(i, (i + 2) % n_row) for i in range(n_row)])  10.4 us
    ppermute x7, waiting for transfers between devices, up(): return lax.ppermute(x, 'row', [(i, (i + 2) % n_row) for i in range(n_row)])  10.2 us
    ppermute x11, waiting for transfers between devices, over_low(): return lax.ppermute(x, 'row', [(i, i ^ 1) for i in range(n_row)])  9.07 us
    ppermute x7, starting transfers between devices, over_high(): lax.ppermute(x, 'row', [(i, (i // 2 ^ k) * 2 + i % 2) for i in range(n_ro...  8.06 us
    ppermute x14, starting transfers between devices, over_col(): return lax.ppermute(x, 'col', [(i, i ^ k) for i in range(n_col)])  7.57 us
  transfers between devices with their start and end apart: 39, of which 19 were waited for; matrix products, arithmetic and copies ran while one was open for 3% of the time, Pallas kernels for 37%

profile of v5, /device:TPU:0, one launch (start us, length us, event | category | flops | bytes accessed | tf_op | source)
XLA Modules:
  0.0 133.1 jit_solution(8616284204646470230)
XLA Ops:
  0.5 1.1 dynamic-slice_bitcast_fusion.2
  1.7 2.9 %collective-permute-start.2 = (bf16[40,1280]{1,0:T(8,128)(2,1)S(1)}, bf16[40,1280]{1,0:T(8,128)(2,1)S(1)}, u32[]{:S(2)}, u32[]{:S(2)}) collective-permute-start(bf16[40,1280]{1,0:T(8,128)(2,1)S(1)} %get-tuple-element.189), channel_id=1, source_target_pairs={{0,2},{1,3},{2,0},{3,1},{4,6},{5,7},{6,4},{7,5},{8,10},{9,11},{10,... | collective-permute-start | bytes 307208 | tf_op jit(solution)/shard_map/ppermute | solution.py:299
  6.3 1.0 half_slab.2
  7.2 1.4 %dynamic-slice_bitcast_fusion = bf16[3,1,160,1280]{3,2,1,0:T(8,128)(2,1)S(1)} fusion(bf16[3,1,2,160,1280]{4,3,2,1,0:T(8,128)(2,1)} %bitcast.53, s32[]{:T(128)S(6)} %select_n.55), kind=kLoop, calls=%fused_computation | loop fusion | bytes 2457604 | tf_op jit(solution)/shard_map/jit(dynamic_index_in_dim)/squeeze | solution.py:320
  8.6 1.8 %collective-permute-start.9 = (bf16[3,1,160,1280]{3,2,1,0:T(8,128)(2,1)S(1)}, bf16[3,1,160,1280]{3,2,1,0:T(8,128)(2,1)S(1)}, u32[]{:S(2)}, u32[]{:S(2)}) collective-permute-start(bf16[3,1,160,1280]{3,2,1,0:T(8,128)(2,1)S(1)} %dynamic-slice_bitcast_fusion), channel_id=1, source_target_pairs={{0,2},{1,3},{2,0},{3,1},{4,6},{5,7},{6,4},{7,5},{8,10},{9,11},{10,... | collective-permute-start | bytes 3686408 | tf_op jit(solution)/shard_map/ppermute | solution.py:299
  10.5 1.6 %collective-permute-start.6 = (bf16[80,1280]{1,0:T(8,128)(2,1)S(1)}, bf16[80,1280]{1,0:T(8,128)(2,1)S(1)}, u32[]{:S(2)}, u32[]{:S(2)}) collective-permute-start(bf16[80,1280]{1,0:T(8,128)(2,1)S(1)} %bitcast.56), channel_id=1, source_target_pairs={{0,8},{4,12},{8,16},{12,20},{16,24},{20,28},{24,0},{28,4},{1,9},{5... | collective-permute-start | bytes 614408 | tf_op jit(solution)/shard_map/ppermute | solution.py:308
  12.1 1.5 %collective-permute-start.7 = (bf16[80,1280]{1,0:T(8,128)(2,1)S(1)}, bf16[80,1280]{1,0:T(8,128)(2,1)S(1)}, u32[]{:S(2)}, u32[]{:S(2)}) collective-permute-start(bf16[80,1280]{1,0:T(8,128)(2,1)S(1)} %bitcast.57), channel_id=1, source_target_pairs={{0,4},{4,0},{8,12},{12,8},{16,20},{20,16},{24,28},{28,24},{1,5},{5... | collective-permute-start | bytes 614408 | tf_op jit(solution)/shard_map/ppermute | solution.py:302
  13.7 1.0 half_slab.3
  14.7 1.6 %collective-permute-start.4 = (bf16[80,1280]{1,0:T(8,128)(2,1)S(1)}, bf16[80,1280]{1,0:T(8,128)(2,1)S(1)}, u32[]{:S(2)}, u32[]{:S(2)}) collective-permute-start(bf16[80,1280]{1,0:T(8,128)(2,1)S(1)} %bitcast.59), channel_id=1, source_target_pairs={{0,8},{4,12},{8,16},{12,20},{16,24},{20,28},{24,0},{28,4},{1,9},{5... | collective-permute-start | bytes 614408 | tf_op jit(solution)/shard_map/ppermute | solution.py:308
  16.9 2.8 %place_pieces.1 = (bf16[3,4,160,1280]{3,2,1,0:T(8,128)(2,1)S(1)}, bf16[3,4,160,1280]{3,2,1,0:T(8,128)(2,1)S(1)}) custom-call(s32[4]{0:T(128)S(1)} %pad_add_fusion.ids, s32[20,20]{1,0:T(8,128)S(1)} %copy-done.2, bf16[3,1,2,160,1280]{4,3,2,1,0:T(8,128)(2,1)S(1)} %bitcast.54, bf16[3,1,2,160,1280]{4,3,2,1,0:T(8,128)(2,1)} %bitcast.11.refs_1_), custom_call_target="tpu_custom_call" | custom-call | tf_op jit(solution)/shard_map/place_pieces/pallas_call | solution.py:40
  20.3 1.1 collective-permute-start.10
  21.4 1.9 %collective-permute-start.11 = (bf16[80,1280]{1,0:T(8,128)(2,1)S(1)}, bf16[80,1280]{1,0:T(8,128)(2,1)S(1)}, u32[]{:S(2)}, u32[]{:S(2)}) collective-permute-start(bf16[80,1280]{1,0:T(8,128)(2,1)S(1)} %collective-permute-done.6.refs_1_), channel_id=1, source_target_pairs={{0,4},{4,0},{8,12},{12,8},{16,20},{20,16},{24,28},{28,24},{1,5},{5... | collective-permute-start | bytes 614408 | tf_op jit(solution)/shard_map/ppermute | solution.py:302
  23.3 1.0 collective-permute-done.4.refs_5_
  24.3 1.6 %collective-permute-start.14 = (bf16[80,1280]{1,0:T(8,128)(2,1)S(1)}, bf16[80,1280]{1,0:T(8,128)(2,1)S(1)}, u32[]{:S(2)}, u32[]{:S(2)}) collective-permute-start(bf16[80,1280]{1,0:T(8,128)(2,1)S(1)} %collective-permute-done.4.refs_5_), channel_id=1, source_target_pairs={{0,8},{4,12},{8,16},{12,20},{16,24},{20,28},{24,0},{28,4},{1,9},{5... | collective-permute-start | bytes 614408 | tf_op jit(solution)/shard_map/ppermute | solution.py:308
  25.9 1.6 %collective-permute-start.15 = (bf16[80,1280]{1,0:T(8,128)(2,1)S(1)}, bf16[80,1280]{1,0:T(8,128)(2,1)S(1)}, u32[]{:S(2)}, u32[]{:S(2)}) collective-permute-start(bf16[80,1280]{1,0:T(8,128)(2,1)S(1)} %collective-permute-done.4.refs_5_), channel_id=1, source_target_pairs={{0,4},{4,0},{8,12},{12,8},{16,20},{20,16},{24,28},{28,24},{1,5},{5... | collective-permute-start | bytes 614408 | tf_op jit(solution)/shard_map/ppermute | solution.py:302
  27.6 1.3 collective-permute-done.10.refs_2_
  29.1 1.7 %collective-permute-start.12 = (bf16[80,1280]{1,0:T(8,128)(2,1)S(1)}, bf16[80,1280]{1,0:T(8,128)(2,1)S(1)}, u32[]{:S(2)}, u32[]{:S(2)}) collective-permute-start(bf16[80,1280]{1,0:T(8,128)(2,1)S(1)} %collective-permute-done.10.refs_2_), channel_id=1, source_target_pairs={{0,8},{4,12},{8,16},{12,20},{16,24},{20,28},{24,0},{28,4},{1,9},{5... | collective-permute-start | bytes 614408 | tf_op jit(solution)/shard_map/ppermute | solution.py:308
  30.8 1.5 %collective-permute-start.13 = (bf16[80,1280]{1,0:T(8,128)(2,1)S(1)}, bf16[80,1280]{1,0:T(8,128)(2,1)S(1)}, u32[]{:S(2)}, u32[]{:S(2)}) collective-permute-start(bf16[80,1280]{1,0:T(8,128)(2,1)S(1)} %collective-permute-done.10.refs_2_), channel_id=1, source_target_pairs={{0,4},{4,0},{8,12},{12,8},{16,20},{20,16},{24,28},{28,24},{1,5},{5... | collective-permute-start | bytes 614408 | tf_op jit(solution)/shard_map/ppermute | solution.py:302
  32.3 1.8 %collective-permute-done.14.refs_6_ = bf16[80,1280]{1,0:T(8,128)(2,1)S(1)} collective-permute-done((bf16[80,1280]{1,0:T(8,128)(2,1)S(1)}, bf16[80,1280]{1,0:T(8,128)(2,1)S(1)}, u32[]{:S(2)}, u32[]{:S(2)}) %collective-permute-start.14) | collective-permute-done | bytes 204832 | tf_op jit(solution)/shard_map/ppermute | solution.py:308
  34.1 1.5 %collective-permute-start.17 = (bf16[80,1280]{1,0:T(8,128)(2,1)S(1)}, bf16[80,1280]{1,0:T(8,128)(2,1)S(1)}, u32[]{:S(2)}, u32[]{:S(2)}) collective-permute-start(bf16[80,1280]{1,0:T(8,128)(2,1)S(1)} %collective-permute-done.14.refs_6_), channel_id=1, source_target_pairs={{0,4},{4,0},{8,12},{12,8},{16,20},{20,16},{24,28},{28,24},{1,5},{5... | collective-permute-start | bytes 614408 | tf_op jit(solution)/shard_map/ppermute | solution.py:302
  35.7 1.1 collective-permute-start.16
  38.8 2.2 %collective-permute-done.17.refs_14_ = bf16[80,1280]{1,0:T(8,128)(2,1)S(1)} collective-permute-done((bf16[80,1280]{1,0:T(8,128)(2,1)S(1)}, bf16[80,1280]{1,0:T(8,128)(2,1)S(1)}, u32[]{:S(2)}, u32[]{:S(2)}) %collective-permute-start.17) | collective-permute-done | bytes 204832 | tf_op jit(solution)/shard_map/ppermute | solution.py:302
  40.9 1.6 %collective-permute-start.22 = (bf16[80,1280]{1,0:T(8,128)(2,1)S(1)}, bf16[80,1280]{1,0:T(8,128)(2,1)S(1)}, u32[]{:S(2)}, u32[]{:S(2)}) collective-permute-start(bf16[80,1280]{1,0:T(8,128)(2,1)S(1)} %collective-permute-done.17.refs_14_), channel_id=1, source_target_pairs={{0,8},{4,12},{8,16},{12,20},{16,24},{20,28},{24,0},{28,4},{1,9},{5... | collective-permute-start | bytes 614408 | tf_op jit(solution)/shard_map/ppermute | solution.py:308
  44.0 4.5 %collective-permute-done.22.refs_15_ = bf16[80,1280]{1,0:T(8,128)(2,1)S(1)} collective-permute-done((bf16[80,1280]{1,0:T(8,128)(2,1)S(1)}, bf16[80,1280]{1,0:T(8,128)(2,1)S(1)}, u32[]{:S(2)}, u32[]{:S(2)}) %collective-permute-start.22) | collective-permute-done | bytes 204832 | tf_op jit(solution)/shard_map/ppermute | solution.py:308
  48.5 1.5 %collective-permute-start.21 = (bf16[80,1280]{1,0:T(8,128)(2,1)S(1)}, bf16[80,1280]{1,0:T(8,128)(2,1)S(1)}, u32[]{:S(2)}, u32[]{:S(2)}) collective-permute-start(bf16[80,1280]{1,0:T(8,128)(2,1)S(1)} %collective-permute-done.12.refs_3_), channel_id=1, source_target_pairs={{0,4},{4,0},{8,12},{12,8},{16,20},{20,16},{24,28},{28,24},{1,5},{5... | collective-permute-start | bytes 614408 | tf_op jit(solution)/shard_map/ppermute | solution.py:302
  51.0 3.3 %collective-permute-done.21.refs_11_ = bf16[80,1280]{1,0:T(8,128)(2,1)S(1)} collective-permute-done((bf16[80,1280]{1,0:T(8,128)(2,1)S(1)}, bf16[80,1280]{1,0:T(8,128)(2,1)S(1)}, u32[]{:S(2)}, u32[]{:S(2)}) %collective-permute-start.21) | collective-permute-done | bytes 204832 | tf_op jit(solution)/shard_map/ppermute | solution.py:302
  55.1 0.9 place_parts.1.refs_0_
  56.0 5.3 %send_part.4 = (bf16[768,1280]{1,0:T(8,128)(2,1)S(1)}, bf16[4,160,256]{2,1,0:T(8,128)(2,1)S(1)}, bf16[640,6]{1,0:T(8,128)(2,1)S(1)}, bf16[640,6]{1,0:T(8,128)(2,1)S(1)}) custom-call(s32[4]{0:T(128)S(1)} %pad_add_fusion.ids, bf16[3,4,160,1280]{3,2,1,0:T(8,128)(2,1)S(1)} %place_parts.1.refs_0_, bf16[3,4,160,1280]{3,2,1,0:T(8,128)(2,1)S(1)} %get-tuple-element.138.refs_1_, ...), custom_call_target="tpu_custom_call" | custom-call | tf_op jit(solution)/shard_map/send_part/pallas_call | solution.py:40
  61.3 1.6 %collective-permute-start.23 = (bf16[4,160,256]{2,1,0:T(8,128)(2,1)S(1)}, bf16[4,160,256]{2,1,0:T(8,128)(2,1)S(1)}, u32[]{:S(2)}, u32[]{:S(2)}) collective-permute-start(bf16[4,160,256]{2,1,0:T(8,128)(2,1)S(1)} %get-tuple-element.133), channel_id=1, source_target_pairs={{0,4},{4,0},{8,12},{12,8},{16,20},{20,16},{24,28},{28,24},{1,5},{5... | collective-permute-start | bytes 983048 | tf_op jit(solution)/shard_map/ppermute | solution.py:302
  62.9 7.8 %send_part.5 = (bf16[1152,1280]{1,0:T(8,128)(2,1)S(1)}, bf16[4,160,384]{2,1,0:T(8,128)(2,1)S(1)}) custom-call(s32[4]{0:T(128)S(1)} %pad_add_fusion.ids, bf16[3,4,160,1280]{3,2,1,0:T(8,128)(2,1)S(1)} %place_parts.1.refs_0_, bf16[3,4,160,1280]{3,2,1,0:T(8,128)(2,1)S(1)} %get-tuple-element.138.refs_1_, bf16[1280,1280]{1,0:T(8,128)(2,1)S(1)} %bitcast.50, ...), custom_call_target="tpu_custom_call" | custom-call | tf_op jit(solution)/shard_map/send_part/pallas_call | solution.py:40
  72.3 1.4 %collective-permute-done.24.refs_0_ = bf16[3,1,160,1280]{3,2,1,0:T(8,128)(2,1)S(1)} collective-permute-done((bf16[3,1,160,1280]{3,2,1,0:T(8,128)(2,1)S(1)}, bf16[3,1,160,1280]{3,2,1,0:T(8,128)(2,1)S(1)}, u32[]{:S(2)}, u32[]{:S(2)}) %collective-permute-start.24) | collective-permute-done | bytes 1228832 | tf_op jit(solution)/shard_map/ppermute | solution.py:299
  73.6 0.9 place_halves.5.refs_1_
  74.6 7.6 %send_part.6 = (bf16[1152,1280]{1,0:T(8,128)(2,1)S(1)}, bf16[4,160,384]{2,1,0:T(8,128)(2,1)S(1)}) custom-call(s32[4]{0:T(128)S(1)} %pad_add_fusion.ids, bf16[3,4,160,1280]{3,2,1,0:T(8,128)(2,1)S(1)} %place_parts.1.refs_0_, bf16[3,4,160,1280]{3,2,1,0:T(8,128)(2,1)S(1)} %place_halves.5.refs_1_, bf16[1280,1280]{1,0:T(8,128)(2,1)S(1)} %bitcast.51, ...), custom_call_target="tpu_custom_call" | custom-call | tf_op jit(solution)/shard_map/send_part/pallas_call | solution.py:40
  82.8 1.6 %collective-permute-done.25.refs_7_ = bf16[4,160,384]{2,1,0:T(8,128)(2,1)S(1)} collective-permute-done((bf16[4,160,384]{2,1,0:T(8,128)(2,1)S(1)}, bf16[4,160,384]{2,1,0:T(8,128)(2,1)S(1)}, u32[]{:S(2)}, u32[]{:S(2)}) %collective-permute-start.25) | collective-permute-done | bytes 491552 | tf_op jit(solution)/shard_map/ppermute | solution.py:302
  84.4 5.0 %keep_part.3 = (f32[2,160,640]{2,1,0:T(8,128)S(1)}, bf16[2,160,640]{2,1,0:T(8,128)(2,1)S(1)}) custom-call(s32[4]{0:T(128)S(1)} %pad_add_fusion.ids, bf16[3,640,1280]{2,1,0:T(8,128)(2,1)S(1)} %bitcast.46, bf16[640,6]{1,0:T(8,128)(2,1)S(1)} %get-tuple-element.144.refs_1_, bf16[768,1280]{1,0:T(8,128)(2,1)S(1)} %get-tuple-element.145.refs_2_, ...), custom_call_target="tpu_custom_call" | custom-call | tf_op jit(solution)/shard_map/keep_part/pallas_call | solution.py:40
  89.5 5.1 %send_part.7 = (bf16[768,1280]{1,0:T(8,128)(2,1)S(1)}, bf16[4,160,256]{2,1,0:T(8,128)(2,1)S(1)}) custom-call(s32[4]{0:T(128)S(1)} %pad_add_fusion.ids, bf16[3,4,160,1280]{3,2,1,0:T(8,128)(2,1)S(1)} %place_parts.1.refs_0_, bf16[3,4,160,1280]{3,2,1,0:T(8,128)(2,1)S(1)} %place_halves.5.refs_1_, bf16[1280,1280]{1,0:T(8,128)(2,1)S(1)} %bitcast.52, ...), custom_call_target="tpu_custom_call" | custom-call | tf_op jit(solution)/shard_map/send_part/pallas_call | solution.py:40
  95.5 3.5 %keep_part.4 = (f32[2,160,384]{2,1,0:T(8,128)S(1)}, bf16[2,160,384]{2,1,0:T(8,128)(2,1)S(1)}) custom-call(s32[4]{0:T(128)S(1)} %pad_add_fusion.ids, bf16[3,640,1280]{2,1,0:T(8,128)(2,1)S(1)} %bitcast.47, bf16[640,6]{1,0:T(8,128)(2,1)S(1)} %get-tuple-element.144.refs_1_, bf16[1152,1280]{1,0:T(8,128)(2,1)S(1)} %get-tuple-element.155.refs_2_, ...), custom_call_target="tpu_custom_call" | custom-call | tf_op jit(solution)/shard_map/keep_part/pallas_call | solution.py:40
  99.0 1.2 collective-permute-start.28
  101.4 1.1 collective-permute-start.30
  102.5 6.7 %collective-permute-done.28.got = bf16[2,160,384]{2,1,0:T(8,128)(2,1)S(1)} collective-permute-done((bf16[2,160,384]{2,1,0:T(8,128)(2,1)S(1)}, bf16[2,160,384]{2,1,0:T(8,128)(2,1)S(1)}, u32[]{:S(2)}, u32[]{:S(2)}) %collective-permute-start.28) | collective-permute-done | bytes 245792 | tf_op jit(solution)/shard_map/ppermute | solution.py:305
  109.8 1.2 collective-permute-start.32
  111.0 2.1 %keep_part.5 = (f32[160,256]{1,0:T(8,128)S(1)}, bf16[160,256]{1,0:T(8,128)(2,1)S(1)}, bf16[160,256]{1,0:T(8,128)(2,1)S(1)}, bf16[160,256]{1,0:T(8,128)(2,1)S(1)}) custom-call(s32[4]{0:T(128)S(1)} %pad_add_fusion.ids, bf16[3,640,1280]{2,1,0:T(8,128)(2,1)S(1)} %bitcast.48, bf16[640,6]{1,0:T(8,128)(2,1)S(1)} %get-tuple-element.144.refs_1_, ...), custom_call_target="tpu_custom_call" | custom-call | tf_op jit(solution)/shard_map/keep_part/pallas_call | solution.py:40
  113.1 2.9 %collective-permute-done.30 = bf16[1,160,640]{2,1,0:T(8,128)(2,1)S(1)} collective-permute-done((bf16[1,160,640]{2,1,0:T(8,128)(2,1)S(1)}, bf16[1,160,640]{2,1,0:T(8,128)(2,1)S(1)}, u32[]{:S(2)}, u32[]{:S(2)}) %collective-permute-start.30) | collective-permute-done | bytes 204832 | tf_op jit(solution)/shard_map/ppermute | solution.py:305
  116.7 4.3 %collective-permute-start.37 = (bf16[160,256]{1,0:T(8,128)(2,1)S(1)}, bf16[160,256]{1,0:T(8,128)(2,1)S(1)}, u32[]{:S(2)}, u32[]{:S(2)}) collective-permute-start(bf16[160,256]{1,0:T(8,128)(2,1)S(1)} %get-tuple-element.180), channel_id=1, source_target_pairs={{0,24},{4,28},{8,16},{12,20},{16,8},{20,12},{24,0},{28,4},{1,25},{... | collective-permute-start | bytes 245768 | tf_op jit(solution)/shard_map/ppermute | solution.py:305
  122.4 2.0 %collective-permute-done.37.refs_2_ = bf16[160,256]{1,0:T(8,128)(2,1)S(1)} collective-permute-done((bf16[160,256]{1,0:T(8,128)(2,1)S(1)}, bf16[160,256]{1,0:T(8,128)(2,1)S(1)}, u32[]{:S(2)}, u32[]{:S(2)}) %collective-permute-start.37) | collective-permute-done | bytes 81952 | tf_op jit(solution)/shard_map/ppermute | solution.py:305
  125.1 2.8 %collective-permute-done.33.refs_2_ = f32[160,384]{1,0:T(8,128)S(1)} collective-permute-done((f32[160,384]{1,0:T(8,128)S(1)}, f32[160,384]{1,0:T(8,128)S(1)}, u32[]{:S(2)}, u32[]{:S(2)}) %collective-permute-start.33) | collective-permute-done | bytes 245792 | tf_op jit(solution)/shard_map/ppermute | solution.py:299
  128.0 3.3 %collective-permute-done.38.refs_4_ = f32[160,256]{1,0:T(8,128)S(1)} collective-permute-done((f32[160,256]{1,0:T(8,128)S(1)}, f32[160,256]{1,0:T(8,128)S(1)}, u32[]{:S(2)}, u32[]{:S(2)}) %collective-permute-start.38) | collective-permute-done | bytes 163872 | tf_op jit(solution)/shard_map/ppermute | solution.py:299
  131.4 1.5 %finish.1 = f32[4,160,320]{2,1,0:T(8,128)} custom-call(s32[4]{0:T(128)S(1)} %pad_add_fusion.ids, f32[160,320]{1,0:T(8,128)S(1)} %collective-permute-done.31.refs_0_, f32[160,320]{1,0:T(8,128)S(1)} %get-tuple-element.184.refs_1_, f32[160,384]{1,0:T(8,128)S(1)} %collective-permute-done.33.refs_2_, f32[160,64]{1,0:T(8,128)S(1)} %collective-permute-done.34.refs_3_, ...), custom_call_target="tpu_custom_call" | custom-call | tf_op jit(solution)/shard_map/finish/pallas_call | solution.py:40
  (81 shorter events, 16.7 us)
Async XLA Ops:
  0.0 5.4 %copy-start = (bf16[3,160,1280]{2,1,0:T(8,128)(2,1)S(1)}, bf16[3,160,1280]{2,1,0:T(8,128)(2,1)}, u32[]{:S(2)}) copy-start(bf16[3,160,1280]{2,1,0:T(8,128)(2,1)} %param.8) | copy-start | bytes 3686404
  0.0 6.1 %copy-start.3 = (s32[4,20,20]{2,0,1:T(4,128)S(1)}, s32[4,20,20]{2,0,1:T(4,128)}, u32[]{:S(2)}) copy-start(s32[4,20,20]{2,0,1:T(4,128)} %param.10) | copy-start | bytes 19204
  0.0 6.2 %collective-permute-start = (bf16[3,320,1280]{2,1,0:T(8,128)(2,1)}, bf16[3,320,1280]{2,1,0:T(8,128)(2,1)}, u32[]{:S(2)}, u32[]{:S(2)}) collective-permute-start(bf16[3,320,1280]{2,1,0:T(8,128)(2,1)} %param.7), channel_id=1, source_target_pairs={{0,1},{1,0},{2,3},{3,2},{4,5},{5,4},{6,7},{7,6},{8,9},{9,8},{10,11... | collective-permute-start | bytes 7372808 | tf_op jit(solution)/shard_map/ppermute | solution.py:299
  1.5 4.7 %collective-permute-start.1 = (bf16[40,1280]{1,0:T(8,128)(2,1)S(1)}, bf16[40,1280]{1,0:T(8,128)(2,1)S(1)}, u32[]{:S(2)}, u32[]{:S(2)}) collective-permute-start(bf16[40,1280]{1,0:T(8,128)(2,1)S(1)} %get-tuple-element.188), channel_id=1, source_target_pairs={{0,1},{1,0},{2,3},{3,2},{4,5},{5,4},{6,7},{7,6},{8,9},{9,8},{10,11... | collective-permute-start | bytes 307208 | tf_op jit(solution)/shard_map/ppermute | solution.py:299
  1.7 8.7 %collective-permute-start.2 = (bf16[40,1280]{1,0:T(8,128)(2,1)S(1)}, bf16[40,1280]{1,0:T(8,128)(2,1)S(1)}, u32[]{:S(2)}, u32[]{:S(2)}) collective-permute-start(bf16[40,1280]{1,0:T(8,128)(2,1)S(1)} %get-tuple-element.189), channel_id=1, source_target_pairs={{0,2},{1,3},{2,0},{3,1},{4,6},{5,7},{6,4},{7,5},{8,10},{9,11},{10,... | collective-permute-start | bytes 307208 | tf_op jit(solution)/shard_map/ppermute | solution.py:299
  4.6 5.9 %collective-permute-start.3 = (bf16[40,1280]{1,0:T(8,128)(2,1)S(1)}, bf16[40,1280]{1,0:T(8,128)(2,1)S(1)}, u32[]{:S(2)}, u32[]{:S(2)}) collective-permute-start(bf16[40,1280]{1,0:T(8,128)(2,1)S(1)} %get-tuple-element.186), channel_id=1, source_target_pairs={{0,3},{1,2},{2,1},{3,0},{4,7},{5,6},{6,5},{7,4},{8,11},{9,10},{10,... | collective-permute-start | bytes 307208 | tf_op jit(solution)/shard_map/ppermute | solution.py:299
  5.7 11.1 %copy-start.2 = (s32[20,20]{1,0:T(8,128)S(1)}, s32[20,20]{1,0:T(8,128)}, u32[]{:S(2)}) copy-start(s32[20,20]{1,0:T(8,128)} %tiles.9) | copy-start | bytes 4804
  5.9 11.0 %copy-start.1 = (bf16[3,320,1280]{2,1,0:T(8,128)(2,1)S(1)}, bf16[3,320,1280]{2,1,0:T(8,128)(2,1)}, u32[]{:S(2)}) copy-start(bf16[3,320,1280]{2,1,0:T(8,128)(2,1)} %param.7) | copy-start | bytes 7372804
  8.6 34.6 %collective-permute-start.9 = (bf16[3,1,160,1280]{3,2,1,0:T(8,128)(2,1)S(1)}, bf16[3,1,160,1280]{3,2,1,0:T(8,128)(2,1)S(1)}, u32[]{:S(2)}, u32[]{:S(2)}) collective-permute-start(bf16[3,1,160,1280]{3,2,1,0:T(8,128)(2,1)S(1)} %dynamic-slice_bitcast_fusion), channel_id=1, source_target_pairs={{0,2},{1,3},{2,0},{3,1},{4,6},{5,7},{6,4},{7,5},{8,10},{9,11},{10,... | collective-permute-start | bytes 3686408 | tf_op jit(solution)/shard_map/ppermute | solution.py:299
  10.5 9.8 %collective-permute-start.6 = (bf16[80,1280]{1,0:T(8,128)(2,1)S(1)}, bf16[80,1280]{1,0:T(8,128)(2,1)S(1)}, u32[]{:S(2)}, u32[]{:S(2)}) collective-permute-start(bf16[80,1280]{1,0:T(8,128)(2,1)S(1)} %bitcast.56), channel_id=1, source_target_pairs={{0,8},{4,12},{8,16},{12,20},{16,24},{20,28},{24,0},{28,4},{1,9},{5... | collective-permute-start | bytes 614408 | tf_op jit(solution)/shard_map/ppermute | solution.py:308
  12.1 8.1 %collective-permute-start.7 = (bf16[80,1280]{1,0:T(8,128)(2,1)S(1)}, bf16[80,1280]{1,0:T(8,128)(2,1)S(1)}, u32[]{:S(2)}, u32[]{:S(2)}) collective-permute-start(bf16[80,1280]{1,0:T(8,128)(2,1)S(1)} %bitcast.57), channel_id=1, source_target_pairs={{0,4},{4,0},{8,12},{12,8},{16,20},{20,16},{24,28},{28,24},{1,5},{5... | collective-permute-start | bytes 614408 | tf_op jit(solution)/shard_map/ppermute | solution.py:302
  14.7 9.6 %collective-permute-start.4 = (bf16[80,1280]{1,0:T(8,128)(2,1)S(1)}, bf16[80,1280]{1,0:T(8,128)(2,1)S(1)}, u32[]{:S(2)}, u32[]{:S(2)}) collective-permute-start(bf16[80,1280]{1,0:T(8,128)(2,1)S(1)} %bitcast.59), channel_id=1, source_target_pairs={{0,8},{4,12},{8,16},{12,20},{16,24},{20,28},{24,0},{28,4},{1,9},{5... | collective-permute-start | bytes 614408 | tf_op jit(solution)/shard_map/ppermute | solution.py:308
  16.3 8.0 %collective-permute-start.5 = (bf16[80,1280]{1,0:T(8,128)(2,1)S(1)}, bf16[80,1280]{1,0:T(8,128)(2,1)S(1)}, u32[]{:S(2)}, u32[]{:S(2)}) collective-permute-start(bf16[80,1280]{1,0:T(8,128)(2,1)S(1)} %bitcast.60), channel_id=1, source_target_pairs={{0,4},{4,0},{8,12},{12,8},{16,20},{20,16},{24,28},{28,24},{1,5},{5... | collective-permute-start | bytes 614408 | tf_op jit(solution)/shard_map/ppermute | solution.py:302
  20.3 8.5 %collective-permute-start.10 = (bf16[80,1280]{1,0:T(8,128)(2,1)S(1)}, bf16[80,1280]{1,0:T(8,128)(2,1)S(1)}, u32[]{:S(2)}, u32[]{:S(2)}) collective-permute-start(bf16[80,1280]{1,0:T(8,128)(2,1)S(1)} %collective-permute-done.6.refs_1_), channel_id=1, source_target_pairs={{0,8},{4,12},{8,16},{12,20},{16,24},{20,28},{24,0},{28,4},{1,9},{5... | collective-permute-start | bytes 614408 | tf_op jit(solution)/shard_map/ppermute | solution.py:308
  21.4 7.7 %collective-permute-start.11 = (bf16[80,1280]{1,0:T(8,128)(2,1)S(1)}, bf16[80,1280]{1,0:T(8,128)(2,1)S(1)}, u32[]{:S(2)}, u32[]{:S(2)}) collective-permute-start(bf16[80,1280]{1,0:T(8,128)(2,1)S(1)} %collective-permute-done.6.refs_1_), channel_id=1, source_target_pairs={{0,4},{4,0},{8,12},{12,8},{16,20},{20,16},{24,28},{28,24},{1,5},{5... | collective-permute-start | bytes 614408 | tf_op jit(solution)/shard_map/ppermute | solution.py:302
  24.3 9.8 %collective-permute-start.14 = (bf16[80,1280]{1,0:T(8,128)(2,1)S(1)}, bf16[80,1280]{1,0:T(8,128)(2,1)S(1)}, u32[]{:S(2)}, u32[]{:S(2)}) collective-permute-start(bf16[80,1280]{1,0:T(8,128)(2,1)S(1)} %collective-permute-done.4.refs_5_), channel_id=1, source_target_pairs={{0,8},{4,12},{8,16},{12,20},{16,24},{20,28},{24,0},{28,4},{1,9},{5... | collective-permute-start | bytes 614408 | tf_op jit(solution)/shard_map/ppermute | solution.py:308
  25.9 8.2 %collective-permute-start.15 = (bf16[80,1280]{1,0:T(8,128)(2,1)S(1)}, bf16[80,1280]{1,0:T(8,128)(2,1)S(1)}, u32[]{:S(2)}, u32[]{:S(2)}) collective-permute-start(bf16[80,1280]{1,0:T(8,128)(2,1)S(1)} %collective-permute-done.4.refs_5_), channel_id=1, source_target_pairs={{0,4},{4,0},{8,12},{12,8},{16,20},{20,16},{24,28},{28,24},{1,5},{5... | collective-permute-start | bytes 614408 | tf_op jit(solution)/shard_map/ppermute | solution.py:302
  29.1 8.0 %collective-permute-start.12 = (bf16[80,1280]{1,0:T(8,128)(2,1)S(1)}, bf16[80,1280]{1,0:T(8,128)(2,1)S(1)}, u32[]{:S(2)}, u32[]{:S(2)}) collective-permute-start(bf16[80,1280]{1,0:T(8,128)(2,1)S(1)} %collective-permute-done.10.refs_2_), channel_id=1, source_target_pairs={{0,8},{4,12},{8,16},{12,20},{16,24},{20,28},{24,0},{28,4},{1,9},{5... | collective-permute-start | bytes 614408 | tf_op jit(solution)/shard_map/ppermute | solution.py:308
  30.8 7.9 %collective-permute-start.13 = (bf16[80,1280]{1,0:T(8,128)(2,1)S(1)}, bf16[80,1280]{1,0:T(8,128)(2,1)S(1)}, u32[]{:S(2)}, u32[]{:S(2)}) collective-permute-start(bf16[80,1280]{1,0:T(8,128)(2,1)S(1)} %collective-permute-done.10.refs_2_), channel_id=1, source_target_pairs={{0,4},{4,0},{8,12},{12,8},{16,20},{20,16},{24,28},{28,24},{1,5},{5... | collective-permute-start | bytes 614408 | tf_op jit(solution)/shard_map/ppermute | solution.py:302
  34.1 6.8 %collective-permute-start.17 = (bf16[80,1280]{1,0:T(8,128)(2,1)S(1)}, bf16[80,1280]{1,0:T(8,128)(2,1)S(1)}, u32[]{:S(2)}, u32[]{:S(2)}) collective-permute-start(bf16[80,1280]{1,0:T(8,128)(2,1)S(1)} %collective-permute-done.14.refs_6_), channel_id=1, source_target_pairs={{0,4},{4,0},{8,12},{12,8},{16,20},{20,16},{24,28},{28,24},{1,5},{5... | collective-permute-start | bytes 614408 | tf_op jit(solution)/shard_map/ppermute | solution.py:302
  35.7 7.6 %collective-permute-start.16 = (bf16[80,1280]{1,0:T(8,128)(2,1)S(1)}, bf16[80,1280]{1,0:T(8,128)(2,1)S(1)}, u32[]{:S(2)}, u32[]{:S(2)}) collective-permute-start(bf16[80,1280]{1,0:T(8,128)(2,1)S(1)} %collective-permute-done.14.refs_6_), channel_id=1, source_target_pairs={{0,8},{4,12},{8,16},{12,20},{16,24},{20,28},{24,0},{28,4},{1,9},{5... | collective-permute-start | bytes 614408 | tf_op jit(solution)/shard_map/ppermute | solution.py:308
  37.1 33.5 %collective-permute-start.8 = (bf16[3,1,160,1280]{3,2,1,0:T(8,128)(2,1)S(1)}, bf16[3,1,160,1280]{3,2,1,0:T(8,128)(2,1)S(1)}, u32[]{:S(2)}, u32[]{:S(2)}) collective-permute-start(bf16[3,1,160,1280]{3,2,1,0:T(8,128)(2,1)S(1)} %dynamic-slice_bitcast_fusion.1), channel_id=1, source_target_pairs={{0,2},{1,3},{2,0},{3,1},{4,6},{5,7},{6,4},{7,5},{8,10},{9,11},{10,... | collective-permute-start | bytes 3686408 | tf_op jit(solution)/shard_map/ppermute | solution.py:299
  40.9 7.6 %collective-permute-start.22 = (bf16[80,1280]{1,0:T(8,128)(2,1)S(1)}, bf16[80,1280]{1,0:T(8,128)(2,1)S(1)}, u32[]{:S(2)}, u32[]{:S(2)}) collective-permute-start(bf16[80,1280]{1,0:T(8,128)(2,1)S(1)} %collective-permute-done.17.refs_14_), channel_id=1, source_target_pairs={{0,8},{4,12},{8,16},{12,20},{16,24},{20,28},{24,0},{28,4},{1,9},{5... | collective-permute-start | bytes 614408 | tf_op jit(solution)/shard_map/ppermute | solution.py:308
  43.3 11.7 %collective-permute-start.18 = (bf16[1,1,160,1280]{3,2,1,0:T(8,128)(2,1)S(1)}, bf16[1,1,160,1280]{3,2,1,0:T(8,128)(2,1)S(1)}, u32[]{:S(2)}, u32[]{:S(2)}) collective-permute-start(bf16[1,1,160,1280]{3,2,1,0:T(8,128)(2,1)S(1)} %get-tuple-element.183), channel_id=1, source_target_pairs={{0,1},{1,0},{2,3},{3,2},{4,5},{5,4},{6,7},{7,6},{8,9},{9,8},{10,11... | collective-permute-start | bytes 1228808 | tf_op jit(solution)/shard_map/ppermute | solution.py:299
  43.4 11.7 %collective-permute-start.19 = (bf16[1,1,160,1280]{3,2,1,0:T(8,128)(2,1)S(1)}, bf16[1,1,160,1280]{3,2,1,0:T(8,128)(2,1)S(1)}, u32[]{:S(2)}, u32[]{:S(2)}) collective-permute-start(bf16[1,1,160,1280]{3,2,1,0:T(8,128)(2,1)S(1)} %get-tuple-element.182), channel_id=1, source_target_pairs={{0,1},{1,0},{2,3},{3,2},{4,5},{5,4},{6,7},{7,6},{8,9},{9,8},{10,11... | collective-permute-start | bytes 1228808 | tf_op jit(solution)/shard_map/ppermute | solution.py:299
  43.9 11.2 %collective-permute-start.20 = (bf16[1,1,160,1280]{3,2,1,0:T(8,128)(2,1)S(1)}, bf16[1,1,160,1280]{3,2,1,0:T(8,128)(2,1)S(1)}, u32[]{:S(2)}, u32[]{:S(2)}) collective-permute-start(bf16[1,1,160,1280]{3,2,1,0:T(8,128)(2,1)S(1)} %get-tuple-element.181), channel_id=1, source_target_pairs={{0,1},{1,0},{2,3},{3,2},{4,5},{5,4},{6,7},{7,6},{8,9},{9,8},{10,11... | collective-permute-start | bytes 1228808 | tf_op jit(solution)/shard_map/ppermute | solution.py:299
  48.5 5.8 %collective-permute-start.21 = (bf16[80,1280]{1,0:T(8,128)(2,1)S(1)}, bf16[80,1280]{1,0:T(8,128)(2,1)S(1)}, u32[]{:S(2)}, u32[]{:S(2)}) collective-permute-start(bf16[80,1280]{1,0:T(8,128)(2,1)S(1)} %collective-permute-done.12.refs_3_), channel_id=1, source_target_pairs={{0,4},{4,0},{8,12},{12,8},{16,20},{20,16},{24,28},{28,24},{1,5},{5... | collective-permute-start | bytes 614408 | tf_op jit(solution)/shard_map/ppermute | solution.py:302
  61.3 9.3 %collective-permute-start.23 = (bf16[4,160,256]{2,1,0:T(8,128)(2,1)S(1)}, bf16[4,160,256]{2,1,0:T(8,128)(2,1)S(1)}, u32[]{:S(2)}, u32[]{:S(2)}) collective-permute-start(bf16[4,160,256]{2,1,0:T(8,128)(2,1)S(1)} %get-tuple-element.133), channel_id=1, source_target_pairs={{0,4},{4,0},{8,12},{12,8},{16,20},{20,16},{24,28},{28,24},{1,5},{5... | collective-permute-start | bytes 983048 | tf_op jit(solution)/shard_map/ppermute | solution.py:302
  70.7 3.0 %collective-permute-start.24 = (bf16[3,1,160,1280]{3,2,1,0:T(8,128)(2,1)S(1)}, bf16[3,1,160,1280]{3,2,1,0:T(8,128)(2,1)S(1)}, u32[]{:S(2)}, u32[]{:S(2)}) collective-permute-start(bf16[3,1,160,1280]{3,2,1,0:T(8,128)(2,1)S(1)} %collective-permute-done.8.refs_0_), channel_id=1, source_target_pairs={{0,1},{1,0},{2,3},{3,2},{4,5},{5,4},{6,7},{7,6},{8,9},{9,8},{10,11... | collective-permute-start | bytes 3686408 | tf_op jit(solution)/shard_map/ppermute | solution.py:299
  70.7 13.6 %collective-permute-start.25 = (bf16[4,160,384]{2,1,0:T(8,128)(2,1)S(1)}, bf16[4,160,384]{2,1,0:T(8,128)(2,1)S(1)}, u32[]{:S(2)}, u32[]{:S(2)}) collective-permute-start(bf16[4,160,384]{2,1,0:T(8,128)(2,1)S(1)} %get-tuple-element.148), channel_id=1, source_target_pairs={{0,4},{4,0},{8,12},{12,8},{16,20},{20,16},{24,28},{28,24},{1,5},{5... | collective-permute-start | bytes 1474568 | tf_op jit(solution)/shard_map/ppermute | solution.py:302
  82.2 13.3 %collective-permute-start.26 = (bf16[4,160,384]{2,1,0:T(8,128)(2,1)S(1)}, bf16[4,160,384]{2,1,0:T(8,128)(2,1)S(1)}, u32[]{:S(2)}, u32[]{:S(2)}) collective-permute-start(bf16[4,160,384]{2,1,0:T(8,128)(2,1)S(1)} %get-tuple-element.156), channel_id=1, source_target_pairs={{0,4},{4,0},{8,12},{12,8},{16,20},{20,16},{24,28},{28,24},{1,5},{5... | collective-permute-start | bytes 1474568 | tf_op jit(solution)/shard_map/ppermute | solution.py:302
  89.4 11.3 %collective-permute-start.27 = (bf16[2,160,640]{2,1,0:T(8,128)(2,1)S(1)}, bf16[2,160,640]{2,1,0:T(8,128)(2,1)S(1)}, u32[]{:S(2)}, u32[]{:S(2)}) collective-permute-start(bf16[2,160,640]{2,1,0:T(8,128)(2,1)S(1)} %get-tuple-element.160), channel_id=1, source_target_pairs={{0,8},{4,12},{8,0},{12,4},{16,24},{20,28},{24,16},{28,20},{1,9},{5... | collective-permute-start | bytes 1228808 | tf_op jit(solution)/shard_map/ppermute | solution.py:305
  99.0 10.2 %collective-permute-start.28 = (bf16[2,160,384]{2,1,0:T(8,128)(2,1)S(1)}, bf16[2,160,384]{2,1,0:T(8,128)(2,1)S(1)}, u32[]{:S(2)}, u32[]{:S(2)}) collective-permute-start(bf16[2,160,384]{2,1,0:T(8,128)(2,1)S(1)} %get-tuple-element.163), channel_id=1, source_target_pairs={{0,8},{4,12},{8,0},{12,4},{16,24},{20,28},{24,16},{28,20},{1,9},{5... | collective-permute-start | bytes 737288 | tf_op jit(solution)/shard_map/ppermute | solution.py:305
  100.2 10.8 %collective-permute-start.29 = (bf16[4,160,256]{2,1,0:T(8,128)(2,1)S(1)}, bf16[4,160,256]{2,1,0:T(8,128)(2,1)S(1)}, u32[]{:S(2)}, u32[]{:S(2)}) collective-permute-start(bf16[4,160,256]{2,1,0:T(8,128)(2,1)S(1)} %get-tuple-element.168), channel_id=1, source_target_pairs={{0,4},{4,0},{8,12},{12,8},{16,20},{20,16},{24,28},{28,24},{1,5},{5... | collective-permute-start | bytes 983048 | tf_op jit(solution)/shard_map/ppermute | solution.py:302
  101.4 14.6 %collective-permute-start.30 = (bf16[1,160,640]{2,1,0:T(8,128)(2,1)S(1)}, bf16[1,160,640]{2,1,0:T(8,128)(2,1)S(1)}, u32[]{:S(2)}, u32[]{:S(2)}) collective-permute-start(bf16[1,160,640]{2,1,0:T(8,128)(2,1)S(1)} %get-tuple-element.171), channel_id=1, source_target_pairs={{0,16},{4,20},{8,24},{12,28},{16,0},{20,4},{24,8},{28,12},{1,17},{... | collective-permute-start | bytes 614408 | tf_op jit(solution)/shard_map/ppermute | solution.py:305
  109.8 11.2 %collective-permute-start.32 = (bf16[1,160,384]{2,1,0:T(8,128)(2,1)S(1)}, bf16[1,160,384]{2,1,0:T(8,128)(2,1)S(1)}, u32[]{:S(2)}, u32[]{:S(2)}) collective-permute-start(bf16[1,160,384]{2,1,0:T(8,128)(2,1)S(1)} %get-tuple-element.175), channel_id=1, source_target_pairs={{0,16},{4,20},{8,24},{12,28},{16,0},{20,4},{24,8},{28,12},{1,17},{... | collective-permute-start | bytes 368648 | tf_op jit(solution)/shard_map/ppermute | solution.py:305
  116.6 5.8 %collective-permute-start.35 = (bf16[160,256]{1,0:T(8,128)(2,1)S(1)}, bf16[160,256]{1,0:T(8,128)(2,1)S(1)}, u32[]{:S(2)}, u32[]{:S(2)}) collective-permute-start(bf16[160,256]{1,0:T(8,128)(2,1)S(1)} %get-tuple-element.178), channel_id=1, source_target_pairs={{0,8},{4,12},{8,0},{12,4},{16,24},{20,28},{24,16},{28,20},{1,9},{5... | collective-permute-start | bytes 245768 | tf_op jit(solution)/shard_map/ppermute | solution.py:305
  116.6 5.7 %collective-permute-start.36 = (bf16[160,256]{1,0:T(8,128)(2,1)S(1)}, bf16[160,256]{1,0:T(8,128)(2,1)S(1)}, u32[]{:S(2)}, u32[]{:S(2)}) collective-permute-start(bf16[160,256]{1,0:T(8,128)(2,1)S(1)} %get-tuple-element.179), channel_id=1, source_target_pairs={{0,16},{4,20},{8,24},{12,28},{16,0},{20,4},{24,8},{28,12},{1,17},{... | collective-permute-start | bytes 245768 | tf_op jit(solution)/shard_map/ppermute | solution.py:305
  116.7 7.7 %collective-permute-start.37 = (bf16[160,256]{1,0:T(8,128)(2,1)S(1)}, bf16[160,256]{1,0:T(8,128)(2,1)S(1)}, u32[]{:S(2)}, u32[]{:S(2)}) collective-permute-start(bf16[160,256]{1,0:T(8,128)(2,1)S(1)} %get-tuple-element.180), channel_id=1, source_target_pairs={{0,24},{4,28},{8,16},{12,20},{16,8},{20,12},{24,0},{28,4},{1,25},{... | collective-permute-start | bytes 245768 | tf_op jit(solution)/shard_map/ppermute | solution.py:305
  121.6 6.3 %collective-permute-start.33 = (f32[160,384]{1,0:T(8,128)S(1)}, f32[160,384]{1,0:T(8,128)S(1)}, u32[]{:S(2)}, u32[]{:S(2)}) collective-permute-start(f32[160,384]{1,0:T(8,128)S(1)} %add_up.4), channel_id=1, source_target_pairs={{0,2},{1,3},{2,0},{3,1},{4,6},{5,7},{6,4},{7,5},{8,10},{9,11},{10,... | collective-permute-start | bytes 737288 | tf_op jit(solution)/shard_map/ppermute | solution.py:299
  122.3 5.7 %collective-permute-start.31 = (f32[160,320]{1,0:T(8,128)S(1)}, f32[160,320]{1,0:T(8,128)S(1)}, u32[]{:S(2)}, u32[]{:S(2)}) collective-permute-start(f32[160,320]{1,0:T(8,128)S(1)} %get-tuple-element.185), channel_id=1, source_target_pairs={{0,1},{1,0},{2,3},{3,2},{4,5},{5,4},{6,7},{7,6},{8,9},{9,8},{10,11... | collective-permute-start | bytes 614408 | tf_op jit(solution)/shard_map/ppermute | solution.py:299
  125.0 6.4 %collective-permute-start.38 = (f32[160,256]{1,0:T(8,128)S(1)}, f32[160,256]{1,0:T(8,128)S(1)}, u32[]{:S(2)}, u32[]{:S(2)}) collective-permute-start(f32[160,256]{1,0:T(8,128)S(1)} %add_up.5), channel_id=1, source_target_pairs={{0,3},{1,2},{2,1},{3,0},{4,7},{5,6},{6,5},{7,4},{8,11},{9,10},{10,... | collective-permute-start | bytes 491528 | tf_op jit(solution)/shard_map/ppermute | solution.py:299
  127.9 3.4 %collective-permute-start.34 = (f32[160,64]{1,0:T(8,128)S(1)}, f32[160,64]{1,0:T(8,128)S(1)}, u32[]{:S(2)}, u32[]{:S(2)}) collective-permute-start(f32[160,64]{1,0:T(8,128)S(1)} %slice.51), channel_id=1, source_target_pairs={{0,1},{1,0},{2,3},{3,2},{4,5},{5,4},{6,7},{7,6},{8,9},{9,8},{10,11... | collective-permute-start | bytes 122888 | tf_op jit(solution)/shard_map/ppermute | solution.py:299

commit v6 on v5

--- a/solution.py
+++ b/solution.py
@@ -275,10 +275,14 @@
     parts, out, whole, sems = refs[:-3], refs[-3], refs[-2], refs[-1]
     copies = []
     for k in range(whole.shape[0]):
-        for (piece, start, count), part in zip(places, parts, strict=True):
-            if piece == k:
+        found = [(place, part) for place, part in zip(places, parts, strict=True) if place[0] == k]
+        source = whole.at[k]
+        if len(found) == 1 and found[0][1].shape == source.shape:
+            source = found[0][1]
+        else:
+            for (_, start, count), part in found:
                 whole[k, :, start : start + count] = part[:, :count]
-        copy = pltpu.make_async_copy(whole.at[k], out.at[ids[COL] ^ k], sems.at[k])
+        copy = pltpu.make_async_copy(source, out.at[ids[COL] ^ k], sems.at[k])
         copy.start()
         copies.append(copy)
     for copy in copies:

time: 133 us -> 133 us (level)
  no operation moved by 1% of the time
where the time goes in v6:
time: 133 us
  Pallas kernels  50.1 us (38%)
  starting transfers between devices  39.3 us (30%)
  waiting for transfers between devices  38.5 us (29%)
  local copies, waits for them, and re-layouts  2.99 us (2%)
    pallas_call x21, Pallas kernels, kernel_call(): pl.pallas_call(body, out_shape=outs, in_specs=[SMEM] + [VMEM] * (len(ins)...  50.1 us
    ppermute x11, starting transfers between devices, over_low(): return lax.ppermute(x, 'row', [(i, i ^ 1) for i in range(n_row)])  13.3 us
    ppermute x7, waiting for transfers between devices, over_high(): lax.ppermute(x, 'row', [(i, (i // 2 ^ k) * 2 + i % 2) for i in range(n_ro...  11.6 us
    ppermute x7, starting transfers between devices, up(): return lax.ppermute(x, 'row', [(i, (i + 2) % n_row) for i in range(n_row)])  10.4 us
    ppermute x7, waiting for transfers between devices, up(): return lax.ppermute(x, 'row', [(i, (i + 2) % n_row) for i in range(n_row)])  10.2 us
    ppermute x11, waiting for transfers between devices, over_low(): return lax.ppermute(x, 'row', [(i, i ^ 1) for i in range(n_row)])  9.07 us
    ppermute x7, starting transfers between devices, over_high(): lax.ppermute(x, 'row', [(i, (i // 2 ^ k) * 2 + i % 2) for i in range(n_ro...  8.06 us
    ppermute x14, starting transfers between devices, over_col(): return lax.ppermute(x, 'col', [(i, i ^ k) for i in range(n_col)])  7.57 us
  transfers between devices with their start and end apart: 39, of which 19 were waited for; matrix products, arithmetic and copies ran while one was open for 3% of the time, Pallas kernels for 37%

profile of v6, /device:TPU:0, one launch (start us, length us, event | category | flops | bytes accessed | tf_op | source)
XLA Modules:
  0.0 133.1 jit_solution(4637323363083821563)
XLA Ops:
  0.5 1.1 dynamic-slice_bitcast_fusion.2
  1.7 2.9 %collective-permute-start.2 = (bf16[40,1280]{1,0:T(8,128)(2,1)S(1)}, bf16[40,1280]{1,0:T(8,128)(2,1)S(1)}, u32[]{:S(2)}, u32[]{:S(2)}) collective-permute-start(bf16[40,1280]{1,0:T(8,128)(2,1)S(1)} %get-tuple-element.189), channel_id=1, source_target_pairs={{0,2},{1,3},{2,0},{3,1},{4,6},{5,7},{6,4},{7,5},{8,10},{9,11},{10,... | collective-permute-start | bytes 307208 | tf_op jit(solution)/shard_map/ppermute | solution.py:303
  6.3 1.0 half_slab.2
  7.2 1.4 %dynamic-slice_bitcast_fusion = bf16[3,1,160,1280]{3,2,1,0:T(8,128)(2,1)S(1)} fusion(bf16[3,1,2,160,1280]{4,3,2,1,0:T(8,128)(2,1)} %bitcast.53, s32[]{:T(128)S(6)} %select_n.55), kind=kLoop, calls=%fused_computation | loop fusion | bytes 2457604 | tf_op jit(solution)/shard_map/jit(dynamic_index_in_dim)/squeeze | solution.py:324
  8.6 1.8 %collective-permute-start.9 = (bf16[3,1,160,1280]{3,2,1,0:T(8,128)(2,1)S(1)}, bf16[3,1,160,1280]{3,2,1,0:T(8,128)(2,1)S(1)}, u32[]{:S(2)}, u32[]{:S(2)}) collective-permute-start(bf16[3,1,160,1280]{3,2,1,0:T(8,128)(2,1)S(1)} %dynamic-slice_bitcast_fusion), channel_id=1, source_target_pairs={{0,2},{1,3},{2,0},{3,1},{4,6},{5,7},{6,4},{7,5},{8,10},{9,11},{10,... | collective-permute-start | bytes 3686408 | tf_op jit(solution)/shard_map/ppermute | solution.py:303
  10.5 1.6 %collective-permute-start.6 = (bf16[80,1280]{1,0:T(8,128)(2,1)S(1)}, bf16[80,1280]{1,0:T(8,128)(2,1)S(1)}, u32[]{:S(2)}, u32[]{:S(2)}) collective-permute-start(bf16[80,1280]{1,0:T(8,128)(2,1)S(1)} %bitcast.56), channel_id=1, source_target_pairs={{0,8},{4,12},{8,16},{12,20},{16,24},{20,28},{24,0},{28,4},{1,9},{5... | collective-permute-start | bytes 614408 | tf_op jit(solution)/shard_map/ppermute | solution.py:312
  12.1 1.5 %collective-permute-start.7 = (bf16[80,1280]{1,0:T(8,128)(2,1)S(1)}, bf16[80,1280]{1,0:T(8,128)(2,1)S(1)}, u32[]{:S(2)}, u32[]{:S(2)}) collective-permute-start(bf16[80,1280]{1,0:T(8,128)(2,1)S(1)} %bitcast.57), channel_id=1, source_target_pairs={{0,4},{4,0},{8,12},{12,8},{16,20},{20,16},{24,28},{28,24},{1,5},{5... | collective-permute-start | bytes 614408 | tf_op jit(solution)/shard_map/ppermute | solution.py:306
  13.7 1.0 half_slab.3
  14.7 1.6 %collective-permute-start.4 = (bf16[80,1280]{1,0:T(8,128)(2,1)S(1)}, bf16[80,1280]{1,0:T(8,128)(2,1)S(1)}, u32[]{:S(2)}, u32[]{:S(2)}) collective-permute-start(bf16[80,1280]{1,0:T(8,128)(2,1)S(1)} %bitcast.59), channel_id=1, source_target_pairs={{0,8},{4,12},{8,16},{12,20},{16,24},{20,28},{24,0},{28,4},{1,9},{5... | collective-permute-start | bytes 614408 | tf_op jit(solution)/shard_map/ppermute | solution.py:312
  16.9 2.8 %place_pieces.1 = (bf16[3,4,160,1280]{3,2,1,0:T(8,128)(2,1)S(1)}, bf16[3,4,160,1280]{3,2,1,0:T(8,128)(2,1)S(1)}) custom-call(s32[4]{0:T(128)S(1)} %pad_add_fusion.ids, s32[20,20]{1,0:T(8,128)S(1)} %copy-done.2, bf16[3,1,2,160,1280]{4,3,2,1,0:T(8,128)(2,1)S(1)} %bitcast.54, bf16[3,1,2,160,1280]{4,3,2,1,0:T(8,128)(2,1)} %bitcast.11.refs_1_), custom_call_target="tpu_custom_call" | custom-call | tf_op jit(solution)/shard_map/place_pieces/pallas_call | solution.py:40
  20.3 1.1 collective-permute-start.10
  21.4 1.9 %collective-permute-start.11 = (bf16[80,1280]{1,0:T(8,128)(2,1)S(1)}, bf16[80,1280]{1,0:T(8,128)(2,1)S(1)}, u32[]{:S(2)}, u32[]{:S(2)}) collective-permute-start(bf16[80,1280]{1,0:T(8,128)(2,1)S(1)} %collective-permute-done.6.refs_1_), channel_id=1, source_target_pairs={{0,4},{4,0},{8,12},{12,8},{16,20},{20,16},{24,28},{28,24},{1,5},{5... | collective-permute-start | bytes 614408 | tf_op jit(solution)/shard_map/ppermute | solution.py:306
  23.3 1.0 collective-permute-done.4.refs_5_
  24.3 1.6 %collective-permute-start.14 = (bf16[80,1280]{1,0:T(8,128)(2,1)S(1)}, bf16[80,1280]{1,0:T(8,128)(2,1)S(1)}, u32[]{:S(2)}, u32[]{:S(2)}) collective-permute-start(bf16[80,1280]{1,0:T(8,128)(2,1)S(1)} %collective-permute-done.4.refs_5_), channel_id=1, source_target_pairs={{0,8},{4,12},{8,16},{12,20},{16,24},{20,28},{24,0},{28,4},{1,9},{5... | collective-permute-start | bytes 614408 | tf_op jit(solution)/shard_map/ppermute | solution.py:312
  25.9 1.6 %collective-permute-start.15 = (bf16[80,1280]{1,0:T(8,128)(2,1)S(1)}, bf16[80,1280]{1,0:T(8,128)(2,1)S(1)}, u32[]{:S(2)}, u32[]{:S(2)}) collective-permute-start(bf16[80,1280]{1,0:T(8,128)(2,1)S(1)} %collective-permute-done.4.refs_5_), channel_id=1, source_target_pairs={{0,4},{4,0},{8,12},{12,8},{16,20},{20,16},{24,28},{28,24},{1,5},{5... | collective-permute-start | bytes 614408 | tf_op jit(solution)/shard_map/ppermute | solution.py:306
  27.6 1.3 collective-permute-done.10.refs_2_
  29.1 1.7 %collective-permute-start.12 = (bf16[80,1280]{1,0:T(8,128)(2,1)S(1)}, bf16[80,1280]{1,0:T(8,128)(2,1)S(1)}, u32[]{:S(2)}, u32[]{:S(2)}) collective-permute-start(bf16[80,1280]{1,0:T(8,128)(2,1)S(1)} %collective-permute-done.10.refs_2_), channel_id=1, source_target_pairs={{0,8},{4,12},{8,16},{12,20},{16,24},{20,28},{24,0},{28,4},{1,9},{5... | collective-permute-start | bytes 614408 | tf_op jit(solution)/shard_map/ppermute | solution.py:312
  30.8 1.5 %collective-permute-start.13 = (bf16[80,1280]{1,0:T(8,128)(2,1)S(1)}, bf16[80,1280]{1,0:T(8,128)(2,1)S(1)}, u32[]{:S(2)}, u32[]{:S(2)}) collective-permute-start(bf16[80,1280]{1,0:T(8,128)(2,1)S(1)} %collective-permute-done.10.refs_2_), channel_id=1, source_target_pairs={{0,4},{4,0},{8,12},{12,8},{16,20},{20,16},{24,28},{28,24},{1,5},{5... | collective-permute-start | bytes 614408 | tf_op jit(solution)/shard_map/ppermute | solution.py:306
  32.3 1.8 %collective-permute-done.14.refs_6_ = bf16[80,1280]{1,0:T(8,128)(2,1)S(1)} collective-permute-done((bf16[80,1280]{1,0:T(8,128)(2,1)S(1)}, bf16[80,1280]{1,0:T(8,128)(2,1)S(1)}, u32[]{:S(2)}, u32[]{:S(2)}) %collective-permute-start.14) | collective-permute-done | bytes 204832 | tf_op jit(solution)/shard_map/ppermute | solution.py:312
  34.1 1.5 %collective-permute-start.17 = (bf16[80,1280]{1,0:T(8,128)(2,1)S(1)}, bf16[80,1280]{1,0:T(8,128)(2,1)S(1)}, u32[]{:S(2)}, u32[]{:S(2)}) collective-permute-start(bf16[80,1280]{1,0:T(8,128)(2,1)S(1)} %collective-permute-done.14.refs_6_), channel_id=1, source_target_pairs={{0,4},{4,0},{8,12},{12,8},{16,20},{20,16},{24,28},{28,24},{1,5},{5... | collective-permute-start | bytes 614408 | tf_op jit(solution)/shard_map/ppermute | solution.py:306
  35.7 1.1 collective-permute-start.16
  38.8 2.2 %collective-permute-done.17.refs_14_ = bf16[80,1280]{1,0:T(8,128)(2,1)S(1)} collective-permute-done((bf16[80,1280]{1,0:T(8,128)(2,1)S(1)}, bf16[80,1280]{1,0:T(8,128)(2,1)S(1)}, u32[]{:S(2)}, u32[]{:S(2)}) %collective-permute-start.17) | collective-permute-done | bytes 204832 | tf_op jit(solution)/shard_map/ppermute | solution.py:306
  40.9 1.6 %collective-permute-start.22 = (bf16[80,1280]{1,0:T(8,128)(2,1)S(1)}, bf16[80,1280]{1,0:T(8,128)(2,1)S(1)}, u32[]{:S(2)}, u32[]{:S(2)}) collective-permute-start(bf16[80,1280]{1,0:T(8,128)(2,1)S(1)} %collective-permute-done.17.refs_14_), channel_id=1, source_target_pairs={{0,8},{4,12},{8,16},{12,20},{16,24},{20,28},{24,0},{28,4},{1,9},{5... | collective-permute-start | bytes 614408 | tf_op jit(solution)/shard_map/ppermute | solution.py:312
  44.0 4.5 %collective-permute-done.22.refs_15_ = bf16[80,1280]{1,0:T(8,128)(2,1)S(1)} collective-permute-done((bf16[80,1280]{1,0:T(8,128)(2,1)S(1)}, bf16[80,1280]{1,0:T(8,128)(2,1)S(1)}, u32[]{:S(2)}, u32[]{:S(2)}) %collective-permute-start.22) | collective-permute-done | bytes 204832 | tf_op jit(solution)/shard_map/ppermute | solution.py:312
  48.5 1.5 %collective-permute-start.21 = (bf16[80,1280]{1,0:T(8,128)(2,1)S(1)}, bf16[80,1280]{1,0:T(8,128)(2,1)S(1)}, u32[]{:S(2)}, u32[]{:S(2)}) collective-permute-start(bf16[80,1280]{1,0:T(8,128)(2,1)S(1)} %collective-permute-done.12.refs_3_), channel_id=1, source_target_pairs={{0,4},{4,0},{8,12},{12,8},{16,20},{20,16},{24,28},{28,24},{1,5},{5... | collective-permute-start | bytes 614408 | tf_op jit(solution)/shard_map/ppermute | solution.py:306
  51.0 3.3 %collective-permute-done.21.refs_11_ = bf16[80,1280]{1,0:T(8,128)(2,1)S(1)} collective-permute-done((bf16[80,1280]{1,0:T(8,128)(2,1)S(1)}, bf16[80,1280]{1,0:T(8,128)(2,1)S(1)}, u32[]{:S(2)}, u32[]{:S(2)}) %collective-permute-start.21) | collective-permute-done | bytes 204832 | tf_op jit(solution)/shard_map/ppermute | solution.py:306
  55.1 0.9 place_parts.1.refs_0_
  56.0 5.3 %send_part.4 = (bf16[768,1280]{1,0:T(8,128)(2,1)S(1)}, bf16[4,160,256]{2,1,0:T(8,128)(2,1)S(1)}, bf16[640,6]{1,0:T(8,128)(2,1)S(1)}, bf16[640,6]{1,0:T(8,128)(2,1)S(1)}) custom-call(s32[4]{0:T(128)S(1)} %pad_add_fusion.ids, bf16[3,4,160,1280]{3,2,1,0:T(8,128)(2,1)S(1)} %place_parts.1.refs_0_, bf16[3,4,160,1280]{3,2,1,0:T(8,128)(2,1)S(1)} %get-tuple-element.138.refs_1_, ...), custom_call_target="tpu_custom_call" | custom-call | tf_op jit(solution)/shard_map/send_part/pallas_call | solution.py:40
  61.3 1.6 %collective-permute-start.23 = (bf16[4,160,256]{2,1,0:T(8,128)(2,1)S(1)}, bf16[4,160,256]{2,1,0:T(8,128)(2,1)S(1)}, u32[]{:S(2)}, u32[]{:S(2)}) collective-permute-start(bf16[4,160,256]{2,1,0:T(8,128)(2,1)S(1)} %get-tuple-element.133), channel_id=1, source_target_pairs={{0,4},{4,0},{8,12},{12,8},{16,20},{20,16},{24,28},{28,24},{1,5},{5... | collective-permute-start | bytes 983048 | tf_op jit(solution)/shard_map/ppermute | solution.py:306
  62.9 7.8 %send_part.5 = (bf16[1152,1280]{1,0:T(8,128)(2,1)S(1)}, bf16[4,160,384]{2,1,0:T(8,128)(2,1)S(1)}) custom-call(s32[4]{0:T(128)S(1)} %pad_add_fusion.ids, bf16[3,4,160,1280]{3,2,1,0:T(8,128)(2,1)S(1)} %place_parts.1.refs_0_, bf16[3,4,160,1280]{3,2,1,0:T(8,128)(2,1)S(1)} %get-tuple-element.138.refs_1_, bf16[1280,1280]{1,0:T(8,128)(2,1)S(1)} %bitcast.50, ...), custom_call_target="tpu_custom_call" | custom-call | tf_op jit(solution)/shard_map/send_part/pallas_call | solution.py:40
  72.3 1.4 %collective-permute-done.24.refs_0_ = bf16[3,1,160,1280]{3,2,1,0:T(8,128)(2,1)S(1)} collective-permute-done((bf16[3,1,160,1280]{3,2,1,0:T(8,128)(2,1)S(1)}, bf16[3,1,160,1280]{3,2,1,0:T(8,128)(2,1)S(1)}, u32[]{:S(2)}, u32[]{:S(2)}) %collective-permute-start.24) | collective-permute-done | bytes 1228832 | tf_op jit(solution)/shard_map/ppermute | solution.py:303
  73.6 0.9 place_halves.5.refs_1_
  74.6 7.6 %send_part.6 = (bf16[1152,1280]{1,0:T(8,128)(2,1)S(1)}, bf16[4,160,384]{2,1,0:T(8,128)(2,1)S(1)}) custom-call(s32[4]{0:T(128)S(1)} %pad_add_fusion.ids, bf16[3,4,160,1280]{3,2,1,0:T(8,128)(2,1)S(1)} %place_parts.1.refs_0_, bf16[3,4,160,1280]{3,2,1,0:T(8,128)(2,1)S(1)} %place_halves.5.refs_1_, bf16[1280,1280]{1,0:T(8,128)(2,1)S(1)} %bitcast.51, ...), custom_call_target="tpu_custom_call" | custom-call | tf_op jit(solution)/shard_map/send_part/pallas_call | solution.py:40
  82.8 1.6 %collective-permute-done.25.refs_7_ = bf16[4,160,384]{2,1,0:T(8,128)(2,1)S(1)} collective-permute-done((bf16[4,160,384]{2,1,0:T(8,128)(2,1)S(1)}, bf16[4,160,384]{2,1,0:T(8,128)(2,1)S(1)}, u32[]{:S(2)}, u32[]{:S(2)}) %collective-permute-start.25) | collective-permute-done | bytes 491552 | tf_op jit(solution)/shard_map/ppermute | solution.py:306
  84.4 5.0 %keep_part.3 = (f32[2,160,640]{2,1,0:T(8,128)S(1)}, bf16[2,160,640]{2,1,0:T(8,128)(2,1)S(1)}) custom-call(s32[4]{0:T(128)S(1)} %pad_add_fusion.ids, bf16[3,640,1280]{2,1,0:T(8,128)(2,1)S(1)} %bitcast.46, bf16[640,6]{1,0:T(8,128)(2,1)S(1)} %get-tuple-element.144.refs_1_, bf16[768,1280]{1,0:T(8,128)(2,1)S(1)} %get-tuple-element.145.refs_2_, ...), custom_call_target="tpu_custom_call" | custom-call | tf_op jit(solution)/shard_map/keep_part/pallas_call | solution.py:40
  89.5 5.1 %send_part.7 = (bf16[768,1280]{1,0:T(8,128)(2,1)S(1)}, bf16[4,160,256]{2,1,0:T(8,128)(2,1)S(1)}) custom-call(s32[4]{0:T(128)S(1)} %pad_add_fusion.ids, bf16[3,4,160,1280]{3,2,1,0:T(8,128)(2,1)S(1)} %place_parts.1.refs_0_, bf16[3,4,160,1280]{3,2,1,0:T(8,128)(2,1)S(1)} %place_halves.5.refs_1_, bf16[1280,1280]{1,0:T(8,128)(2,1)S(1)} %bitcast.52, ...), custom_call_target="tpu_custom_call" | custom-call | tf_op jit(solution)/shard_map/send_part/pallas_call | solution.py:40
  95.5 3.5 %keep_part.4 = (f32[2,160,384]{2,1,0:T(8,128)S(1)}, bf16[2,160,384]{2,1,0:T(8,128)(2,1)S(1)}) custom-call(s32[4]{0:T(128)S(1)} %pad_add_fusion.ids, bf16[3,640,1280]{2,1,0:T(8,128)(2,1)S(1)} %bitcast.47, bf16[640,6]{1,0:T(8,128)(2,1)S(1)} %get-tuple-element.144.refs_1_, bf16[1152,1280]{1,0:T(8,128)(2,1)S(1)} %get-tuple-element.155.refs_2_, ...), custom_call_target="tpu_custom_call" | custom-call | tf_op jit(solution)/shard_map/keep_part/pallas_call | solution.py:40
  99.0 1.2 collective-permute-start.28
  101.4 1.1 collective-permute-start.30
  102.5 6.7 %collective-permute-done.28.got = bf16[2,160,384]{2,1,0:T(8,128)(2,1)S(1)} collective-permute-done((bf16[2,160,384]{2,1,0:T(8,128)(2,1)S(1)}, bf16[2,160,384]{2,1,0:T(8,128)(2,1)S(1)}, u32[]{:S(2)}, u32[]{:S(2)}) %collective-permute-start.28) | collective-permute-done | bytes 245792 | tf_op jit(solution)/shard_map/ppermute | solution.py:309
  109.8 1.2 collective-permute-start.32
  111.0 2.1 %keep_part.5 = (f32[160,256]{1,0:T(8,128)S(1)}, bf16[160,256]{1,0:T(8,128)(2,1)S(1)}, bf16[160,256]{1,0:T(8,128)(2,1)S(1)}, bf16[160,256]{1,0:T(8,128)(2,1)S(1)}) custom-call(s32[4]{0:T(128)S(1)} %pad_add_fusion.ids, bf16[3,640,1280]{2,1,0:T(8,128)(2,1)S(1)} %bitcast.48, bf16[640,6]{1,0:T(8,128)(2,1)S(1)} %get-tuple-element.144.refs_1_, ...), custom_call_target="tpu_custom_call" | custom-call | tf_op jit(solution)/shard_map/keep_part/pallas_call | solution.py:40
  113.1 2.9 %collective-permute-done.30 = bf16[1,160,640]{2,1,0:T(8,128)(2,1)S(1)} collective-permute-done((bf16[1,160,640]{2,1,0:T(8,128)(2,1)S(1)}, bf16[1,160,640]{2,1,0:T(8,128)(2,1)S(1)}, u32[]{:S(2)}, u32[]{:S(2)}) %collective-permute-start.30) | collective-permute-done | bytes 204832 | tf_op jit(solution)/shard_map/ppermute | solution.py:309
  116.7 4.3 %collective-permute-start.37 = (bf16[160,256]{1,0:T(8,128)(2,1)S(1)}, bf16[160,256]{1,0:T(8,128)(2,1)S(1)}, u32[]{:S(2)}, u32[]{:S(2)}) collective-permute-start(bf16[160,256]{1,0:T(8,128)(2,1)S(1)} %get-tuple-element.180), channel_id=1, source_target_pairs={{0,24},{4,28},{8,16},{12,20},{16,8},{20,12},{24,0},{28,4},{1,25},{... | collective-permute-start | bytes 245768 | tf_op jit(solution)/shard_map/ppermute | solution.py:309
  122.4 2.0 %collective-permute-done.37.refs_2_ = bf16[160,256]{1,0:T(8,128)(2,1)S(1)} collective-permute-done((bf16[160,256]{1,0:T(8,128)(2,1)S(1)}, bf16[160,256]{1,0:T(8,128)(2,1)S(1)}, u32[]{:S(2)}, u32[]{:S(2)}) %collective-permute-start.37) | collective-permute-done | bytes 81952 | tf_op jit(solution)/shard_map/ppermute | solution.py:309
  125.1 2.8 %collective-permute-done.33.refs_2_ = f32[160,384]{1,0:T(8,128)S(1)} collective-permute-done((f32[160,384]{1,0:T(8,128)S(1)}, f32[160,384]{1,0:T(8,128)S(1)}, u32[]{:S(2)}, u32[]{:S(2)}) %collective-permute-start.33) | collective-permute-done | bytes 245792 | tf_op jit(solution)/shard_map/ppermute | solution.py:303
  128.0 3.3 %collective-permute-done.38.refs_4_ = f32[160,256]{1,0:T(8,128)S(1)} collective-permute-done((f32[160,256]{1,0:T(8,128)S(1)}, f32[160,256]{1,0:T(8,128)S(1)}, u32[]{:S(2)}, u32[]{:S(2)}) %collective-permute-start.38) | collective-permute-done | bytes 163872 | tf_op jit(solution)/shard_map/ppermute | solution.py:303
  131.4 1.5 %finish.1 = f32[4,160,320]{2,1,0:T(8,128)} custom-call(s32[4]{0:T(128)S(1)} %pad_add_fusion.ids, f32[160,320]{1,0:T(8,128)S(1)} %collective-permute-done.31.refs_0_, f32[160,320]{1,0:T(8,128)S(1)} %get-tuple-element.184.refs_1_, f32[160,384]{1,0:T(8,128)S(1)} %collective-permute-done.33.refs_2_, f32[160,64]{1,0:T(8,128)S(1)} %collective-permute-done.34.refs_3_, ...), custom_call_target="tpu_custom_call" | custom-call | tf_op jit(solution)/shard_map/finish/pallas_call | solution.py:40
  (81 shorter events, 16.7 us)
Async XLA Ops:
  0.0 5.4 %copy-start = (bf16[3,160,1280]{2,1,0:T(8,128)(2,1)S(1)}, bf16[3,160,1280]{2,1,0:T(8,128)(2,1)}, u32[]{:S(2)}) copy-start(bf16[3,160,1280]{2,1,0:T(8,128)(2,1)} %param.8) | copy-start | bytes 3686404
  0.0 6.1 %copy-start.3 = (s32[4,20,20]{2,0,1:T(4,128)S(1)}, s32[4,20,20]{2,0,1:T(4,128)}, u32[]{:S(2)}) copy-start(s32[4,20,20]{2,0,1:T(4,128)} %param.10) | copy-start | bytes 19204
  0.0 6.2 %collective-permute-start = (bf16[3,320,1280]{2,1,0:T(8,128)(2,1)}, bf16[3,320,1280]{2,1,0:T(8,128)(2,1)}, u32[]{:S(2)}, u32[]{:S(2)}) collective-permute-start(bf16[3,320,1280]{2,1,0:T(8,128)(2,1)} %param.7), channel_id=1, source_target_pairs={{0,1},{1,0},{2,3},{3,2},{4,5},{5,4},{6,7},{7,6},{8,9},{9,8},{10,11... | collective-permute-start | bytes 7372808 | tf_op jit(solution)/shard_map/ppermute | solution.py:303
  1.5 4.7 %collective-permute-start.1 = (bf16[40,1280]{1,0:T(8,128)(2,1)S(1)}, bf16[40,1280]{1,0:T(8,128)(2,1)S(1)}, u32[]{:S(2)}, u32[]{:S(2)}) collective-permute-start(bf16[40,1280]{1,0:T(8,128)(2,1)S(1)} %get-tuple-element.188), channel_id=1, source_target_pairs={{0,1},{1,0},{2,3},{3,2},{4,5},{5,4},{6,7},{7,6},{8,9},{9,8},{10,11... | collective-permute-start | bytes 307208 | tf_op jit(solution)/shard_map/ppermute | solution.py:303
  1.7 8.7 %collective-permute-start.2 = (bf16[40,1280]{1,0:T(8,128)(2,1)S(1)}, bf16[40,1280]{1,0:T(8,128)(2,1)S(1)}, u32[]{:S(2)}, u32[]{:S(2)}) collective-permute-start(bf16[40,1280]{1,0:T(8,128)(2,1)S(1)} %get-tuple-element.189), channel_id=1, source_target_pairs={{0,2},{1,3},{2,0},{3,1},{4,6},{5,7},{6,4},{7,5},{8,10},{9,11},{10,... | collective-permute-start | bytes 307208 | tf_op jit(solution)/shard_map/ppermute | solution.py:303
  4.6 5.9 %collective-permute-start.3 = (bf16[40,1280]{1,0:T(8,128)(2,1)S(1)}, bf16[40,1280]{1,0:T(8,128)(2,1)S(1)}, u32[]{:S(2)}, u32[]{:S(2)}) collective-permute-start(bf16[40,1280]{1,0:T(8,128)(2,1)S(1)} %get-tuple-element.186), channel_id=1, source_target_pairs={{0,3},{1,2},{2,1},{3,0},{4,7},{5,6},{6,5},{7,4},{8,11},{9,10},{10,... | collective-permute-start | bytes 307208 | tf_op jit(solution)/shard_map/ppermute | solution.py:303
  5.7 11.1 %copy-start.2 = (s32[20,20]{1,0:T(8,128)S(1)}, s32[20,20]{1,0:T(8,128)}, u32[]{:S(2)}) copy-start(s32[20,20]{1,0:T(8,128)} %tiles.9) | copy-start | bytes 4804
  5.9 11.0 %copy-start.1 = (bf16[3,320,1280]{2,1,0:T(8,128)(2,1)S(1)}, bf16[3,320,1280]{2,1,0:T(8,128)(2,1)}, u32[]{:S(2)}) copy-start(bf16[3,320,1280]{2,1,0:T(8,128)(2,1)} %param.7) | copy-start | bytes 7372804
  8.6 34.6 %collective-permute-start.9 = (bf16[3,1,160,1280]{3,2,1,0:T(8,128)(2,1)S(1)}, bf16[3,1,160,1280]{3,2,1,0:T(8,128)(2,1)S(1)}, u32[]{:S(2)}, u32[]{:S(2)}) collective-permute-start(bf16[3,1,160,1280]{3,2,1,0:T(8,128)(2,1)S(1)} %dynamic-slice_bitcast_fusion), channel_id=1, source_target_pairs={{0,2},{1,3},{2,0},{3,1},{4,6},{5,7},{6,4},{7,5},{8,10},{9,11},{10,... | collective-permute-start | bytes 3686408 | tf_op jit(solution)/shard_map/ppermute | solution.py:303
  10.5 9.8 %collective-permute-start.6 = (bf16[80,1280]{1,0:T(8,128)(2,1)S(1)}, bf16[80,1280]{1,0:T(8,128)(2,1)S(1)}, u32[]{:S(2)}, u32[]{:S(2)}) collective-permute-start(bf16[80,1280]{1,0:T(8,128)(2,1)S(1)} %bitcast.56), channel_id=1, source_target_pairs={{0,8},{4,12},{8,16},{12,20},{16,24},{20,28},{24,0},{28,4},{1,9},{5... | collective-permute-start | bytes 614408 | tf_op jit(solution)/shard_map/ppermute | solution.py:312
  12.1 8.1 %collective-permute-start.7 = (bf16[80,1280]{1,0:T(8,128)(2,1)S(1)}, bf16[80,1280]{1,0:T(8,128)(2,1)S(1)}, u32[]{:S(2)}, u32[]{:S(2)}) collective-permute-start(bf16[80,1280]{1,0:T(8,128)(2,1)S(1)} %bitcast.57), channel_id=1, source_target_pairs={{0,4},{4,0},{8,12},{12,8},{16,20},{20,16},{24,28},{28,24},{1,5},{5... | collective-permute-start | bytes 614408 | tf_op jit(solution)/shard_map/ppermute | solution.py:306
  14.7 9.6 %collective-permute-start.4 = (bf16[80,1280]{1,0:T(8,128)(2,1)S(1)}, bf16[80,1280]{1,0:T(8,128)(2,1)S(1)}, u32[]{:S(2)}, u32[]{:S(2)}) collective-permute-start(bf16[80,1280]{1,0:T(8,128)(2,1)S(1)} %bitcast.59), channel_id=1, source_target_pairs={{0,8},{4,12},{8,16},{12,20},{16,24},{20,28},{24,0},{28,4},{1,9},{5... | collective-permute-start | bytes 614408 | tf_op jit(solution)/shard_map/ppermute | solution.py:312
  16.3 8.0 %collective-permute-start.5 = (bf16[80,1280]{1,0:T(8,128)(2,1)S(1)}, bf16[80,1280]{1,0:T(8,128)(2,1)S(1)}, u32[]{:S(2)}, u32[]{:S(2)}) collective-permute-start(bf16[80,1280]{1,0:T(8,128)(2,1)S(1)} %bitcast.60), channel_id=1, source_target_pairs={{0,4},{4,0},{8,12},{12,8},{16,20},{20,16},{24,28},{28,24},{1,5},{5... | collective-permute-start | bytes 614408 | tf_op jit(solution)/shard_map/ppermute | solution.py:306
  20.3 8.5 %collective-permute-start.10 = (bf16[80,1280]{1,0:T(8,128)(2,1)S(1)}, bf16[80,1280]{1,0:T(8,128)(2,1)S(1)}, u32[]{:S(2)}, u32[]{:S(2)}) collective-permute-start(bf16[80,1280]{1,0:T(8,128)(2,1)S(1)} %collective-permute-done.6.refs_1_), channel_id=1, source_target_pairs={{0,8},{4,12},{8,16},{12,20},{16,24},{20,28},{24,0},{28,4},{1,9},{5... | collective-permute-start | bytes 614408 | tf_op jit(solution)/shard_map/ppermute | solution.py:312
  21.4 7.7 %collective-permute-start.11 = (bf16[80,1280]{1,0:T(8,128)(2,1)S(1)}, bf16[80,1280]{1,0:T(8,128)(2,1)S(1)}, u32[]{:S(2)}, u32[]{:S(2)}) collective-permute-start(bf16[80,1280]{1,0:T(8,128)(2,1)S(1)} %collective-permute-done.6.refs_1_), channel_id=1, source_target_pairs={{0,4},{4,0},{8,12},{12,8},{16,20},{20,16},{24,28},{28,24},{1,5},{5... | collective-permute-start | bytes 614408 | tf_op jit(solution)/shard_map/ppermute | solution.py:306
  24.3 9.8 %collective-permute-start.14 = (bf16[80,1280]{1,0:T(8,128)(2,1)S(1)}, bf16[80,1280]{1,0:T(8,128)(2,1)S(1)}, u32[]{:S(2)}, u32[]{:S(2)}) collective-permute-start(bf16[80,1280]{1,0:T(8,128)(2,1)S(1)} %collective-permute-done.4.refs_5_), channel_id=1, source_target_pairs={{0,8},{4,12},{8,16},{12,20},{16,24},{20,28},{24,0},{28,4},{1,9},{5... | collective-permute-start | bytes 614408 | tf_op jit(solution)/shard_map/ppermute | solution.py:312
  25.9 8.2 %collective-permute-start.15 = (bf16[80,1280]{1,0:T(8,128)(2,1)S(1)}, bf16[80,1280]{1,0:T(8,128)(2,1)S(1)}, u32[]{:S(2)}, u32[]{:S(2)}) collective-permute-start(bf16[80,1280]{1,0:T(8,128)(2,1)S(1)} %collective-permute-done.4.refs_5_), channel_id=1, source_target_pairs={{0,4},{4,0},{8,12},{12,8},{16,20},{20,16},{24,28},{28,24},{1,5},{5... | collective-permute-start | bytes 614408 | tf_op jit(solution)/shard_map/ppermute | solution.py:306
  29.1 8.0 %collective-permute-start.12 = (bf16[80,1280]{1,0:T(8,128)(2,1)S(1)}, bf16[80,1280]{1,0:T(8,128)(2,1)S(1)}, u32[]{:S(2)}, u32[]{:S(2)}) collective-permute-start(bf16[80,1280]{1,0:T(8,128)(2,1)S(1)} %collective-permute-done.10.refs_2_), channel_id=1, source_target_pairs={{0,8},{4,12},{8,16},{12,20},{16,24},{20,28},{24,0},{28,4},{1,9},{5... | collective-permute-start | bytes 614408 | tf_op jit(solution)/shard_map/ppermute | solution.py:312
  30.8 7.9 %collective-permute-start.13 = (bf16[80,1280]{1,0:T(8,128)(2,1)S(1)}, bf16[80,1280]{1,0:T(8,128)(2,1)S(1)}, u32[]{:S(2)}, u32[]{:S(2)}) collective-permute-start(bf16[80,1280]{1,0:T(8,128)(2,1)S(1)} %collective-permute-done.10.refs_2_), channel_id=1, source_target_pairs={{0,4},{4,0},{8,12},{12,8},{16,20},{20,16},{24,28},{28,24},{1,5},{5... | collective-permute-start | bytes 614408 | tf_op jit(solution)/shard_map/ppermute | solution.py:306
  34.1 6.8 %collective-permute-start.17 = (bf16[80,1280]{1,0:T(8,128)(2,1)S(1)}, bf16[80,1280]{1,0:T(8,128)(2,1)S(1)}, u32[]{:S(2)}, u32[]{:S(2)}) collective-permute-start(bf16[80,1280]{1,0:T(8,128)(2,1)S(1)} %collective-permute-done.14.refs_6_), channel_id=1, source_target_pairs={{0,4},{4,0},{8,12},{12,8},{16,20},{20,16},{24,28},{28,24},{1,5},{5... | collective-permute-start | bytes 614408 | tf_op jit(solution)/shard_map/ppermute | solution.py:306
  35.7 7.6 %collective-permute-start.16 = (bf16[80,1280]{1,0:T(8,128)(2,1)S(1)}, bf16[80,1280]{1,0:T(8,128)(2,1)S(1)}, u32[]{:S(2)}, u32[]{:S(2)}) collective-permute-start(bf16[80,1280]{1,0:T(8,128)(2,1)S(1)} %collective-permute-done.14.refs_6_), channel_id=1, source_target_pairs={{0,8},{4,12},{8,16},{12,20},{16,24},{20,28},{24,0},{28,4},{1,9},{5... | collective-permute-start | bytes 614408 | tf_op jit(solution)/shard_map/ppermute | solution.py:312
  37.1 33.5 %collective-permute-start.8 = (bf16[3,1,160,1280]{3,2,1,0:T(8,128)(2,1)S(1)}, bf16[3,1,160,1280]{3,2,1,0:T(8,128)(2,1)S(1)}, u32[]{:S(2)}, u32[]{:S(2)}) collective-permute-start(bf16[3,1,160,1280]{3,2,1,0:T(8,128)(2,1)S(1)} %dynamic-slice_bitcast_fusion.1), channel_id=1, source_target_pairs={{0,2},{1,3},{2,0},{3,1},{4,6},{5,7},{6,4},{7,5},{8,10},{9,11},{10,... | collective-permute-start | bytes 3686408 | tf_op jit(solution)/shard_map/ppermute | solution.py:303
  40.9 7.6 %collective-permute-start.22 = (bf16[80,1280]{1,0:T(8,128)(2,1)S(1)}, bf16[80,1280]{1,0:T(8,128)(2,1)S(1)}, u32[]{:S(2)}, u32[]{:S(2)}) collective-permute-start(bf16[80,1280]{1,0:T(8,128)(2,1)S(1)} %collective-permute-done.17.refs_14_), channel_id=1, source_target_pairs={{0,8},{4,12},{8,16},{12,20},{16,24},{20,28},{24,0},{28,4},{1,9},{5... | collective-permute-start | bytes 614408 | tf_op jit(solution)/shard_map/ppermute | solution.py:312
  43.3 11.7 %collective-permute-start.18 = (bf16[1,1,160,1280]{3,2,1,0:T(8,128)(2,1)S(1)}, bf16[1,1,160,1280]{3,2,1,0:T(8,128)(2,1)S(1)}, u32[]{:S(2)}, u32[]{:S(2)}) collective-permute-start(bf16[1,1,160,1280]{3,2,1,0:T(8,128)(2,1)S(1)} %get-tuple-element.183), channel_id=1, source_target_pairs={{0,1},{1,0},{2,3},{3,2},{4,5},{5,4},{6,7},{7,6},{8,9},{9,8},{10,11... | collective-permute-start | bytes 1228808 | tf_op jit(solution)/shard_map/ppermute | solution.py:303
  43.4 11.7 %collective-permute-start.19 = (bf16[1,1,160,1280]{3,2,1,0:T(8,128)(2,1)S(1)}, bf16[1,1,160,1280]{3,2,1,0:T(8,128)(2,1)S(1)}, u32[]{:S(2)}, u32[]{:S(2)}) collective-permute-start(bf16[1,1,160,1280]{3,2,1,0:T(8,128)(2,1)S(1)} %get-tuple-element.182), channel_id=1, source_target_pairs={{0,1},{1,0},{2,3},{3,2},{4,5},{5,4},{6,7},{7,6},{8,9},{9,8},{10,11... | collective-permute-start | bytes 1228808 | tf_op jit(solution)/shard_map/ppermute | solution.py:303
  43.9 11.2 %collective-permute-start.20 = (bf16[1,1,160,1280]{3,2,1,0:T(8,128)(2,1)S(1)}, bf16[1,1,160,1280]{3,2,1,0:T(8,128)(2,1)S(1)}, u32[]{:S(2)}, u32[]{:S(2)}) collective-permute-start(bf16[1,1,160,1280]{3,2,1,0:T(8,128)(2,1)S(1)} %get-tuple-element.181), channel_id=1, source_target_pairs={{0,1},{1,0},{2,3},{3,2},{4,5},{5,4},{6,7},{7,6},{8,9},{9,8},{10,11... | collective-permute-start | bytes 1228808 | tf_op jit(solution)/shard_map/ppermute | solution.py:303
  48.5 5.8 %collective-permute-start.21 = (bf16[80,1280]{1,0:T(8,128)(2,1)S(1)}, bf16[80,1280]{1,0:T(8,128)(2,1)S(1)}, u32[]{:S(2)}, u32[]{:S(2)}) collective-permute-start(bf16[80,1280]{1,0:T(8,128)(2,1)S(1)} %collective-permute-done.12.refs_3_), channel_id=1, source_target_pairs={{0,4},{4,0},{8,12},{12,8},{16,20},{20,16},{24,28},{28,24},{1,5},{5... | collective-permute-start | bytes 614408 | tf_op jit(solution)/shard_map/ppermute | solution.py:306
  61.3 9.3 %collective-permute-start.23 = (bf16[4,160,256]{2,1,0:T(8,128)(2,1)S(1)}, bf16[4,160,256]{2,1,0:T(8,128)(2,1)S(1)}, u32[]{:S(2)}, u32[]{:S(2)}) collective-permute-start(bf16[4,160,256]{2,1,0:T(8,128)(2,1)S(1)} %get-tuple-element.133), channel_id=1, source_target_pairs={{0,4},{4,0},{8,12},{12,8},{16,20},{20,16},{24,28},{28,24},{1,5},{5... | collective-permute-start | bytes 983048 | tf_op jit(solution)/shard_map/ppermute | solution.py:306
  70.7 3.0 %collective-permute-start.24 = (bf16[3,1,160,1280]{3,2,1,0:T(8,128)(2,1)S(1)}, bf16[3,1,160,1280]{3,2,1,0:T(8,128)(2,1)S(1)}, u32[]{:S(2)}, u32[]{:S(2)}) collective-permute-start(bf16[3,1,160,1280]{3,2,1,0:T(8,128)(2,1)S(1)} %collective-permute-done.8.refs_0_), channel_id=1, source_target_pairs={{0,1},{1,0},{2,3},{3,2},{4,5},{5,4},{6,7},{7,6},{8,9},{9,8},{10,11... | collective-permute-start | bytes 3686408 | tf_op jit(solution)/shard_map/ppermute | solution.py:303
  70.7 13.6 %collective-permute-start.25 = (bf16[4,160,384]{2,1,0:T(8,128)(2,1)S(1)}, bf16[4,160,384]{2,1,0:T(8,128)(2,1)S(1)}, u32[]{:S(2)}, u32[]{:S(2)}) collective-permute-start(bf16[4,160,384]{2,1,0:T(8,128)(2,1)S(1)} %get-tuple-element.148), channel_id=1, source_target_pairs={{0,4},{4,0},{8,12},{12,8},{16,20},{20,16},{24,28},{28,24},{1,5},{5... | collective-permute-start | bytes 1474568 | tf_op jit(solution)/shard_map/ppermute | solution.py:306
  82.2 13.3 %collective-permute-start.26 = (bf16[4,160,384]{2,1,0:T(8,128)(2,1)S(1)}, bf16[4,160,384]{2,1,0:T(8,128)(2,1)S(1)}, u32[]{:S(2)}, u32[]{:S(2)}) collective-permute-start(bf16[4,160,384]{2,1,0:T(8,128)(2,1)S(1)} %get-tuple-element.156), channel_id=1, source_target_pairs={{0,4},{4,0},{8,12},{12,8},{16,20},{20,16},{24,28},{28,24},{1,5},{5... | collective-permute-start | bytes 1474568 | tf_op jit(solution)/shard_map/ppermute | solution.py:306
  89.4 11.3 %collective-permute-start.27 = (bf16[2,160,640]{2,1,0:T(8,128)(2,1)S(1)}, bf16[2,160,640]{2,1,0:T(8,128)(2,1)S(1)}, u32[]{:S(2)}, u32[]{:S(2)}) collective-permute-start(bf16[2,160,640]{2,1,0:T(8,128)(2,1)S(1)} %get-tuple-element.160), channel_id=1, source_target_pairs={{0,8},{4,12},{8,0},{12,4},{16,24},{20,28},{24,16},{28,20},{1,9},{5... | collective-permute-start | bytes 1228808 | tf_op jit(solution)/shard_map/ppermute | solution.py:309
  99.0 10.2 %collective-permute-start.28 = (bf16[2,160,384]{2,1,0:T(8,128)(2,1)S(1)}, bf16[2,160,384]{2,1,0:T(8,128)(2,1)S(1)}, u32[]{:S(2)}, u32[]{:S(2)}) collective-permute-start(bf16[2,160,384]{2,1,0:T(8,128)(2,1)S(1)} %get-tuple-element.163), channel_id=1, source_target_pairs={{0,8},{4,12},{8,0},{12,4},{16,24},{20,28},{24,16},{28,20},{1,9},{5... | collective-permute-start | bytes 737288 | tf_op jit(solution)/shard_map/ppermute | solution.py:309
  100.2 10.8 %collective-permute-start.29 = (bf16[4,160,256]{2,1,0:T(8,128)(2,1)S(1)}, bf16[4,160,256]{2,1,0:T(8,128)(2,1)S(1)}, u32[]{:S(2)}, u32[]{:S(2)}) collective-permute-start(bf16[4,160,256]{2,1,0:T(8,128)(2,1)S(1)} %get-tuple-element.168), channel_id=1, source_target_pairs={{0,4},{4,0},{8,12},{12,8},{16,20},{20,16},{24,28},{28,24},{1,5},{5... | collective-permute-start | bytes 983048 | tf_op jit(solution)/shard_map/ppermute | solution.py:306
  101.4 14.6 %collective-permute-start.30 = (bf16[1,160,640]{2,1,0:T(8,128)(2,1)S(1)}, bf16[1,160,640]{2,1,0:T(8,128)(2,1)S(1)}, u32[]{:S(2)}, u32[]{:S(2)}) collective-permute-start(bf16[1,160,640]{2,1,0:T(8,128)(2,1)S(1)} %get-tuple-element.171), channel_id=1, source_target_pairs={{0,16},{4,20},{8,24},{12,28},{16,0},{20,4},{24,8},{28,12},{1,17},{... | collective-permute-start | bytes 614408 | tf_op jit(solution)/shard_map/ppermute | solution.py:309
  109.8 11.2 %collective-permute-start.32 = (bf16[1,160,384]{2,1,0:T(8,128)(2,1)S(1)}, bf16[1,160,384]{2,1,0:T(8,128)(2,1)S(1)}, u32[]{:S(2)}, u32[]{:S(2)}) collective-permute-start(bf16[1,160,384]{2,1,0:T(8,128)(2,1)S(1)} %get-tuple-element.175), channel_id=1, source_target_pairs={{0,16},{4,20},{8,24},{12,28},{16,0},{20,4},{24,8},{28,12},{1,17},{... | collective-permute-start | bytes 368648 | tf_op jit(solution)/shard_map/ppermute | solution.py:309
  116.6 5.8 %collective-permute-start.35 = (bf16[160,256]{1,0:T(8,128)(2,1)S(1)}, bf16[160,256]{1,0:T(8,128)(2,1)S(1)}, u32[]{:S(2)}, u32[]{:S(2)}) collective-permute-start(bf16[160,256]{1,0:T(8,128)(2,1)S(1)} %get-tuple-element.178), channel_id=1, source_target_pairs={{0,8},{4,12},{8,0},{12,4},{16,24},{20,28},{24,16},{28,20},{1,9},{5... | collective-permute-start | bytes 245768 | tf_op jit(solution)/shard_map/ppermute | solution.py:309
  116.6 5.7 %collective-permute-start.36 = (bf16[160,256]{1,0:T(8,128)(2,1)S(1)}, bf16[160,256]{1,0:T(8,128)(2,1)S(1)}, u32[]{:S(2)}, u32[]{:S(2)}) collective-permute-start(bf16[160,256]{1,0:T(8,128)(2,1)S(1)} %get-tuple-element.179), channel_id=1, source_target_pairs={{0,16},{4,20},{8,24},{12,28},{16,0},{20,4},{24,8},{28,12},{1,17},{... | collective-permute-start | bytes 245768 | tf_op jit(solution)/shard_map/ppermute | solution.py:309
  116.7 7.7 %collective-permute-start.37 = (bf16[160,256]{1,0:T(8,128)(2,1)S(1)}, bf16[160,256]{1,0:T(8,128)(2,1)S(1)}, u32[]{:S(2)}, u32[]{:S(2)}) collective-permute-start(bf16[160,256]{1,0:T(8,128)(2,1)S(1)} %get-tuple-element.180), channel_id=1, source_target_pairs={{0,24},{4,28},{8,16},{12,20},{16,8},{20,12},{24,0},{28,4},{1,25},{... | collective-permute-start | bytes 245768 | tf_op jit(solution)/shard_map/ppermute | solution.py:309
  121.6 6.3 %collective-permute-start.33 = (f32[160,384]{1,0:T(8,128)S(1)}, f32[160,384]{1,0:T(8,128)S(1)}, u32[]{:S(2)}, u32[]{:S(2)}) collective-permute-start(f32[160,384]{1,0:T(8,128)S(1)} %add_up.4), channel_id=1, source_target_pairs={{0,2},{1,3},{2,0},{3,1},{4,6},{5,7},{6,4},{7,5},{8,10},{9,11},{10,... | collective-permute-start | bytes 737288 | tf_op jit(solution)/shard_map/ppermute | solution.py:303
  122.3 5.7 %collective-permute-start.31 = (f32[160,320]{1,0:T(8,128)S(1)}, f32[160,320]{1,0:T(8,128)S(1)}, u32[]{:S(2)}, u32[]{:S(2)}) collective-permute-start(f32[160,320]{1,0:T(8,128)S(1)} %get-tuple-element.185), channel_id=1, source_target_pairs={{0,1},{1,0},{2,3},{3,2},{4,5},{5,4},{6,7},{7,6},{8,9},{9,8},{10,11... | collective-permute-start | bytes 614408 | tf_op jit(solution)/shard_map/ppermute | solution.py:303
  125.0 6.4 %collective-permute-start.38 = (f32[160,256]{1,0:T(8,128)S(1)}, f32[160,256]{1,0:T(8,128)S(1)}, u32[]{:S(2)}, u32[]{:S(2)}) collective-permute-start(f32[160,256]{1,0:T(8,128)S(1)} %add_up.5), channel_id=1, source_target_pairs={{0,3},{1,2},{2,1},{3,0},{4,7},{5,6},{6,5},{7,4},{8,11},{9,10},{10,... | collective-permute-start | bytes 491528 | tf_op jit(solution)/shard_map/ppermute | solution.py:303
  127.9 3.4 %collective-permute-start.34 = (f32[160,64]{1,0:T(8,128)S(1)}, f32[160,64]{1,0:T(8,128)S(1)}, u32[]{:S(2)}, u32[]{:S(2)}) collective-permute-start(f32[160,64]{1,0:T(8,128)S(1)} %slice.51), channel_id=1, source_target_pairs={{0,1},{1,0},{2,3},{3,2},{4,5},{5,4},{6,7},{7,6},{8,9},{9,8},{10,11... | collective-permute-start | bytes 122888 | tf_op jit(solution)/shard_map/ppermute | solution.py:303
